TPU v7x, 32 devices: a whole 2x2x4 slice. The times are simulated.
32 devices in a mesh: cells: 4 (over y, x), genes: 8 (over z, core).
Axes of the slice: x: 2, y: 2, z: 4, core: 2. Of those that a mesh axis runs over, the one named last changes fastest.
Arguments:
- inputs: float32 [16, 2048, 200], P('cells', 'genes'), may hold values from -6 to 6
- lengths: int32 [16], P('cells'), may hold values from 1 to 2048, as said below
- tissue_ids: int32 [16], P('cells'), may hold values from 0 to 15
- tissue_table: float32 [16, 200], replicated, may hold values from -3 to 3
- first_gain: float32 [200], replicated, may hold values from 0.1 to 1.9
- first_bias: float32 [200], replicated, may hold values from -1.75 to 1.75
- joint_weight: float32 [200, 1920], replicated, may hold values from -0.21875 to 0.21875
- feature_draws: float32 [10, 266, 64], replicated, may hold values from -6 to 6
- output_weight: float32 [640, 200], replicated, may hold values from -6 to 6
- output_bias: float32 [200], replicated, may hold values from -1.75 to 1.75
- second_gain: float32 [200], replicated, may hold values from 0.1 to 1.9
- second_bias: float32 [200], replicated, may hold values from -1.75 to 1.75
- hidden_weight: float32 [200, 800], replicated, may hold values from -0.4375 to 0.4375
- hidden_bias: float32 [800], replicated, may hold values from -1.75 to 1.75
- return_weight: float32 [800, 200], replicated, may hold values from -0.21875 to 0.21875
- return_bias: float32 [200], replicated, may hold values from -3 to 3
- cotangent: bfloat16 [16, 2048, 200], P('cells', 'genes'), may hold values from -6 to 6
Outputs:
- outputs: float32 [16, 2048, 200], P('cells', 'genes')
- input_grad: float32 [16, 2048, 200], P('cells', 'genes')
- tissue_grad: float32 [16, 200], replicated
- first_gain_grad: float32 [200], replicated
- first_bias_grad: float32 [200], replicated
- joint_grad: float32 [200, 1920], replicated
- output_weight_grad: float32 [640, 200], replicated
- output_bias_grad: float32 [200], replicated
- second_gain_grad: float32 [200], replicated
- second_bias_grad: float32 [200], replicated
- hidden_weight_grad: float32 [200, 800], replicated
- hidden_bias_grad: float32 [800], replicated
- return_weight_grad: float32 [800, 200], replicated
- return_bias_grad: float32 [200], replicated
Inputs may be any that keep to these rules, and one draw needn't show every extreme that they name: `lengths`: among the 4 cells held by each index of cells, one has all 2048 genes present.
All inputs are finite; a program needn't handle non-finite values.
Results may differ from a plain program's by a relative error of at most 0.012.
The roundings to bfloat16 on the way count: a program that leaves them out, or rounds other values in their place, can miss the bound.
Values sent between devices are 32-bit elements; how exact they have to be, the bound alone decides.
No kernel may reach another device: no remote copies, remote signals or barrier semaphores. Data moves between devices by JAX's collectives and lax.ppermute only.
A program may use at most 128 MiB of HBM per device.

v0:
```python
import functools

import jax
import jax.numpy as jnp
from jax import lax
from jax.experimental import pallas as pl
from jax.experimental.pallas import tpu as pltpu
from jax.sharding import Mesh
from jax.sharding import PartitionSpec as P

EPSILON = 1e-05
LOWEST = -1e30
bf16 = jnp.bfloat16
f32 = jnp.float32
LANES = 128


def dot(left, right):
    return jnp.dot(left, right, preferred_element_type=f32)


def dot_lanes(left, right):
    return lax.dot_general(left, right, (((1,), (1,)), ((), ())), preferred_element_type=f32)


def norm_rows(values):
    centered = values - jnp.mean(values, 0, keepdims=True)
    inverse = lax.rsqrt(jnp.mean(centered * centered, 0, keepdims=True) + EPSILON)
    return centered * inverse, inverse


def norm_back_rows(upstream, normed, inverse, gain):
    scaled = upstream * gain
    return inverse * (
        scaled
        - jnp.mean(scaled, 0, keepdims=True)
        - normed * jnp.mean(scaled * normed, 0, keepdims=True)
    )


def fold(values):
    total = values[:, :LANES]
    for at in range(LANES, values.shape[1], LANES):
        total = total + values[:, at : at + LANES]
    return total


def split_low(values):
    high = values.astype(bf16)
    return high, (values - high.astype(f32)).astype(bf16)


def lane_index(shape):
    return lax.broadcasted_iota(jnp.int32, shape, len(shape) - 1)


def row_index(shape):
    return lax.broadcasted_iota(jnp.int32, shape, len(shape) - 2)


class Sizes:
    def __init__(self, mesh_sizes, inputs, feature_draws, hidden_weight):
        self.homes, self.rest = mesh_sizes["home"], mesh_sizes["rest"]
        _, self.genes, self.width = inputs.shape
        self.heads, self.feats, self.head = feature_draws.shape
        self.inner = self.heads * self.head
        self.hidden = hidden_weight.shape[1]
        self.rows = -(-self.feats // 16) * 16
        self.ext = self.head + 16
        self.scale = self.head ** (-0.25)


VMEM = pl.BlockSpec(memory_space=pltpu.VMEM)
SMEM = pl.BlockSpec(memory_space=pltpu.SMEM)


def call(name, body, args, out, scratch=(), megabytes=4, smem=0, aliases={}, flops=0):
    return pl.pallas_call(
        body,
        out_shape=out,
        in_specs=[SMEM] * smem + [VMEM] * (len(args) - smem),
        out_specs=jax.tree.map(lambda _: VMEM, out),
        scratch_shapes=list(scratch),
        input_output_aliases=aliases,
        compiler_params=pltpu.CompilerParams(vmem_limit_bytes=megabytes * 1024 * 1024),
        cost_estimate=pl.CostEstimate(flops=int(flops), bytes_accessed=1024, transcendentals=0),
        name=name,
    )(*args)


def array(*shape, dtype=f32):
    return jax.ShapeDtypeStruct(shape, dtype)


def prepare_body(s, tissue, joint, draws, out_t, hid, ret_t, hidden_bias, *refs):
    rows, table = refs[:6], refs[6]
    joint_t, draws_low, draws_t, out_wt, out_w, hid_w, hid_wt, ret_wt, ret_w, joint_w, cols, bias = refs[7:]
    joint_w[...] = joint[...].astype(bf16)
    joint_t[...] = joint[...].T.astype(bf16)
    for h in range(s.heads):
        draw = draws[h]
        filler = jnp.broadcast_to(draw[:, :1], (s.head, s.rows - s.feats))
        draws_low[h] = jnp.concatenate([draw, filler], 1).T.astype(bf16)
        draws_t[h] = jnp.concatenate([draw, jnp.zeros_like(filler)], 1).astype(bf16)
    out_wt[...] = out_t[...].astype(bf16)
    out_w[...] = out_t[...].T.astype(bf16)
    hid_w[...] = hid[...].astype(bf16)
    hid_wt[...] = hid[...].T.astype(bf16)
    ret_wt[...] = ret_t[...].astype(bf16)
    ret_w[...] = ret_t[...].T.astype(bf16)
    stacked = [r[...] for r in rows] + [table[pl.ds(tissue[0], 1), :]]
    stacked += [jnp.zeros((1, s.width), f32)]
    cols[...] = jnp.concatenate(stacked, 0).T
    bias[...] = jnp.broadcast_to(hidden_bias[...], (8, s.hidden)).T


def prepare(s, tissue, joint, draws, out_t, hid, ret_t, hidden_bias, rows, table):
    w, i, f = s.width, s.inner, s.hidden
    out = [
        array(3 * i, w, dtype=bf16),
        array(s.heads, s.rows, s.head, dtype=bf16),
        array(s.heads, s.head, s.rows, dtype=bf16),
        array(w, i, dtype=bf16),
        array(i, w, dtype=bf16),
        array(w, f, dtype=bf16),
        array(f, w, dtype=bf16),
        array(w, f, dtype=bf16),
        array(f, w, dtype=bf16),
        array(w, 3 * i, dtype=bf16),
        array(w, 8),
        array(f, 8),
    ]
    args = [tissue[None], joint, draws, out_t, hid, ret_t, hidden_bias[None], *[r[None] for r in rows], table]
    return call("prepare", functools.partial(prepare_body, s), args, out, smem=1, megabytes=8, flops=4e9)


def keys_body(s, base, count, fresh, *refs):
    refs = list(refs)
    place = refs.pop(0)
    xs = [refs.pop(0) for _ in range(count)]
    cols, joint_t, draws = (refs.pop(0) for _ in range(3))
    if not fresh:
        kv_prev = refs.pop(0)
        refs.pop(0), refs.pop(0)
    kv, shifted, qkv, ext, dashes, tops, cuts = refs
    scale = s.scale
    last_row = s.rows - 1
    tail = (s.heads, LANES - s.head, s.genes)
    ext[:, s.head :, :] = jnp.where(row_index(tail) == 0, 1.0, 0.0).astype(bf16)
    if fresh:
        state = jnp.full((16, 1), LOWEST, f32)
    else:
        state = jnp.concatenate([kv_prev[h, last_row:, 0:1] for h in range(s.heads)] + [jnp.full((16 - s.heads, 1), LOWEST, f32)], 0)
    for n in range(count):
        x = xs[n][...] + cols[:, 6:7]
        shifted[base + n] = x
        normed, _ = norm_rows(x)
        first = (normed * cols[:, 0:1] + cols[:, 1:2]).astype(bf16)
        for part in (1, 2, 0):
            rows = slice(part * s.inner, (part + 1) * s.inner)
            made = dot(joint_t[rows, :], first).astype(bf16)
            qkv[base + n, rows, :] = made
            if part == 2:
                for h in range(s.heads):
                    ext[h, : s.head, :] = made[h * s.head : (h + 1) * s.head]
        for h in range(s.heads):
            key = qkv[base + n, s.inner + h * s.head : s.inner + (h + 1) * s.head, :]
            dash = dot(draws[h], key)
            dashes[h] = dash
            key_f = key.astype(f32)
            cuts[h : h + 1, :] = jnp.sum(key_f * key_f, 0, keepdims=True) * (scale * scale * 0.5)
            tops[h : h + 1, :] = jnp.max(dash, 0, keepdims=True) * scale
        valid = place[base + n] + lane_index((1, s.genes)) < place[s.homes]
        new = jnp.maximum(state, jnp.max(jnp.where(valid, tops[...], LOWEST), 1, keepdims=True))
        decay = jnp.exp(state - new)
        state = new
        lifts = jnp.where(valid, cuts[...] + new, 1e30)
        for h in range(s.heads):
            feats = jnp.exp(scale * dashes[h] - lifts[h : h + 1]).astype(bf16)
            part = dot_lanes(feats, ext[h])
            if n == 0 and fresh:
                kv[h] = part
            else:
                kv[h] = (kv_prev if n == 0 else kv)[h] * decay[h : h + 1] + part
    for h in range(s.heads):
        kv[h, last_row:, :] = jnp.broadcast_to(state[h : h + 1], (1, LANES))


def run_keys(s, base, count, place, xs, cols, joint_t, draws, before=None):
    out = [
        array(s.heads, s.rows, LANES),
        array(s.homes, s.width, s.genes),
        array(s.homes, 3 * s.inner, s.genes, dtype=bf16),
    ]
    args = [place, *xs, cols, joint_t, draws]
    aliases = {}
    if before is not None:
        aliases = {len(args) + 1: 1, len(args) + 2: 2}
        args += list(before)
    scratch = [
        pltpu.VMEM((s.heads, LANES, s.genes), bf16),
        pltpu.VMEM((s.heads, s.rows, s.genes), f32),
        pltpu.VMEM((16, s.genes), f32),
        pltpu.VMEM((16, s.genes), f32),
    ]
    body = functools.partial(keys_body, s, base, count, before is None)
    return call("keys", body, args, out, scratch, 10, 1, aliases, 3e9 * count)


def merged(own, other, kept_rows, kept_lanes):
    last = own.shape[0] - 1
    own_peak, other_peak = own[last:, 0:1], other[last:, 0:1]
    peak = jnp.maximum(own_peak, other_peak)
    total = own * jnp.exp(own_peak - peak) + other * jnp.exp(other_peak - peak)
    inside = (row_index(own.shape) < kept_rows) & (lane_index(own.shape) < kept_lanes)
    return jnp.where(inside, total, 0.0), peak


def eye_like(size):
    return (row_index((size, size)) == lane_index((size, size))).astype(f32).astype(bf16)


def middle_body(s, base, count, first, final, *refs):
    refs = list(refs)

    def take(n):
        taken = refs[:n]
        del refs[:n]
        return taken

    (side,) = take(1)
    before = take(2) if first else take(9)
    shifted, qkv = take(2)
    cots = take(count)
    cols, hidden_bias, draws, draws_t, out_w, out_wt = take(6)
    hid_w, hid_wt, ret_w, ret_wt, joint = take(5)
    outputs = take(count)
    middle_grad, query_part = take(2)
    results = take(3) if final else take(9)
    if first:
        kv3, kv_t = take(2) if final else results[:2]
    else:
        kv3, kv_t = before[:2]
    feats, att, att_low, over, att_grad, query_grad = take(6)
    cot_all, out_all, *sums = refs
    acc_q, acc_o, acc_r, acc_h, acc_cols, acc_hb, values_grad = sums
    scale = s.scale
    ext = s.ext
    if first:
        kv_own, kv_other = before
        eye = eye_like(2 * ext)
        for h in range(s.heads):
            total, _ = merged(kv_own[h], kv_other[h], s.feats, s.head + 1)
            high, low = split_low(total[:, :ext])
            kv3[h] = jnp.concatenate([high, low, high], 1)
            kv_t[h] = dot_lanes(eye, jnp.concatenate([high, low], 1)).astype(bf16)
        for acc in sums:
            acc[...] = jnp.zeros_like(acc)
    else:
        for acc, was in zip(sums, before[2:]):
            acc[...] = was[...]
    for n in range(count):
        cot_all[n] = cots[n][...]

    def block(j, carry):
        def attend(h):
            rows = slice(h * s.head, (h + 1) * s.head)
            query = qkv[base + j, rows, :]
            query_f = query.astype(f32)
            cut = jnp.sum(query_f * query_f, 0, keepdims=True) * (scale * scale * 0.5)
            value = jnp.exp(scale * dot(draws[h], query) - cut)
            feats[h] = value
            both = dot(kv_t[h], value.astype(bf16))
            total = both[:ext] + both[ext:]
            inverse = 1.0 / total[s.head : s.head + 1]
            over[h : h + 1, :] = inverse
            result = total[: s.head] * inverse
            att[rows, :] = result
            att_low[rows, :] = result.astype(bf16)

        for h in range(s.heads):
            attend(h)

        x = shifted[base + j]
        middle = x + dot(out_wt[...], att_low[...]) + cols[:, 2:3]
        normed, inverse = norm_rows(middle)
        gain = cols[:, 3:4]
        second = (normed * gain + cols[:, 4:5]).astype(bf16)
        pre = dot(hid_wt[...], second) + hidden_bias[:, 0:1]
        cumulative = 0.5 * (1.0 + lax.erf(pre * 0.7071067811865476))
        act = (pre * cumulative).astype(bf16)
        slope = cumulative + pre * (jnp.exp(-0.5 * pre * pre) * 0.3989422804014327)
        out_all[j] = middle + dot(ret_wt[...], act) + cols[:, 5:6]
        cot = cot_all[j]
        cot_low = cot.astype(bf16)
        pre_low = (dot(ret_w[...], cot_low) * slope).astype(bf16)
        acc_r[...] += dot_lanes(cot_low, act)
        acc_h[...] += dot_lanes(second, pre_low)
        acc_hb[...] += fold(pre_low.astype(f32))
        second_grad = dot(hid_w[...], pre_low)
        grad = cot + norm_back_rows(second_grad, normed, inverse, gain)
        middle_grad[j] = grad
        branch = grad.astype(bf16)
        acc_cols[0] += fold(branch.astype(f32))
        acc_cols[1] += fold(second_grad * normed)
        acc_cols[2] += fold(second_grad)
        acc_cols[3] += fold(cot)
        acc_o[...] += dot_lanes(branch, att_low[...])
        att_grad[...] = dot(out_w[...], branch)

        def back(h):
            rows = slice(h * s.head, (h + 1) * s.head)
            upstream = att_grad[rows, :]
            inverse = over[h : h + 1, :]
            numer = upstream * inverse
            denom = -jnp.sum(upstream * att[rows, :], 0, keepdims=True) * inverse
            tail_shape = (ext - s.head, s.genes)
            tail = jnp.where(row_index(tail_shape) == 0, denom, 0.0)
            high, low = split_low(jnp.concatenate([numer, tail], 0))
            value = feats[h]
            gap = jnp.zeros((LANES - ext, s.genes), bf16)
            sums = dot_lanes(value.astype(bf16), jnp.concatenate([high, gap, low, gap], 0))
            values_grad[h] += sums[:, :LANES] + sums[:, LANES:]
            back_feats = dot(kv3[h], jnp.concatenate([high, high, low], 0)) * value
            query = qkv[base + j, rows, :].astype(f32)
            total = jnp.sum(back_feats, 0, keepdims=True)
            result = scale * dot(draws_t[h], back_feats.astype(bf16)) - query * (total * (scale * scale))
            query_grad[rows, :] = result.astype(bf16)

        for h in range(s.heads):
            back(h)
        normal = (norm_rows(x)[0] * cols[:, 0:1] + cols[:, 1:2]).astype(bf16)
        acc_q[...] += dot_lanes(normal, query_grad[...])
        query_part[j] = dot(joint[:, : s.inner], query_grad[...])
        return carry

    lax.fori_loop(0, count, block, 0)
    for n in range(count):
        outputs[n][...] = out_all[n]
    if not final:
        if not first:
            results[0][...], results[1][...] = kv3[...], kv_t[...]
        for result, acc in zip(results[2:], sums):
            result[...] = acc[...]
        return
    results[0][...] = values_grad[...]
    keep, send = results[1:]
    spare = s.hidden % LANES
    lane = lane_index((s.width, LANES))
    last = jnp.zeros((s.width, LANES), f32)
    spot = 2 * spare
    for n in range(4):
        last = jnp.where(lane == spot, jnp.sum(acc_cols[n], 1, keepdims=True), last)
        spot += 1
    for n in range(s.hidden // s.width):
        piece = acc_hb[n * s.width : (n + 1) * s.width, :]
        last = jnp.where(lane == spot, jnp.sum(piece, 1, keepdims=True), last)
        spot += 1
    if spare:
        tops = [acc[:, s.hidden - spare :] for acc in (acc_r, acc_h)]
        last = jnp.concatenate(tops + [last[:, 2 * spare :]], 1)
    tiles = []
    for acc in (acc_q, acc_o, acc_r, acc_h):
        tiles += [(acc, n * LANES) for n in range(acc.shape[1] // LANES)]
    deal_tiles(side[0], s.width, keep, send, tiles, last)


def deal_tiles(side, width, keep, send, tiles, last):
    half = keep.shape[0]

    def put(row, value):
        for part in (0, 1):
            begin, end = max(row, part * half), min(row + value.shape[0], (part + 1) * half)
            if begin < end:
                piece = value[begin - row : end - row]
                spots = slice(begin - part * half, end - part * half)
                if send is None:
                    keep[spots, :] = piece
                    continue

                @pl.when(side == part)
                def _():
                    keep[spots, :] = piece

                @pl.when(side != part)
                def _():
                    send[spots, :] = piece

    row = 0
    for acc, at in tiles:
        put(row, acc[:, at : at + LANES])
        row += width
    put(row, last)
    row += width
    total = half if send is None else 2 * half
    if row < total:
        put(row, jnp.zeros((total - row, LANES), f32))


def padded(rows, parts):
    return -(-rows // (8 * parts)) * 8 * parts


def halves(s, tiles, parts):
    rows = padded(tiles * s.width, parts)
    return [array(rows // 2, LANES), array(rows // 2, LANES)]


def run_middle(s, parts, side, groups, kv_own, kv_other, shifted, qkv, cots, weights):
    sums = [
        array(s.width, s.inner),
        array(s.width, s.inner),
        array(s.width, s.hidden),
        array(s.width, s.hidden),
        array(4, s.width, LANES),
        array(s.hidden, LANES),
        array(s.heads, s.rows, LANES),
    ]
    forms = [
        array(s.heads, s.rows, 3 * s.ext, dtype=bf16),
        array(s.heads, 2 * s.ext, s.rows, dtype=bf16),
    ]
    ends = [array(s.heads, s.rows, LANES)]
    ends += halves(s, 2 * (s.inner // LANES) + 2 * (s.hidden // LANES) + 1, parts)
    before, base = [kv_own, kv_other], 0
    outputs, middle_grad, query_part = [], [], []
    for index, count in enumerate(groups):
        first, final = index == 0, index == len(groups) - 1
        tokens = array(count, s.width, s.genes)
        out = [array(s.width, s.genes)] * count + [tokens, tokens]
        out += ends if final else forms + sums
        scratch = list(forms) if first and final else []
        scratch += [
            array(s.heads, s.rows, s.genes),
            array(s.inner, s.genes),
            array(s.inner, s.genes, dtype=bf16),
            array(16, s.genes),
            array(s.inner, s.genes),
            array(s.inner, s.genes, dtype=bf16),
            tokens,
            tokens,
        ] + sums
        scratch = [pltpu.VMEM(a.shape, a.dtype) for a in scratch]
        args = [side[None], *before, shifted, qkv, *cots[base : base + count], *weights]
        body = functools.partial(middle_body, s, base, count, first, final)
        made = call("middle", body, args, out, scratch, 18, 1, flops=7e9 * count)
        outputs += made[:count]
        middle_grad.append(made[count])
        query_part.append(made[count + 1])
        before, base = made[count + 2 :], base + count
    return outputs, middle_grad, query_part, before


def last_body(s, groups, *refs):
    refs = list(refs)
    place, vg_own, vg_other, kv_own, kv_other, shifted, qkv = (refs.pop(0) for _ in range(7))
    middle_grads = [refs.pop(0) for _ in groups]
    query_parts = [refs.pop(0) for _ in groups]
    cols, draws, draws_t, joint = (refs.pop(0) for _ in range(4))
    input_grad = [refs.pop(0) for _ in range(s.homes)]
    keep, send, vg2, vg_t, ext2, grads, result_all, acc, acc_cols = refs
    scale = s.scale
    ext = s.ext
    eye = eye_like(ext)
    peaks = []
    for h in range(s.heads):
        total = vg_own[h] + vg_other[h]
        inside = row_index(total.shape) < s.feats
        high, low = split_low(jnp.where(inside, total, 0.0)[:, :ext])
        vg2[h] = jnp.concatenate([high, low], 1)
        vg_t[h] = dot_lanes(eye, high)[: s.head].astype(bf16)
        peaks.append(jnp.maximum(kv_own[h, s.rows - 1 :, 0:1], kv_other[h, s.rows - 1 :, 0:1]))
    tail = (s.heads, ext - s.head, s.genes)
    ones = jnp.where(row_index(tail) == 0, 1.0, 0.0).astype(bf16)
    ext2[:, s.head : ext, :] = ones
    ext2[:, ext + s.head :, :] = ones
    acc[...] = jnp.zeros_like(acc)
    acc_cols[...] = jnp.zeros_like(acc_cols)

    def block(base, middle_grad, query_part, i, carry):
        j = base + i
        valid = place[j] + lane_index((1, s.genes)) < place[s.homes]

        def head(h):
            rows = slice(h * s.head, (h + 1) * s.head)
            key = qkv[j, s.inner + h * s.head : s.inner + (h + 1) * s.head, :]
            value = qkv[j, 2 * s.inner + h * s.head : 2 * s.inner + (h + 1) * s.head, :]
            ext2[h, : s.head, :] = value
            ext2[h, ext : ext + s.head, :] = value
            key_f = key.astype(f32)
            cut = jnp.sum(key_f * key_f, 0, keepdims=True) * (scale * scale * 0.5)
            cut = jnp.where(valid, cut + peaks[h], 1e30)
            feats = jnp.exp(scale * dot(draws[h], key) - cut)
            back_feats = dot(vg2[h], ext2[h]) * feats
            total = jnp.sum(back_feats, 0, keepdims=True)
            result = scale * dot(draws_t[h], back_feats.astype(bf16)) - key_f * (total * (scale * scale))
            grads[rows, :] = result.astype(bf16)
            result = dot(vg_t[h], feats.astype(bf16))
            grads[s.inner + h * s.head : s.inner + (h + 1) * s.head, :] = result.astype(bf16)

        for h in range(s.heads):
            head(h)
        normed, inverse = norm_rows(shifted[j])
        gain = cols[:, 0:1]
        first = (normed * gain + cols[:, 1:2]).astype(bf16)
        acc[...] += dot_lanes(first, grads[...])
        first_grad = query_part[i] + dot(joint[:, s.inner :], grads[...])
        result = middle_grad[i] + norm_back_rows(first_grad, normed, inverse, gain)
        result_all[j] = result
        acc_cols[0] += fold(first_grad * normed)
        acc_cols[1] += fold(first_grad)
        acc_cols[2] += fold(result)
        return carry

    base = 0
    for count, middle_grad, query_part in zip(groups, middle_grads, query_parts):
        lax.fori_loop(0, count, functools.partial(block, base, middle_grad, query_part), 0)
        base += count
    for n in range(s.homes):
        input_grad[n][...] = result_all[n]
    lane = lane_index((s.width, LANES))
    sums = [jnp.sum(acc_cols[n], 1, keepdims=True) for n in range(3)]
    last = jnp.where(lane == 0, sums[0], jnp.where(lane == 1, sums[1], 0.0))
    last = jnp.where(lane == 2 + place[s.homes + 1], sums[2], last)
    tiles = [(acc, n * LANES) for n in range(acc.shape[1] // LANES)]
    deal_tiles(place[s.homes + 2], s.width, keep, send, tiles, last)


def run_last(s, parts, groups, place, vg_own, vg_other, kv_own, kv_other, shifted, qkv, middle_grad, query_part, weights):
    out = [array(s.width, s.genes)] * s.homes + halves(s, 2 * (s.inner // LANES) + 1, parts)
    scratch = [
        pltpu.VMEM((s.heads, s.rows, 2 * s.ext), bf16),
        pltpu.VMEM((s.heads, s.head, s.rows), bf16),
        pltpu.VMEM((s.heads, 2 * s.ext, s.genes), bf16),
        pltpu.VMEM((2 * s.inner, s.genes), bf16),
        pltpu.VMEM((s.homes, s.width, s.genes), f32),
        pltpu.VMEM((s.width, 2 * s.inner), f32),
        pltpu.VMEM((3, s.width, LANES), f32),
    ]
    args = [place, vg_own, vg_other, kv_own, kv_other, shifted, qkv, *middle_grad, *query_part, *weights]
    return call("last", functools.partial(last_body, s, groups), args, out, scratch, 10, 1, flops=15e9)


def partners(size, step):
    return [(i, i ^ step) for i in range(size)]


def send(values, axis, size):
    return [lax.ppermute(values[k], axis, partners(size, k)) for k in range(1, size)]


def add_split(index, terms, parts):
    rows = terms[0].shape[0] // parts

    def body(place, *refs):
        ins, outs = refs[: len(terms)], refs[len(terms) :]
        for k in range(parts):
            at = pl.multiple_of((place[0] ^ k) * rows, 8) if parts > 1 else 0
            total = ins[0][pl.ds(at, rows), :]
            for other in ins[1:]:
                total = total + other[pl.ds(at, rows), :]
            outs[k][...] = total

    out = [array(rows, LANES)] * parts
    return call("add_split", body, [index[None], *terms], out, smem=1, flops=1e9)


def stack_rows(pieces):
    def body(*refs):
        at = 0
        for ref in refs[:-1]:
            refs[-1][at : at + ref.shape[0], :] = ref[...]
            at += ref.shape[0]

    return call("stack", body, pieces, array(sum(p.shape[0] for p in pieces), LANES), flops=5e8)


def place_blocks(s, home, blocks):
    def body(place, *refs):
        for k in range(s.homes):
            refs[-1][place[0] ^ k] = refs[k][...]

    return call("place_blocks", body, [home[None], *blocks], array(s.homes, s.width, s.genes), smem=1, flops=1e9)


def finish_body(s, sizes, tissues, place, early_own, early_other, late_own, late_other, *refs):
    early, late = refs[-2:]
    outs = refs[:-2]
    if sizes is None:
        early[...] = early_own[...]
        late[...] = late_own[...]
    else:
        cells, homes = sizes
        for whole_ref, sources in ((early, (early_own, early_other)), (late, (late_own, late_other))):
            rows = whole_ref.shape[0] // (2 * cells * homes)
            for a in range(2):
                for b in range(cells):
                    for c in range(homes):
                        spot = ((place[0] ^ a) * cells + (place[1] ^ b)) * homes + (place[2] ^ c)
                        at = (b * homes + c) * rows
                        whole_ref[pl.ds(pl.multiple_of(spot * rows, 8), rows), :] = sources[a][at : at + rows, :]
    ni, nh, spare = s.inner // LANES, s.hidden // LANES, s.hidden % LANES
    w = s.width

    def tile(ref, n):
        return ref[n * w : (n + 1) * w, :]

    joint, out_t, hid, ret_t, ob, sg, sb, rb, hb, tissue, fg, fb = outs
    for n in range(ni):
        joint[:, n * LANES : (n + 1) * LANES] = tile(early, n)
        out_t[:, n * LANES : (n + 1) * LANES] = tile(early, ni + n)
    for n in range(2 * ni):
        joint[:, (ni + n) * LANES : (ni + n + 1) * LANES] = tile(late, n)
    for n in range(nh):
        ret_t[:, n * LANES : (n + 1) * LANES] = tile(early, 2 * ni + n)
        hid[:, n * LANES : (n + 1) * LANES] = tile(early, 2 * ni + nh + n)
    mixed = tile(early, 2 * ni + 2 * nh)
    ret_t[:, nh * LANES :] = mixed[:, :spare]
    hid[:, nh * LANES :] = mixed[:, spare : 2 * spare]
    columns = mixed.T
    at = 2 * spare
    for ref in (ob, sg, sb, rb):
        ref[...] = columns[at : at + 1, :]
        at += 1
    hb[...] = columns[at : at + s.hidden // w, :]
    columns = tile(late, 2 * ni).T
    fg[...] = columns[0:1, :]
    fb[...] = columns[1:2, :]
    tissue[...] = columns[2 : 2 + tissues, :]


def finish(s, sizes, tissues, place, early, late):
    w = s.width
    row = array(1, w)
    out = [array(w, 3 * s.inner), array(w, s.inner), array(w, s.hidden), array(w, s.hidden)]
    out += [row, row, row, row, array(s.hidden // w, w), array(tissues, w), row, row]
    doubled = 1 if sizes is None else 2
    scratch = [pltpu.VMEM((doubled * b[0].shape[0], LANES), f32) for b in (early, late)]
    body = functools.partial(finish_body, s, sizes, tissues)
    return call("finish", body, [place, *early, *late], out, scratch, 8, 1, flops=3e9)


def solution(mesh):
    def run(inputs, lengths, *others):
        cells_axis, genes_axis = mesh.shape["cells"], mesh.shape["genes"]
        homes = inputs.shape[0] // cells_axis
        rest = genes_axis // homes
        sizes = {"cells": cells_axis, "home": homes, "rest": rest}
        fine = Mesh(mesh.devices.reshape(cells_axis, homes, rest), ("cells", "home", "rest"))
        tokens = P("cells", ("home", "rest"), None)
        return jax.shard_map(
            lambda *args: local(sizes, *args),
            mesh=fine,
            in_specs=(tokens, P("cells"), P("cells")) + (P(),) * 13 + (tokens,),
            out_specs=(tokens, tokens) + (P(),) * 12,
            check_vma=False,
        )(inputs, lengths, *others)

    return run


def after(value, *others):
    return lax.optimization_barrier((value, *others))[0]


def local(
    sizes,
    inputs,
    lengths,
    tissue_ids,
    tissue_table,
    first_gain,
    first_bias,
    joint_weight,
    feature_draws,
    output_weight,
    output_bias,
    second_gain,
    second_bias,
    hidden_weight,
    hidden_bias,
    return_weight,
    return_bias,
    cotangent,
):
    s = Sizes(sizes, inputs, feature_draws, hidden_weight)
    homes, rest, cells = s.homes, s.rest, sizes["cells"]
    parts = cells * homes * rest
    home = lax.axis_index("home").astype(jnp.int32)
    side = lax.axis_index("rest").astype(jnp.int32)
    half_side = side % 2
    cell = lax.axis_index("cells").astype(jnp.int32)
    paired = rest == 2

    def pick(array, k):
        return lax.dynamic_index_in_dim(array, home ^ k, 0, False)

    inputs_t = inputs.transpose(0, 2, 1)
    cot_t = cotangent.transpose(0, 2, 1)
    mine = [pick(inputs_t, k) for k in range(homes)]
    arrived = send(mine, "home", homes)
    my_cots = [pick(cot_t, k).astype(f32) for k in range(homes)]
    tissue = pick(tissue_ids, 0)
    starts = [(((home ^ k) * rest + side) * s.genes) for k in range(homes)]
    place = jnp.stack(starts + [pick(lengths, 0), tissue, half_side]).astype(jnp.int32)
    rows = (first_gain, first_bias, output_bias, second_gain, second_bias, return_bias)
    joint_t, draws, draws_t, out_wt, out_w, hid_w, hid_wt, ret_wt, ret_w, joint, cols, bias = prepare(
        s,
        tissue,
        joint_weight,
        feature_draws.transpose(0, 2, 1),
        output_weight.T,
        hidden_weight,
        return_weight.T,
        hidden_bias,
        rows,
        tissue_table,
    )
    state = run_keys(s, 0, 1, place, mine[:1], cols, joint_t, draws)
    late_cots = [my_cots[0]] + [after(c, *arrived) for c in my_cots[1:]]
    arrived_cot = my_cots[:1] + send(late_cots, "home", homes)
    if homes > 1:
        state = run_keys(s, 1, homes - 1, place, arrived, cols, joint_t, draws, state)
    kv, shifted, qkv = state

    def other(value):
        return lax.ppermute(value, "rest", partners(2, 1))

    if paired:
        kv_other = other(after(kv, arrived_cot[1]))
    else:
        last_row = (jnp.arange(s.rows) == s.rows - 1)[None, :, None]
        if rest > 2:
            peak = kv[:, -1:, :]
            top = lax.pmax(peak, "rest")
            kv = lax.psum(kv * jnp.exp(peak - top), "rest")
            kv = jnp.where(last_row, top, kv)
        kv_other = jnp.where(last_row, LOWEST, jnp.zeros_like(kv))
    weights = (cols, bias, draws, draws_t, out_w, out_wt, hid_w, hid_wt, ret_w, ret_wt, joint)
    groups = (homes // 2, homes - homes // 2) if homes > 1 else (homes,)
    out_blocks, middle_grad, query_part, made = run_middle(
        s, parts, half_side, groups, kv, kv_other, shifted, qkv, arrived_cot, weights
    )
    vg, early_keep, early_send = made
    vg_other = other(vg) if paired else jnp.zeros_like(vg)
    if rest > 2:
        vg = lax.psum(vg, "rest")
    made = run_last(
        s,
        parts,
        groups,
        place,
        vg,
        vg_other,
        kv,
        kv_other,
        shifted,
        qkv,
        middle_grad,
        query_part,
        (cols, draws, draws_t, joint),
    )
    grad_blocks, late_keep, late_send = made[:homes], made[homes], made[homes + 1]

    def return_home(own, received):
        return place_blocks(s, home, [own] + received).transpose(0, 2, 1)

    out_received = send(out_blocks, "home", homes)
    grad_received = send(grad_blocks, "home", homes)

    if paired and cells in (2, 4) and homes in (2, 4):

        def spread(pieces, axis, size):
            return [pieces[0]] + send(pieces, axis, size)

        def repeated(piece, axis, size):
            return [piece] + send([piece] * size, axis, size)

        early = spread(add_split(cell, [early_keep, other(early_send)], cells), "cells", cells)
        outputs = return_home(out_blocks[0], out_received)
        late_send = after(late_send, *out_received, *early[1:])
        made = add_split(cell, [late_keep, other(late_send)], cells)
        late = spread(made, "cells", cells)
        early[0] = after(early[0], made[0])
        early = spread(add_split(home, early, homes), "home", homes)
        late[0] = after(late[0], outputs)
        made = add_split(home, late, homes)
        late = spread(made, "home", homes)
        early[0] = after(early[0], made[0])
        early = repeated(add_split(home, early, 1)[0], "home", homes)
        made = add_split(home, late, 1)[0]
        late = repeated(made, "home", homes)
        early[0] = after(early[0], made)
        early = repeated(stack_rows(early), "cells", cells)
        late[0] = after(late[0], *grad_received)
        made = stack_rows(late)
        late = repeated(made, "cells", cells)
        early[0] = after(early[0], made)
        early = stack_rows(early)
        late = stack_rows(late)
        early, late = (early, other(early)), (late, other(late))
        order = (cells, homes)
    else:
        axes = ("rest", "cells", "home")

        def summed(keep, sent):
            swap = half_side == 1
            whole_sum = jnp.where(swap, jnp.concatenate([sent, keep]), jnp.concatenate([keep, sent]))
            total = lax.psum(whole_sum, axes)
            return total, total

        outputs = return_home(out_blocks[0], out_received)
        early, late, order = summed(early_keep, early_send), summed(late_keep, late_send), None
    joint_grad, out_t, hid, ret_t, ob, sg, sb, rb, hb, tissue_grad, fg, fb = finish(
        s, order, tissue_table.shape[0], jnp.stack([side, cell, home]), early, late
    )
    return (
        outputs,
        return_home(grad_blocks[0], grad_received),
        tissue_grad,
        fg[0],
        fb[0],
        joint_grad,
        out_t.T,
        ob[0],
        sg[0],
        sb[0],
        hid,
        hb.reshape(-1),
        ret_t.T,
        rb[0],
    )
```

profile of v0, /device:TPU:0, one launch (start us, length us, event | category | flops | bytes accessed | tf_op | source)
XLA Modules:
  0.0 173.4 jit_solution(18411427327100809978)
XLA Ops:
  2.2 4.1 %collective-permute-start.1 = (f32[200,256]{1,0:T(8,128)S(1)}, f32[200,256]{1,0:T(8,128)S(1)}, u32[]{:S(2)}, u32[]{:S(2)}) collective-permute-start(f32[200,256]{1,0:T(8,128)S(1)} %get-tuple-element.181), channel_id=1, source_target_pairs={{0,4},{2,6},{4,0},{6,2},{1,5},{3,7},{5,1},{7,3},{8,12},{10,14},{12... | collective-permute-start | bytes 614408 | tf_op jit(solution)/shard_map/ppermute | solution.py:549
  15.0 1.8 %prepare.1 = (bf16[1920,200]{1,0:T(8,128)(2,1)S(1)}, bf16[10,272,64]{2,1,0:T(8,128)(2,1)S(1)}, bf16[10,64,272]{2,1,0:T(8,128)(2,1)S(1)}, bf16[200,640]{1,0:T(8,1...) custom-call(s32[1]{0:T(128)} %dynamic_slice.34.tissue, ...), custom_call_target="tpu_custom_call" | custom-call | flops 4000000000 | bytes 1024 | tf_op jit(solution)/shard_map/prepare/pallas_call | solution.py:78
  16.9 2.5 %keys.2 = (f32[10,272,128]{2,1,0:T(8,128)S(1)}, f32[4,200,256]{2,1,0:T(8,128)S(1)}, bf16[4,1920,256]{2,1,0:T(8,128)(2,1)S(1)}) custom-call(s32[7]{0:T(128)S(1)} %stack.36.refs_0_, f32[200,256]{1,0:T(8,128)S(1)} %get-tuple-element.180.refs_1_, f32[200,8]{1,0:T(8,128)S(1)} %get-tuple-element.97.refs_2_.refs_4_.refs_7_.refs_14_.refs_11_, ...), custom_call_target="tpu_custom_call" | custom-call | flops 3000000000 | bytes 1024 | tf_op jit(solution)/shard_map/keys/pallas_call | solution.py:78
  19.5 1.8 %collective-permute-done.2.refs_3_ = f32[200,256]{1,0:T(8,128)S(1)} collective-permute-done((f32[200,256]{1,0:T(8,128)S(1)}, f32[200,256]{1,0:T(8,128)S(1)}, u32[]{:S(2)}, u32[]{:S(2)}) %collective-permute-start.2) | collective-permute-done | bytes 204832 | tf_op jit(solution)/shard_map/ppermute | solution.py:549
  21.4 3.9 %collective-permute-start.3 = (f32[200,256]{1,0:T(8,128)S(1)}, f32[200,256]{1,0:T(8,128)S(1)}, u32[]{:S(2)}, u32[]{:S(2)}) collective-permute-start(f32[200,256]{1,0:T(8,128)S(1)} %get-tuple-element.104), channel_id=1, source_target_pairs={{0,2},{2,0},{4,6},{6,4},{1,3},{3,1},{5,7},{7,5},{8,10},{10,8},{12,... | collective-permute-start | bytes 614408 | tf_op jit(solution)/shard_map/ppermute | solution.py:549
  25.3 6.3 %keys.3 = (f32[10,272,128]{2,1,0:T(8,128)S(1)}, f32[4,200,256]{2,1,0:T(8,128)S(1)}, bf16[4,1920,256]{2,1,0:T(8,128)(2,1)S(1)}) custom-call(s32[7]{0:T(128)S(1)} %stack.36.refs_0_, f32[200,256]{1,0:T(8,128)S(1)} %collective-permute-done.refs_1_, f32[200,256]{1,0:T(8,128)S(1)} %collective-permute-done.1.refs_2_, ...), custom_call_target="tpu_custom_call", output_to_operand_aliasing={{1}: (8, {}), {2}: (9, {})} | custom-call | flops 8999999488 | bytes 1024 | tf_op jit(solution)/shard_map/keys/pallas_call | solution.py:78
  31.6 2.5 %collective-permute-start.6 = (f32[200,256]{1,0:T(8,128)S(1)}, f32[200,256]{1,0:T(8,128)S(1)}, u32[]{:S(2)}, u32[]{:S(2)}) collective-permute-start(f32[200,256]{1,0:T(8,128)S(1)} %get-tuple-element.128), channel_id=1, source_target_pairs={{0,4},{2,6},{4,0},{6,2},{1,5},{3,7},{5,1},{7,3},{8,12},{10,14},{12... | collective-permute-start | bytes 614408 | tf_op jit(solution)/shard_map/ppermute | solution.py:549
  35.2 14.5 %middle.2 = (f32[200,256]{1,0:T(8,128)S(1)}, f32[200,256]{1,0:T(8,128)}, f32[2,200,256]{2,1,0:T(8,128)S(1)}, f32[2,200,256]{2,1,0:T(8,128)S(1)}, bf16[10,272,240...) custom-call(s32[1]{0:T(128)} %bitcast.1.refs_0_, ...), custom_call_target="tpu_custom_call" | custom-call | flops 14000000000 | bytes 1024 | tf_op jit(solution)/shard_map/middle/pallas_call | solution.py:78
  50.5 14.8 %middle.3 = (f32[200,256]{1,0:T(8,128)S(1)}, f32[200,256]{1,0:T(8,128)S(1)}, f32[2,200,256]{2,1,0:T(8,128)S(1)}, f32[2,200,256]{2,1,0:T(8,128)S(1)}, f32[10,272,...) custom-call(s32[1]{0:T(128)} %bitcast.1.refs_0_, ...), custom_call_target="tpu_custom_call" | custom-call | flops 14000000000 | bytes 1024 | tf_op jit(solution)/shard_map/middle/pallas_call | solution.py:78
  68.4 3.3 %collective-permute-start.5 = (f32[200,256]{1,0:T(8,128)}, f32[200,256]{1,0:T(8,128)S(1)}, u32[]{:S(2)}, u32[]{:S(2)}) collective-permute-start(f32[200,256]{1,0:T(8,128)} %get-tuple-element.118), channel_id=1, source_target_pairs={{0,2},{2,0},{4,6},{6,4},{1,3},{3,1},{5,7},{7,5},{8,10},{10,8},{12,... | collective-permute-start | bytes 614408 | tf_op jit(solution)/shard_map/ppermute | solution.py:549
  71.8 1.9 %collective-permute-start.8 = (f32[200,256]{1,0:T(8,128)S(1)}, f32[200,256]{1,0:T(8,128)S(1)}, u32[]{:S(2)}, u32[]{:S(2)}) collective-permute-start(f32[200,256]{1,0:T(8,128)S(1)} %get-tuple-element.130), channel_id=1, source_target_pairs={{0,4},{2,6},{4,0},{6,2},{1,5},{3,7},{5,1},{7,3},{8,12},{10,14},{12... | collective-permute-start | bytes 614408 | tf_op jit(solution)/shard_map/ppermute | solution.py:549
  79.6 1.9 %collective-permute-done.5.refs_1_ = f32[200,256]{1,0:T(8,128)S(1)} collective-permute-done((f32[200,256]{1,0:T(8,128)}, f32[200,256]{1,0:T(8,128)S(1)}, u32[]{:S(2)}, u32[]{:S(2)}) %collective-permute-start.5) | collective-permute-done | bytes 204832 | tf_op jit(solution)/shard_map/ppermute | solution.py:549
  84.5 2.1 %copy-done.17 = bf16[4,1920,256]{2,1,0:T(8,128)(2,1)S(1)} copy-done((bf16[4,1920,256]{2,1,0:T(8,128)(2,1)S(1)}, bf16[4,1920,256]{2,1,0:T(8,128)(2,1)}, u32[]{:S(2)}) %copy-start.17) | copy-done | bytes 3932184
  88.6 14.6 %last.1 = (f32[200,256]{1,0:T(8,128)S(1)}, f32[200,256]{1,0:T(8,128)S(1)}, f32[200,256]{1,0:T(8,128)S(1)}, f32[200,256]{1,0:T(8,128)S(1)}, f32[1152,128]{1,0:T(8,128)S(1)}, /*index=5*/f32[1152,128]{1,0:T(8,128)S(1)}) custom-call(s32[7]{0:T(128)S(1)} %stack.36.refs_0_, f32[10,272,128]{2,1,0:T(8,128)} %get-tuple-element.132.refs_1_, ...), custom_call_target="tpu_custom_call" | custom-call | flops 15000000512 | bytes 1024 | tf_op jit(solution)/shard_map/last/pallas_call | solution.py:78
  103.3 2.0 %collective-permute-done.18.refs_1_ = f32[1152,128]{1,0:T(8,128)S(1)} collective-permute-done((f32[1152,128]{1,0:T(8,128)S(1)}, f32[1152,128]{1,0:T(8,128)S(1)}, u32[]{:S(2)}, u32[]{:S(2)}) %collective-permute-start.18) | collective-permute-done | bytes 589856 | tf_op jit(solution)/shard_map/ppermute | solution.py:727
  109.9 2.1 %collective-permute-start.12 = (f32[200,256]{1,0:T(8,128)S(1)}, f32[200,256]{1,0:T(8,128)S(1)}, u32[]{:S(2)}, u32[]{:S(2)}) collective-permute-start(f32[200,256]{1,0:T(8,128)S(1)} %get-tuple-element.139), channel_id=1, source_target_pairs={{0,4},{2,6},{4,0},{6,2},{1,5},{3,7},{5,1},{7,3},{8,12},{10,14},{12... | collective-permute-start | bytes 614408 | tf_op jit(solution)/shard_map/ppermute | solution.py:549
  113.8 2.2 %collective-permute-start.23 = (f32[144,128]{1,0:T(8,128)S(1)}, f32[144,128]{1,0:T(8,128)S(1)}, u32[]{:S(2)}, u32[]{:S(2)}) collective-permute-start(f32[144,128]{1,0:T(8,128)S(1)} %get-tuple-element.160), channel_id=1, source_target_pairs={{0,4},{2,6},{4,0},{6,2},{1,5},{3,7},{5,1},{7,3},{8,12},{10,14},{12... | collective-permute-start | bytes 221192 | tf_op jit(solution)/shard_map/ppermute | solution.py:549
  117.0 4.8 %collective-permute-done.22.refs_1_ = f32[144,128]{1,0:T(8,128)S(1)} collective-permute-done((f32[144,128]{1,0:T(8,128)S(1)}, f32[144,128]{1,0:T(8,128)S(1)}, u32[]{:S(2)}, u32[]{:S(2)}) %collective-permute-start.22) | collective-permute-done | bytes 73760 | tf_op jit(solution)/shard_map/ppermute | solution.py:549
  121.8 2.1 %collective-permute-start.25 = (f32[72,128]{1,0:T(8,128)S(1)}, f32[72,128]{1,0:T(8,128)S(1)}, u32[]{:S(2)}, u32[]{:S(2)}) collective-permute-start(f32[72,128]{1,0:T(8,128)S(1)} %get-tuple-element.162), channel_id=1, source_target_pairs={{0,2},{2,0},{4,6},{6,4},{1,3},{3,1},{5,7},{7,5},{8,10},{10,8},{12,... | collective-permute-start | bytes 110600 | tf_op jit(solution)/shard_map/ppermute | solution.py:549
  123.9 4.3 %collective-permute-done.23.refs_2_ = f32[144,128]{1,0:T(8,128)S(1)} collective-permute-done((f32[144,128]{1,0:T(8,128)S(1)}, f32[144,128]{1,0:T(8,128)S(1)}, u32[]{:S(2)}, u32[]{:S(2)}) %collective-permute-start.23) | collective-permute-done | bytes 73760 | tf_op jit(solution)/shard_map/ppermute | solution.py:549
  129.4 2.7 %collective-permute-start.30 = (f32[144,128]{1,0:T(8,128)S(1)}, f32[144,128]{1,0:T(8,128)S(1)}, u32[]{:S(2)}, u32[]{:S(2)}) collective-permute-start(f32[144,128]{1,0:T(8,128)S(1)} %add_split.10.refs_0_), channel_id=1, source_target_pairs={{0,6},{2,4},{4,2},{6,0},{1,7},{3,5},{5,3},{7,1},{8,14},{10,12},{12... | collective-permute-start | bytes 221192 | tf_op jit(solution)/shard_map/ppermute | solution.py:549
  135.7 3.0 %collective-permute-done.29.refs_2_ = f32[144,128]{1,0:T(8,128)S(1)} collective-permute-done((f32[144,128]{1,0:T(8,128)S(1)}, f32[144,128]{1,0:T(8,128)S(1)}, u32[]{:S(2)}, u32[]{:S(2)}) %collective-permute-start.29) | collective-permute-done | bytes 73760 | tf_op jit(solution)/shard_map/ppermute | solution.py:549
  139.3 2.2 %collective-permute-start.36 = (f32[576,128]{1,0:T(8,128)S(1)}, f32[576,128]{1,0:T(8,128)S(1)}, u32[]{:S(2)}, u32[]{:S(2)}) collective-permute-start(f32[576,128]{1,0:T(8,128)S(1)} %stack.40.refs_0_), channel_id=1, source_target_pairs={{0,24},{8,16},{16,8},{24,0},{1,25},{9,17},{17,9},{25,1},{2,26},{10... | collective-permute-start | bytes 884744 | tf_op jit(solution)/shard_map/ppermute | solution.py:549
  144.4 2.2 %collective-permute-start.33 = (f32[72,128]{1,0:T(8,128)S(1)}, f32[72,128]{1,0:T(8,128)S(1)}, u32[]{:S(2)}, u32[]{:S(2)}) collective-permute-start(f32[72,128]{1,0:T(8,128)S(1)} %add_split.11.refs_0_), channel_id=1, source_target_pairs={{0,6},{2,4},{4,2},{6,0},{1,7},{3,5},{5,3},{7,1},{8,14},{10,12},{12... | collective-permute-start | bytes 110600 | tf_op jit(solution)/shard_map/ppermute | solution.py:549
  146.6 4.1 %collective-permute-done.13.refs_3_ = f32[200,256]{1,0:T(8,128)S(1)} collective-permute-done((f32[200,256]{1,0:T(8,128)S(1)}, f32[200,256]{1,0:T(8,128)S(1)}, u32[]{:S(2)}, u32[]{:S(2)}) %collective-permute-start.13) | collective-permute-done | bytes 204832 | tf_op jit(solution)/shard_map/ppermute | solution.py:549
  150.8 2.6 %collective-permute-start.32 = (f32[72,128]{1,0:T(8,128)S(1)}, f32[72,128]{1,0:T(8,128)S(1)}, u32[]{:S(2)}, u32[]{:S(2)}) collective-permute-start(f32[72,128]{1,0:T(8,128)S(1)} %add_split.11.refs_0_), channel_id=1, source_target_pairs={{0,4},{2,6},{4,0},{6,2},{1,5},{3,7},{5,1},{7,3},{8,12},{10,14},{12... | collective-permute-start | bytes 110600 | tf_op jit(solution)/shard_map/ppermute | solution.py:549
  153.4 2.3 %collective-permute-done.32.refs_2_ = f32[72,128]{1,0:T(8,128)S(1)} collective-permute-done((f32[72,128]{1,0:T(8,128)S(1)}, f32[72,128]{1,0:T(8,128)S(1)}, u32[]{:S(2)}, u32[]{:S(2)}) %collective-permute-start.32) | collective-permute-done | bytes 36896 | tf_op jit(solution)/shard_map/ppermute | solution.py:549
  155.6 1.7 collective-permute-done.31.refs_1_
  157.5 2.4 %collective-permute-start.40 = (f32[288,128]{1,0:T(8,128)S(1)}, f32[288,128]{1,0:T(8,128)S(1)}, u32[]{:S(2)}, u32[]{:S(2)}) collective-permute-start(f32[288,128]{1,0:T(8,128)S(1)} %stack.41.refs_0_), channel_id=1, source_target_pairs={{0,24},{8,16},{16,8},{24,0},{1,25},{9,17},{17,9},{25,1},{2,26},{10... | collective-permute-start | bytes 442376 | tf_op jit(solution)/shard_map/ppermute | solution.py:549
  161.1 4.1 %collective-permute-done.40.refs_3_ = f32[288,128]{1,0:T(8,128)S(1)} collective-permute-done((f32[288,128]{1,0:T(8,128)S(1)}, f32[288,128]{1,0:T(8,128)S(1)}, u32[]{:S(2)}, u32[]{:S(2)}) %collective-permute-start.40) | collective-permute-done | bytes 147488 | tf_op jit(solution)/shard_map/ppermute | solution.py:549
  165.1 2.7 %collective-permute-done.39.refs_2_ = f32[288,128]{1,0:T(8,128)S(1)} collective-permute-done((f32[288,128]{1,0:T(8,128)S(1)}, f32[288,128]{1,0:T(8,128)S(1)}, u32[]{:S(2)}, u32[]{:S(2)}) %collective-permute-start.39) | collective-permute-done | bytes 147488 | tf_op jit(solution)/shard_map/ppermute | solution.py:549
  170.1 2.6 %finish.1 = (f32[200,1920]{1,0:T(8,128)}, f32[200,640]{1,0:T(8,128)}, f32[200,800]{1,0:T(8,128)}, f32[200,800]{1,0:T(8,128)}, f32[1,200]{1,0:T(1,128)}, /*index=...) custom-call(s32[3]{0:T(128)S(1)} %pad_add_fusion.place, ...), custom_call_target="tpu_custom_call" | custom-call | flops 3000000000 | bytes 1024 | tf_op jit(solution)/shard_map/finish/pallas_call | solution.py:78
  (155 shorter events, 45.9 us)
Async XLA Ops:
  2.2 17.3 %collective-permute-start.1 = (f32[200,256]{1,0:T(8,128)S(1)}, f32[200,256]{1,0:T(8,128)S(1)}, u32[]{:S(2)}, u32[]{:S(2)}) collective-permute-start(f32[200,256]{1,0:T(8,128)S(1)} %get-tuple-element.181), channel_id=1, source_target_pairs={{0,4},{2,6},{4,0},{6,2},{1,5},{3,7},{5,1},{7,3},{8,12},{10,14},{12... | collective-permute-start | bytes 614408 | tf_op jit(solution)/shard_map/ppermute | solution.py:549
  6.3 13.2 %collective-permute-start = (f32[200,256]{1,0:T(8,128)S(1)}, f32[200,256]{1,0:T(8,128)S(1)}, u32[]{:S(2)}, u32[]{:S(2)}) collective-permute-start(f32[200,256]{1,0:T(8,128)S(1)} %get-tuple-element.182), channel_id=1, source_target_pairs={{0,2},{2,0},{4,6},{6,4},{1,3},{3,1},{5,7},{7,5},{8,10},{10,8},{12,... | collective-permute-start | bytes 614408 | tf_op jit(solution)/shard_map/ppermute | solution.py:549
  7.9 13.5 %collective-permute-start.2 = (f32[200,256]{1,0:T(8,128)S(1)}, f32[200,256]{1,0:T(8,128)S(1)}, u32[]{:S(2)}, u32[]{:S(2)}) collective-permute-start(f32[200,256]{1,0:T(8,128)S(1)} %get-tuple-element.183), channel_id=1, source_target_pairs={{0,6},{2,4},{4,2},{6,0},{1,7},{3,5},{5,3},{7,1},{8,14},{10,12},{12... | collective-permute-start | bytes 614408 | tf_op jit(solution)/shard_map/ppermute | solution.py:549
  21.4 10.2 %collective-permute-start.3 = (f32[200,256]{1,0:T(8,128)S(1)}, f32[200,256]{1,0:T(8,128)S(1)}, u32[]{:S(2)}, u32[]{:S(2)}) collective-permute-start(f32[200,256]{1,0:T(8,128)S(1)} %get-tuple-element.104), channel_id=1, source_target_pairs={{0,2},{2,0},{4,6},{6,4},{1,3},{3,1},{5,7},{7,5},{8,10},{10,8},{12,... | collective-permute-start | bytes 614408 | tf_op jit(solution)/shard_map/ppermute | solution.py:549
  31.6 18.8 %collective-permute-start.6 = (f32[200,256]{1,0:T(8,128)S(1)}, f32[200,256]{1,0:T(8,128)S(1)}, u32[]{:S(2)}, u32[]{:S(2)}) collective-permute-start(f32[200,256]{1,0:T(8,128)S(1)} %get-tuple-element.128), channel_id=1, source_target_pairs={{0,4},{2,6},{4,0},{6,2},{1,5},{3,7},{5,1},{7,3},{8,12},{10,14},{12... | collective-permute-start | bytes 614408 | tf_op jit(solution)/shard_map/ppermute | solution.py:549
  34.2 16.2 %collective-permute-start.7 = (f32[200,256]{1,0:T(8,128)S(1)}, f32[200,256]{1,0:T(8,128)S(1)}, u32[]{:S(2)}, u32[]{:S(2)}) collective-permute-start(f32[200,256]{1,0:T(8,128)S(1)} %get-tuple-element.129), channel_id=1, source_target_pairs={{0,6},{2,4},{4,2},{6,0},{1,7},{3,5},{5,3},{7,1},{8,14},{10,12},{12... | collective-permute-start | bytes 614408 | tf_op jit(solution)/shard_map/ppermute | solution.py:549
  67.9 15.1 %collective-permute-start.10 = (f32[10,272,128]{2,1,0:T(8,128)}, f32[10,272,128]{2,1,0:T(8,128)}, u32[]{:S(2)}, u32[]{:S(2)}) collective-permute-start(f32[10,272,128]{2,1,0:T(8,128)} %get-tuple-element.132.refs_1_), channel_id=1, source_target_pairs={{0,1},{1,0},{2,3},{3,2},{4,5},{5,4},{6,7},{7,6},{8,9},{9,8},{10,11... | collective-permute-start | bytes 4177928 | tf_op jit(solution)/shard_map/ppermute | solution.py:727
  68.0 7.2 %collective-permute-start.14 = (f32[2304,128]{1,0:T(8,128)}, f32[2304,128]{1,0:T(8,128)}, u32[]{:S(2)}, u32[]{:S(2)}) collective-permute-start(f32[2304,128]{1,0:T(8,128)} %get-tuple-element.142), channel_id=1, source_target_pairs={{0,1},{1,0},{2,3},{3,2},{4,5},{5,4},{6,7},{7,6},{8,9},{9,8},{10,11... | collective-permute-start | bytes 3538952 | tf_op jit(solution)/shard_map/ppermute | solution.py:727
  68.4 13.1 %collective-permute-start.5 = (f32[200,256]{1,0:T(8,128)}, f32[200,256]{1,0:T(8,128)S(1)}, u32[]{:S(2)}, u32[]{:S(2)}) collective-permute-start(f32[200,256]{1,0:T(8,128)} %get-tuple-element.118), channel_id=1, source_target_pairs={{0,2},{2,0},{4,6},{6,4},{1,3},{3,1},{5,7},{7,5},{8,10},{10,8},{12,... | collective-permute-start | bytes 614408 | tf_op jit(solution)/shard_map/ppermute | solution.py:549
  71.8 31.4 %collective-permute-start.8 = (f32[200,256]{1,0:T(8,128)S(1)}, f32[200,256]{1,0:T(8,128)S(1)}, u32[]{:S(2)}, u32[]{:S(2)}) collective-permute-start(f32[200,256]{1,0:T(8,128)S(1)} %get-tuple-element.130), channel_id=1, source_target_pairs={{0,4},{2,6},{4,0},{6,2},{1,5},{3,7},{5,1},{7,3},{8,12},{10,14},{12... | collective-permute-start | bytes 614408 | tf_op jit(solution)/shard_map/ppermute | solution.py:549
  73.7 29.5 %collective-permute-start.9 = (f32[200,256]{1,0:T(8,128)S(1)}, f32[200,256]{1,0:T(8,128)S(1)}, u32[]{:S(2)}, u32[]{:S(2)}) collective-permute-start(f32[200,256]{1,0:T(8,128)S(1)} %get-tuple-element.131), channel_id=1, source_target_pairs={{0,6},{2,4},{4,2},{6,0},{1,7},{3,5},{5,3},{7,1},{8,14},{10,12},{12... | collective-permute-start | bytes 614408 | tf_op jit(solution)/shard_map/ppermute | solution.py:549
  78.0 25.2 %collective-permute-start.15 = (f32[576,128]{1,0:T(8,128)S(1)}, f32[576,128]{1,0:T(8,128)S(1)}, u32[]{:S(2)}, u32[]{:S(2)}) collective-permute-start(f32[576,128]{1,0:T(8,128)S(1)} %get-tuple-element.146), channel_id=1, source_target_pairs={{0,8},{8,0},{16,24},{24,16},{1,9},{9,1},{17,25},{25,17},{2,10},{10... | collective-permute-start | bytes 884744 | tf_op jit(solution)/shard_map/ppermute | solution.py:549
  81.5 21.7 %collective-permute-start.16 = (f32[576,128]{1,0:T(8,128)S(1)}, f32[576,128]{1,0:T(8,128)S(1)}, u32[]{:S(2)}, u32[]{:S(2)}) collective-permute-start(f32[576,128]{1,0:T(8,128)S(1)} %get-tuple-element.147), channel_id=1, source_target_pairs={{0,16},{8,24},{16,0},{24,8},{1,17},{9,25},{17,1},{25,9},{2,18},{10... | collective-permute-start | bytes 884744 | tf_op jit(solution)/shard_map/ppermute | solution.py:549
  83.0 20.2 %collective-permute-start.17 = (f32[576,128]{1,0:T(8,128)S(1)}, f32[576,128]{1,0:T(8,128)S(1)}, u32[]{:S(2)}, u32[]{:S(2)}) collective-permute-start(f32[576,128]{1,0:T(8,128)S(1)} %get-tuple-element.148), channel_id=1, source_target_pairs={{0,24},{8,16},{16,8},{24,0},{1,25},{9,17},{17,9},{25,1},{2,26},{10... | collective-permute-start | bytes 884744 | tf_op jit(solution)/shard_map/ppermute | solution.py:549
  105.4 6.8 %collective-permute-start.19 = (f32[288,128]{1,0:T(8,128)S(1)}, f32[288,128]{1,0:T(8,128)S(1)}, u32[]{:S(2)}, u32[]{:S(2)}) collective-permute-start(f32[288,128]{1,0:T(8,128)S(1)} %get-tuple-element.154), channel_id=1, source_target_pairs={{0,8},{8,0},{16,24},{24,16},{1,9},{9,1},{17,25},{25,17},{2,10},{10... | collective-permute-start | bytes 442376 | tf_op jit(solution)/shard_map/ppermute | solution.py:549
  106.0 7.8 %collective-permute-start.20 = (f32[288,128]{1,0:T(8,128)S(1)}, f32[288,128]{1,0:T(8,128)S(1)}, u32[]{:S(2)}, u32[]{:S(2)}) collective-permute-start(f32[288,128]{1,0:T(8,128)S(1)} %get-tuple-element.155), channel_id=1, source_target_pairs={{0,16},{8,24},{16,0},{24,8},{1,17},{9,25},{17,1},{25,9},{2,18},{10... | collective-permute-start | bytes 442376 | tf_op jit(solution)/shard_map/ppermute | solution.py:549
  107.5 8.5 %collective-permute-start.21 = (f32[288,128]{1,0:T(8,128)S(1)}, f32[288,128]{1,0:T(8,128)S(1)}, u32[]{:S(2)}, u32[]{:S(2)}) collective-permute-start(f32[288,128]{1,0:T(8,128)S(1)} %get-tuple-element.156), channel_id=1, source_target_pairs={{0,24},{8,16},{16,8},{24,0},{1,25},{9,17},{17,9},{25,1},{2,26},{10... | collective-permute-start | bytes 442376 | tf_op jit(solution)/shard_map/ppermute | solution.py:549
  109.9 32.9 %collective-permute-start.11 = (f32[200,256]{1,0:T(8,128)S(1)}, f32[200,256]{1,0:T(8,128)S(1)}, u32[]{:S(2)}, u32[]{:S(2)}) collective-permute-start(f32[200,256]{1,0:T(8,128)S(1)} %get-tuple-element.138), channel_id=1, source_target_pairs={{0,2},{2,0},{4,6},{6,4},{1,3},{3,1},{5,7},{7,5},{8,10},{10,8},{12,... | collective-permute-start | bytes 614408 | tf_op jit(solution)/shard_map/ppermute | solution.py:549
  109.9 34.6 %collective-permute-start.12 = (f32[200,256]{1,0:T(8,128)S(1)}, f32[200,256]{1,0:T(8,128)S(1)}, u32[]{:S(2)}, u32[]{:S(2)}) collective-permute-start(f32[200,256]{1,0:T(8,128)S(1)} %get-tuple-element.139), channel_id=1, source_target_pairs={{0,4},{2,6},{4,0},{6,2},{1,5},{3,7},{5,1},{7,3},{8,12},{10,14},{12... | collective-permute-start | bytes 614408 | tf_op jit(solution)/shard_map/ppermute | solution.py:549
  112.1 9.7 %collective-permute-start.22 = (f32[144,128]{1,0:T(8,128)S(1)}, f32[144,128]{1,0:T(8,128)S(1)}, u32[]{:S(2)}, u32[]{:S(2)}) collective-permute-start(f32[144,128]{1,0:T(8,128)S(1)} %get-tuple-element.159), channel_id=1, source_target_pairs={{0,2},{2,0},{4,6},{6,4},{1,3},{3,1},{5,7},{7,5},{8,10},{10,8},{12,... | collective-permute-start | bytes 221192 | tf_op jit(solution)/shard_map/ppermute | solution.py:549
  113.8 14.4 %collective-permute-start.23 = (f32[144,128]{1,0:T(8,128)S(1)}, f32[144,128]{1,0:T(8,128)S(1)}, u32[]{:S(2)}, u32[]{:S(2)}) collective-permute-start(f32[144,128]{1,0:T(8,128)S(1)} %get-tuple-element.160), channel_id=1, source_target_pairs={{0,4},{2,6},{4,0},{6,2},{1,5},{3,7},{5,1},{7,3},{8,12},{10,14},{12... | collective-permute-start | bytes 221192 | tf_op jit(solution)/shard_map/ppermute | solution.py:549
  116.0 12.2 %collective-permute-start.24 = (f32[144,128]{1,0:T(8,128)S(1)}, f32[144,128]{1,0:T(8,128)S(1)}, u32[]{:S(2)}, u32[]{:S(2)}) collective-permute-start(f32[144,128]{1,0:T(8,128)S(1)} %get-tuple-element.161), channel_id=1, source_target_pairs={{0,6},{2,4},{4,2},{6,0},{1,7},{3,5},{5,3},{7,1},{8,14},{10,12},{12... | collective-permute-start | bytes 221192 | tf_op jit(solution)/shard_map/ppermute | solution.py:549
  121.8 7.6 %collective-permute-start.25 = (f32[72,128]{1,0:T(8,128)S(1)}, f32[72,128]{1,0:T(8,128)S(1)}, u32[]{:S(2)}, u32[]{:S(2)}) collective-permute-start(f32[72,128]{1,0:T(8,128)S(1)} %get-tuple-element.162), channel_id=1, source_target_pairs={{0,2},{2,0},{4,6},{6,4},{1,3},{3,1},{5,7},{7,5},{8,10},{10,8},{12,... | collective-permute-start | bytes 110600 | tf_op jit(solution)/shard_map/ppermute | solution.py:549
  139.3 18.1 %collective-permute-start.36 = (f32[576,128]{1,0:T(8,128)S(1)}, f32[576,128]{1,0:T(8,128)S(1)}, u32[]{:S(2)}, u32[]{:S(2)}) collective-permute-start(f32[576,128]{1,0:T(8,128)S(1)} %stack.40.refs_0_), channel_id=1, source_target_pairs={{0,24},{8,16},{16,8},{24,0},{1,25},{9,17},{17,9},{25,1},{2,26},{10... | collective-permute-start | bytes 884744 | tf_op jit(solution)/shard_map/ppermute | solution.py:549
  141.4 15.9 %collective-permute-start.35 = (f32[576,128]{1,0:T(8,128)S(1)}, f32[576,128]{1,0:T(8,128)S(1)}, u32[]{:S(2)}, u32[]{:S(2)}) collective-permute-start(f32[576,128]{1,0:T(8,128)S(1)} %stack.40.refs_0_), channel_id=1, source_target_pairs={{0,16},{8,24},{16,0},{24,8},{1,17},{9,25},{17,1},{25,9},{2,18},{10... | collective-permute-start | bytes 884744 | tf_op jit(solution)/shard_map/ppermute | solution.py:549
  141.4 15.9 %collective-permute-start.34 = (f32[576,128]{1,0:T(8,128)S(1)}, f32[576,128]{1,0:T(8,128)S(1)}, u32[]{:S(2)}, u32[]{:S(2)}) collective-permute-start(f32[576,128]{1,0:T(8,128)S(1)} %stack.40.refs_0_), channel_id=1, source_target_pairs={{0,8},{8,0},{16,24},{24,16},{1,9},{9,1},{17,25},{25,17},{2,10},{10... | collective-permute-start | bytes 884744 | tf_op jit(solution)/shard_map/ppermute | solution.py:549
  142.8 8.0 %collective-permute-start.13 = (f32[200,256]{1,0:T(8,128)S(1)}, f32[200,256]{1,0:T(8,128)S(1)}, u32[]{:S(2)}, u32[]{:S(2)}) collective-permute-start(f32[200,256]{1,0:T(8,128)S(1)} %get-tuple-element.140), channel_id=1, source_target_pairs={{0,6},{2,4},{4,2},{6,0},{1,7},{3,5},{5,3},{7,1},{8,14},{10,12},{12... | collective-permute-start | bytes 614408 | tf_op jit(solution)/shard_map/ppermute | solution.py:549
  144.4 8.9 %collective-permute-start.33 = (f32[72,128]{1,0:T(8,128)S(1)}, f32[72,128]{1,0:T(8,128)S(1)}, u32[]{:S(2)}, u32[]{:S(2)}) collective-permute-start(f32[72,128]{1,0:T(8,128)S(1)} %add_split.11.refs_0_), channel_id=1, source_target_pairs={{0,6},{2,4},{4,2},{6,0},{1,7},{3,5},{5,3},{7,1},{8,14},{10,12},{12... | collective-permute-start | bytes 110600 | tf_op jit(solution)/shard_map/ppermute | solution.py:549
  157.4 12.6 %collective-permute-start.37 = (f32[2304,128]{1,0:T(8,128)S(1)}, f32[2304,128]{1,0:T(8,128)S(1)}, u32[]{:S(2)}, u32[]{:S(2)}) collective-permute-start(f32[2304,128]{1,0:T(8,128)S(1)} %stack.42.early_own), channel_id=1, source_target_pairs={{0,1},{1,0},{2,3},{3,2},{4,5},{5,4},{6,7},{7,6},{8,9},{9,8},{10,11... | collective-permute-start | bytes 3538952 | tf_op jit(solution)/shard_map/ppermute | solution.py:727
  157.5 7.6 %collective-permute-start.40 = (f32[288,128]{1,0:T(8,128)S(1)}, f32[288,128]{1,0:T(8,128)S(1)}, u32[]{:S(2)}, u32[]{:S(2)}) collective-permute-start(f32[288,128]{1,0:T(8,128)S(1)} %stack.41.refs_0_), channel_id=1, source_target_pairs={{0,24},{8,16},{16,8},{24,0},{1,25},{9,17},{17,9},{25,1},{2,26},{10... | collective-permute-start | bytes 442376 | tf_op jit(solution)/shard_map/ppermute | solution.py:549
  160.0 7.9 %collective-permute-start.39 = (f32[288,128]{1,0:T(8,128)S(1)}, f32[288,128]{1,0:T(8,128)S(1)}, u32[]{:S(2)}, u32[]{:S(2)}) collective-permute-start(f32[288,128]{1,0:T(8,128)S(1)} %stack.41.refs_0_), channel_id=1, source_target_pairs={{0,16},{8,24},{16,0},{24,8},{1,17},{9,25},{17,1},{25,9},{2,18},{10... | collective-permute-start | bytes 442376 | tf_op jit(solution)/shard_map/ppermute | solution.py:549
  160.0 8.0 %collective-permute-start.38 = (f32[288,128]{1,0:T(8,128)S(1)}, f32[288,128]{1,0:T(8,128)S(1)}, u32[]{:S(2)}, u32[]{:S(2)}) collective-permute-start(f32[288,128]{1,0:T(8,128)S(1)} %stack.41.refs_0_), channel_id=1, source_target_pairs={{0,8},{8,0},{16,24},{24,16},{1,9},{9,1},{17,25},{25,17},{2,10},{10... | collective-permute-start | bytes 442376 | tf_op jit(solution)/shard_map/ppermute | solution.py:549
  (48 other events, 381.6 us)
where the time goes:
time: 174 us; the launch traced here: 173 us
  Pallas kernels  61 us (35%)
  starting transfers between devices  55.3 us (32%)
  waiting for transfers between devices  37.9 us (22%)
  local copies, waits for them, and re-layouts  17.9 us (10%)
    pallas_call x19, Pallas kernels, call(): pl.pallas_call(body, out_shape=out, in_specs=[SMEM] * smem + [VMEM] * (le...  61 us
    ppermute x36, starting transfers between devices, send(): lax.ppermute(values[k], axis, partners(size, k))  54.5 us
    ppermute x36, waiting for transfers between devices, send(): lax.ppermute(values[k], axis, partners(size, k))  34.9 us
    unnamed x76, local copies, waits for them, and re-layouts  13.2 us
  transfers between devices with their start and end apart: 42, of which 19 were waited for; matrix products, arithmetic and copies ran while one was open for 2% of the time, Pallas kernels for 25%

commit v1 on v0

--- a/solution.py
+++ b/solution.py
@@ -70,6 +70,7 @@
         self.scale = self.head ** (-0.25)
 
 
+FIRST_MB, FINAL_MB, LAST_MB = 13, 15, 12
 VMEM = pl.BlockSpec(memory_space=pltpu.VMEM)
 SMEM = pl.BlockSpec(memory_space=pltpu.SMEM)
 
@@ -92,7 +93,7 @@
     return jax.ShapeDtypeStruct(shape, dtype)
 
 
-def prepare_body(s, tissue, joint, draws, out_t, hid, ret_t, hidden_bias, *refs):
+def prepare_body(s, place, joint, draws, out_t, hid, ret_t, hidden_bias, *refs):
     rows, table = refs[:6], refs[6]
     joint_t, draws_low, draws_t, out_wt, out_w, hid_w, hid_wt, ret_wt, ret_w, joint_w, cols, bias = refs[7:]
     joint_w[...] = joint[...].astype(bf16)
@@ -108,13 +109,13 @@
     hid_wt[...] = hid[...].T.astype(bf16)
     ret_wt[...] = ret_t[...].astype(bf16)
     ret_w[...] = ret_t[...].T.astype(bf16)
-    stacked = [r[...] for r in rows] + [table[pl.ds(tissue[0], 1), :]]
+    stacked = [r[...] for r in rows] + [table[pl.ds(place[s.homes + 1], 1), :]]
     stacked += [jnp.zeros((1, s.width), f32)]
     cols[...] = jnp.concatenate(stacked, 0).T
     bias[...] = jnp.broadcast_to(hidden_bias[...], (8, s.hidden)).T
 
 
-def prepare(s, tissue, joint, draws, out_t, hid, ret_t, hidden_bias, rows, table):
+def prepare(s, place, joint, draws, out_t, hid, ret_t, hidden_bias, rows, table):
     w, i, f = s.width, s.inner, s.hidden
     out = [
         array(3 * i, w, dtype=bf16),
@@ -130,7 +131,7 @@
         array(w, 8),
         array(f, 8),
     ]
-    args = [tissue[None], joint, draws, out_t, hid, ret_t, hidden_bias[None], *[r[None] for r in rows], table]
+    args = [place, joint, draws, out_t, hid, ret_t, hidden_bias[None], *[r[None] for r in rows], table]
     return call("prepare", functools.partial(prepare_body, s), args, out, smem=1, megabytes=8, flops=4e9)
 
 
@@ -228,21 +229,21 @@
         del refs[:n]
         return taken
 
-    (side,) = take(1)
+    (place,) = take(1)
     before = take(2) if first else take(9)
     shifted, qkv = take(2)
     cots = take(count)
     cols, hidden_bias, draws, draws_t, out_w, out_wt = take(6)
     hid_w, hid_wt, ret_w, ret_wt, joint = take(5)
-    outputs = take(count)
-    middle_grad, query_part = take(2)
+    outputs, middle_grad, query_part = take(3)
     results = take(3) if final else take(9)
     if first:
         kv3, kv_t = take(2) if final else results[:2]
     else:
         kv3, kv_t = before[:2]
     feats, att, att_low, over, att_grad, query_grad = take(6)
-    cot_all, out_all, *sums = refs
+    cot_all, acts, pre_grads = take(3)
+    sums = refs if final else results[2:]
     acc_q, acc_o, acc_r, acc_h, acc_cols, acc_hb, values_grad = sums
     scale = s.scale
     ext = s.ext
@@ -286,18 +287,23 @@
         normed, inverse = norm_rows(middle)
         gain = cols[:, 3:4]
         second = (normed * gain + cols[:, 4:5]).astype(bf16)
-        pre = dot(hid_wt[...], second) + hidden_bias[:, 0:1]
-        cumulative = 0.5 * (1.0 + lax.erf(pre * 0.7071067811865476))
-        act = (pre * cumulative).astype(bf16)
-        slope = cumulative + pre * (jnp.exp(-0.5 * pre * pre) * 0.3989422804014327)
-        out_all[j] = middle + dot(ret_wt[...], act) + cols[:, 5:6]
         cot = cot_all[j]
         cot_low = cot.astype(bf16)
-        pre_low = (dot(ret_w[...], cot_low) * slope).astype(bf16)
-        acc_r[...] += dot_lanes(cot_low, act)
-        acc_h[...] += dot_lanes(second, pre_low)
-        acc_hb[...] += fold(pre_low.astype(f32))
-        second_grad = dot(hid_w[...], pre_low)
+        result = middle + cols[:, 5:6]
+        step = s.hidden // 2
+        for at in range(0, s.hidden, step):
+            part = slice(at, at + step)
+            pre = dot(hid_wt[part, :], second) + hidden_bias[part, 0:1]
+            cumulative = 0.5 * (1.0 + lax.erf(pre * 0.7071067811865476))
+            acts[part, :] = (pre * cumulative).astype(bf16)
+            slope = cumulative + pre * (jnp.exp(-0.5 * pre * pre) * 0.3989422804014327)
+            pre_low = (dot(ret_w[part, :], cot_low) * slope).astype(bf16)
+            pre_grads[part, :] = pre_low
+            acc_hb[part, :] += fold(pre_low.astype(f32))
+        outputs[j] = result + dot(ret_wt[...], acts[...])
+        acc_r[...] += dot_lanes(cot_low, acts[...])
+        acc_h[...] += dot_lanes(second, pre_grads[...])
+        second_grad = dot(hid_w[...], pre_grads[...])
         grad = cot + norm_back_rows(second_grad, normed, inverse, gain)
         middle_grad[j] = grad
         branch = grad.astype(bf16)
@@ -335,13 +341,9 @@
         return carry
 
     lax.fori_loop(0, count, block, 0)
-    for n in range(count):
-        outputs[n][...] = out_all[n]
     if not final:
         if not first:
             results[0][...], results[1][...] = kv3[...], kv_t[...]
-        for result, acc in zip(results[2:], sums):
-            result[...] = acc[...]
         return
     results[0][...] = values_grad[...]
     keep, send = results[1:]
@@ -362,7 +364,7 @@
     tiles = []
     for acc in (acc_q, acc_o, acc_r, acc_h):
         tiles += [(acc, n * LANES) for n in range(acc.shape[1] // LANES)]
-    deal_tiles(side[0], s.width, keep, send, tiles, last)
+    deal_tiles(place[s.homes + 2], s.width, keep, send, tiles, last)
 
 
 def deal_tiles(side, width, keep, send, tiles, last):
@@ -406,7 +408,7 @@
     return [array(rows // 2, LANES), array(rows // 2, LANES)]
 
 
-def run_middle(s, parts, side, groups, kv_own, kv_other, shifted, qkv, cots, weights):
+def run_middle(s, parts, place, groups, kv_own, kv_other, shifted, qkv, cots, weights):
     sums = [
         array(s.width, s.inner),
         array(s.width, s.inner),
@@ -427,7 +429,7 @@
     for index, count in enumerate(groups):
         first, final = index == 0, index == len(groups) - 1
         tokens = array(count, s.width, s.genes)
-        out = [array(s.width, s.genes)] * count + [tokens, tokens]
+        out = [tokens, tokens, tokens]
         out += ends if final else forms + sums
         scratch = list(forms) if first and final else []
         scratch += [
@@ -438,16 +440,18 @@
             array(s.inner, s.genes),
             array(s.inner, s.genes, dtype=bf16),
             tokens,
-            tokens,
-        ] + sums
+            array(s.hidden, s.genes, dtype=bf16),
+            array(s.hidden, s.genes, dtype=bf16),
+        ]
+        scratch += sums if final else []
         scratch = [pltpu.VMEM(a.shape, a.dtype) for a in scratch]
-        args = [side[None], *before, shifted, qkv, *cots[base : base + count], *weights]
+        args = [place, *before, shifted, qkv, *cots[base : base + count], *weights]
         body = functools.partial(middle_body, s, base, count, first, final)
-        made = call("middle", body, args, out, scratch, 18, 1, flops=7e9 * count)
-        outputs += made[:count]
-        middle_grad.append(made[count])
-        query_part.append(made[count + 1])
-        before, base = made[count + 2 :], base + count
+        made = call("middle", body, args, out, scratch, FINAL_MB if final else FIRST_MB, 1, flops=7e9 * count)
+        outputs.append(made[0])
+        middle_grad.append(made[1])
+        query_part.append(made[2])
+        before, base = made[3:], base + count
     return outputs, middle_grad, query_part, before
 
 
@@ -513,8 +517,8 @@
         return carry
 
     base = 0
-    for count, middle_grad, query_part in zip(groups, middle_grads, query_parts):
-        lax.fori_loop(0, count, functools.partial(block, base, middle_grad, query_part), 0)
+    for n, count in enumerate(groups):
+        lax.fori_loop(0, count, functools.partial(block, base, middle_grads[n], query_parts[n]), 0)
         base += count
     for n in range(s.homes):
         input_grad[n][...] = result_all[n]
@@ -538,7 +542,7 @@
         pltpu.VMEM((3, s.width, LANES), f32),
     ]
     args = [place, vg_own, vg_other, kv_own, kv_other, shifted, qkv, *middle_grad, *query_part, *weights]
-    return call("last", functools.partial(last_body, s, groups), args, out, scratch, 10, 1, flops=15e9)
+    return call("last", functools.partial(last_body, s, groups), args, out, scratch, LAST_MB, 1, flops=15e9)
 
 
 def partners(size, step):
@@ -549,20 +553,37 @@
     return [lax.ppermute(values[k], axis, partners(size, k)) for k in range(1, size)]
 
 
-def add_split(index, terms, parts):
+def add_split(place, spot, terms, parts):
     rows = terms[0].shape[0] // parts
 
-    def body(place, *refs):
+    def body(numbers, *refs):
         ins, outs = refs[: len(terms)], refs[len(terms) :]
         for k in range(parts):
-            at = pl.multiple_of((place[0] ^ k) * rows, 8) if parts > 1 else 0
+            at = pl.multiple_of((numbers[spot] ^ k) * rows, 8) if parts > 1 else 0
             total = ins[0][pl.ds(at, rows), :]
             for other in ins[1:]:
                 total = total + other[pl.ds(at, rows), :]
             outs[k][...] = total
 
     out = [array(rows, LANES)] * parts
-    return call("add_split", body, [index[None], *terms], out, smem=1, flops=1e9)
+    return call("add_split", body, [place, *terms], out, smem=1, flops=1e9)
+
+
+def meet(place, spot, early, late, parts):
+    first, second = early[0].shape[0] // parts, late[0].shape[0] // parts
+
+    def body(numbers, *refs):
+        outs = refs[len(early) + len(late) :]
+        for terms, rows, begin in ((refs[: len(early)], first, 0), (refs[len(early) : -parts], second, first)):
+            for k in range(parts):
+                at = pl.multiple_of((numbers[spot] ^ k) * rows, 8)
+                total = terms[0][pl.ds(at, rows), :]
+                for other in terms[1:]:
+                    total = total + other[pl.ds(at, rows), :]
+                outs[k][begin : begin + rows, :] = total
+
+    out = [array(first + second, LANES)] * parts
+    return call("meet", body, [place, *early, *late], out, smem=1, flops=1e9)
 
 
 def stack_rows(pieces):
@@ -572,40 +593,62 @@
             refs[-1][at : at + ref.shape[0], :] = ref[...]
             at += ref.shape[0]
 
-    return call("stack", body, pieces, array(sum(p.shape[0] for p in pieces), LANES), flops=5e8)
-
-
-def place_blocks(s, home, blocks):
-    def body(place, *refs):
+    return call("stack", body, pieces, array(sum(p.shape[0] for p in pieces), LANES), flops=1e9)
+
+
+def forward_pair(near, far):
+    def body(near_ref, far_ref, out):
+        out[0] = near_ref[1]
+        out[1] = far_ref[1]
+
+    return call("forward_pair", body, [near, far], array(*near.shape), flops=1e9)
+
+
+def place_blocks(s, place, near, far, last):
+    def body(numbers, near_ref, far_ref, last_ref, out):
+        home = numbers[s.homes + 4]
+        out[home] = near_ref[0]
+        out[home ^ 1] = last_ref[0]
+        out[home ^ 2] = far_ref[0]
+        out[home ^ 3] = last_ref[1]
+
+    out = array(s.homes, s.width, s.genes)
+    made = call("place_blocks", body, [place, near, far, last], out, smem=1, flops=1e9)
+    return made.transpose(0, 2, 1)
+
+
+def place_apart(s, place, blocks):
+    def body(numbers, *refs):
         for k in range(s.homes):
-            refs[-1][place[0] ^ k] = refs[k][...]
-
-    return call("place_blocks", body, [home[None], *blocks], array(s.homes, s.width, s.genes), smem=1, flops=1e9)
-
-
-def finish_body(s, sizes, tissues, place, early_own, early_other, late_own, late_other, *refs):
+            refs[-1][numbers[s.homes + 4] ^ k] = refs[k][...]
+
+    out = array(s.homes, s.width, s.genes)
+    made = call("place_apart", body, [place, *blocks], out, smem=1, flops=1e9)
+    return made.transpose(0, 2, 1)
+
+
+def finish_body(s, split, tissues, rows, place, own, other, *refs):
     early, late = refs[-2:]
-    outs = refs[:-2]
-    if sizes is None:
-        early[...] = early_own[...]
-        late[...] = late_own[...]
+    joint, out_t, hid, ret_t, ob, sg, sb, rb, hb, tissue, fg, fb = refs[:-2]
+    first, second = rows
+    if split:
+        side, cell, home = (place[s.homes + n] for n in (2, 3, 4))
+        for core in range(2):
+            source = (own, other)[core]
+            for at in range(16):
+                spot = ((side ^ core) * 4 + (cell ^ (at // 4))) * 4 + (home ^ (at % 4))
+                begin = at * (first + second)
+                early[pl.ds(pl.multiple_of(spot * first, 8), first), :] = source[begin : begin + first, :]
+                late[pl.ds(pl.multiple_of(spot * second, 8), second), :] = source[begin + first : begin + first + second, :]
     else:
-        cells, homes = sizes
-        for whole_ref, sources in ((early, (early_own, early_other)), (late, (late_own, late_other))):
-            rows = whole_ref.shape[0] // (2 * cells * homes)
-            for a in range(2):
-                for b in range(cells):
-                    for c in range(homes):
-                        spot = ((place[0] ^ a) * cells + (place[1] ^ b)) * homes + (place[2] ^ c)
-                        at = (b * homes + c) * rows
-                        whole_ref[pl.ds(pl.multiple_of(spot * rows, 8), rows), :] = sources[a][at : at + rows, :]
+        early[...] = own[...]
+        late[...] = other[...]
     ni, nh, spare = s.inner // LANES, s.hidden // LANES, s.hidden % LANES
     w = s.width
 
     def tile(ref, n):
         return ref[n * w : (n + 1) * w, :]
 
-    joint, out_t, hid, ret_t, ob, sg, sb, rb, hb, tissue, fg, fb = outs
     for n in range(ni):
         joint[:, n * LANES : (n + 1) * LANES] = tile(early, n)
         out_t[:, n * LANES : (n + 1) * LANES] = tile(early, ni + n)
@@ -615,8 +658,9 @@
         ret_t[:, n * LANES : (n + 1) * LANES] = tile(early, 2 * ni + n)
         hid[:, n * LANES : (n + 1) * LANES] = tile(early, 2 * ni + nh + n)
     mixed = tile(early, 2 * ni + 2 * nh)
-    ret_t[:, nh * LANES :] = mixed[:, :spare]
-    hid[:, nh * LANES :] = mixed[:, spare : 2 * spare]
+    if spare:
+        ret_t[:, nh * LANES :] = mixed[:, :spare]
+        hid[:, nh * LANES :] = mixed[:, spare : 2 * spare]
     columns = mixed.T
     at = 2 * spare
     for ref in (ob, sg, sb, rb):
@@ -629,15 +673,14 @@
     tissue[...] = columns[2 : 2 + tissues, :]
 
 
-def finish(s, sizes, tissues, place, early, late):
+def finish(s, split, tissues, rows, place, own, other):
     w = s.width
     row = array(1, w)
     out = [array(w, 3 * s.inner), array(w, s.inner), array(w, s.hidden), array(w, s.hidden)]
     out += [row, row, row, row, array(s.hidden // w, w), array(tissues, w), row, row]
-    doubled = 1 if sizes is None else 2
-    scratch = [pltpu.VMEM((doubled * b[0].shape[0], LANES), f32) for b in (early, late)]
-    body = functools.partial(finish_body, s, sizes, tissues)
-    return call("finish", body, [place, *early, *late], out, scratch, 8, 1, flops=3e9)
+    scratch = [pltpu.VMEM((32 * n if split else ref.shape[0], LANES), f32) for n, ref in zip(rows, (own, other))]
+    body = functools.partial(finish_body, s, split, tissues, rows)
+    return call("finish", body, [place, own, other], out, scratch, 8, 1, flops=1e9)
 
 
 def solution(mesh):
@@ -695,18 +738,18 @@
     def pick(array, k):
         return lax.dynamic_index_in_dim(array, home ^ k, 0, False)
 
+    tissue = pick(tissue_ids, 0)
+    starts = [(((home ^ k) * rest + side) * s.genes) for k in range(homes)]
+    place = jnp.stack(starts + [pick(lengths, 0), tissue, half_side, cell, home]).astype(jnp.int32)
     inputs_t = inputs.transpose(0, 2, 1)
     cot_t = cotangent.transpose(0, 2, 1)
     mine = [pick(inputs_t, k) for k in range(homes)]
     arrived = send(mine, "home", homes)
     my_cots = [pick(cot_t, k).astype(f32) for k in range(homes)]
-    tissue = pick(tissue_ids, 0)
-    starts = [(((home ^ k) * rest + side) * s.genes) for k in range(homes)]
-    place = jnp.stack(starts + [pick(lengths, 0), tissue, half_side]).astype(jnp.int32)
     rows = (first_gain, first_bias, output_bias, second_gain, second_bias, return_bias)
     joint_t, draws, draws_t, out_wt, out_w, hid_w, hid_wt, ret_wt, ret_w, joint, cols, bias = prepare(
         s,
-        tissue,
+        place,
         joint_weight,
         feature_draws.transpose(0, 2, 1),
         output_weight.T,
@@ -737,9 +780,9 @@
             kv = jnp.where(last_row, top, kv)
         kv_other = jnp.where(last_row, LOWEST, jnp.zeros_like(kv))
     weights = (cols, bias, draws, draws_t, out_w, out_wt, hid_w, hid_wt, ret_w, ret_wt, joint)
-    groups = (homes // 2, homes - homes // 2) if homes > 1 else (homes,)
+    groups = (2, 2)
     out_blocks, middle_grad, query_part, made = run_middle(
-        s, parts, half_side, groups, kv, kv_other, shifted, qkv, arrived_cot, weights
+        s, parts, place, groups, kv, kv_other, shifted, qkv, arrived_cot, weights
     )
     vg, early_keep, early_send = made
     vg_other = other(vg) if paired else jnp.zeros_like(vg)
@@ -762,13 +805,15 @@
     )
     grad_blocks, late_keep, late_send = made[:homes], made[homes], made[homes + 1]
 
-    def return_home(own, received):
-        return place_blocks(s, home, [own] + received).transpose(0, 2, 1)
-
-    out_received = send(out_blocks, "home", homes)
+    out_far = lax.ppermute(out_blocks[1], "home", partners(homes, 2))
     grad_received = send(grad_blocks, "home", homes)
 
-    if paired and cells in (2, 4) and homes in (2, 4):
+    def finish_outputs(far):
+        near = lax.ppermute(forward_pair(out_blocks[0], far), "home", partners(homes, 1))
+        return place_blocks(s, place, out_blocks[0], far, near)
+
+    split = paired and cells == 4 and homes == 4
+    if split:
 
         def spread(pieces, axis, size):
             return [pieces[0]] + send(pieces, axis, size)
@@ -776,47 +821,34 @@
         def repeated(piece, axis, size):
             return [piece] + send([piece] * size, axis, size)
 
-        early = spread(add_split(cell, [early_keep, other(early_send)], cells), "cells", cells)
-        outputs = return_home(out_blocks[0], out_received)
-        late_send = after(late_send, *out_received, *early[1:])
-        made = add_split(cell, [late_keep, other(late_send)], cells)
-        late = spread(made, "cells", cells)
-        early[0] = after(early[0], made[0])
-        early = spread(add_split(home, early, homes), "home", homes)
-        late[0] = after(late[0], outputs)
-        made = add_split(home, late, homes)
-        late = spread(made, "home", homes)
-        early[0] = after(early[0], made[0])
-        early = repeated(add_split(home, early, 1)[0], "home", homes)
-        made = add_split(home, late, 1)[0]
-        late = repeated(made, "home", homes)
-        early[0] = after(early[0], made)
-        early = repeated(stack_rows(early), "cells", cells)
-        late[0] = after(late[0], *grad_received)
-        made = stack_rows(late)
-        late = repeated(made, "cells", cells)
-        early[0] = after(early[0], made)
-        early = stack_rows(early)
-        late = stack_rows(late)
-        early, late = (early, other(early)), (late, other(late))
-        order = (cells, homes)
+        outputs = finish_outputs(after(out_far, late_keep))
+        early = spread(add_split(place, homes + 3, [early_keep, other(early_send)], cells), "cells", cells)
+        late_send = after(late_send, out_far, *early[1:])
+        late = spread(add_split(place, homes + 3, [late_keep, other(late_send)], cells), "cells", cells)
+        rows = (early[0].shape[0] // homes, late[0].shape[0] // homes)
+        both = spread(meet(place, homes + 4, early, late, homes), "home", homes)
+        both[0] = after(both[0], outputs)
+        both = repeated(add_split(place, homes + 4, both, 1)[0], "home", homes)
+        both = repeated(stack_rows(both), "cells", cells)
+        both[0] = after(both[0], grad_received[1])
+        both = stack_rows(both)
+        sums = (both, other(after(both, grad_received[0], grad_received[2])))
     else:
         axes = ("rest", "cells", "home")
 
         def summed(keep, sent):
             swap = half_side == 1
             whole_sum = jnp.where(swap, jnp.concatenate([sent, keep]), jnp.concatenate([keep, sent]))
-            total = lax.psum(whole_sum, axes)
-            return total, total
-
-        outputs = return_home(out_blocks[0], out_received)
-        early, late, order = summed(early_keep, early_send), summed(late_keep, late_send), None
+            return lax.psum(whole_sum, axes)
+
+        outputs = finish_outputs(out_far)
+        sums, rows = (summed(early_keep, early_send), summed(late_keep, late_send)), (0, 0)
     joint_grad, out_t, hid, ret_t, ob, sg, sb, rb, hb, tissue_grad, fg, fb = finish(
-        s, order, tissue_table.shape[0], jnp.stack([side, cell, home]), early, late
+        s, split, tissue_table.shape[0], rows, place, *sums
     )
     return (
         outputs,
-        return_home(grad_blocks[0], grad_received),
+        place_apart(s, place, [grad_blocks[0]] + grad_received),
         tissue_grad,
         fg[0],
         fb[0],

time: 174 us -> 155 us (0.89)
  local copies, waits for them, and re-layouts: 17.9 us -> 9.12 us
  starting transfers between devices: 55.3 us -> 49 us
  waiting for transfers between devices: 37.9 us -> 35.3 us
    ppermute x36 -> x24, starting transfers between devices: 54.5 us -> 40.3 us  [send(): lax.ppermute(values[k], axis, partners(size, k))]
    unnamed x76 -> x32, local copies, waits for them, and re-layouts: 13.2 us -> 4.5 us
    ppermute x0 -> x2, starting transfers between devices: none -> 8.03 us  [the longest x1 6.17 us: local(): out_far = lax.ppermute(out_blocks[1], 'home', partners(homes, 2))]
    ppermute x36 -> x24, waiting for transfers between devices: 34.9 us -> 32.4 us  [send(): lax.ppermute(values[k], axis, partners(size, k))]
    pallas_call x19 -> x16, Pallas kernels: 61 us -> 60.5 us  [call(): pl.pallas_call(body, out_shape=out, in_specs=[SMEM] * smem + [VMEM] * (le...]
  transfers between devices with their start and end apart: 42 -> 31, of which waited for: 19 -> 12; matrix products, arithmetic and copies ran while one was open for 2% -> 2% of each run, Pallas kernels for 25% -> 28%
where the time goes in v1:
time: 155 us
  Pallas kernels  60.5 us (39%)
  starting transfers between devices  49 us (32%)
  waiting for transfers between devices  35.3 us (23%)
  local copies, waits for them, and re-layouts  9.12 us (6%)
    pallas_call x16, Pallas kernels, call(): pl.pallas_call(body, out_shape=out, in_specs=[SMEM] * smem + [VMEM] * (le...  60.5 us
    ppermute x24, starting transfers between devices, send(): lax.ppermute(values[k], axis, partners(size, k))  40.3 us
    ppermute x24, waiting for transfers between devices, send(): lax.ppermute(values[k], axis, partners(size, k))  32.4 us
    ppermute x1, starting transfers between devices, local(): out_far = lax.ppermute(out_blocks[1], 'home', partners(homes, 2))  6.17 us
    unnamed x32, local copies, waits for them, and re-layouts  4.5 us
  transfers between devices with their start and end apart: 31, of which 12 were waited for; matrix products, arithmetic and copies ran while one was open for 2% of the time, Pallas kernels for 28%

profile of v1, /device:TPU:0, one launch (start us, length us, event | category | flops | bytes accessed | tf_op | source)
XLA Modules:
  0.0 155.0 jit_solution(10352005179884110200)
XLA Ops:
  2.2 4.1 %collective-permute-start.1 = (f32[200,256]{1,0:T(8,128)S(1)}, f32[200,256]{1,0:T(8,128)S(1)}, u32[]{:S(2)}, u32[]{:S(2)}) collective-permute-start(f32[200,256]{1,0:T(8,128)S(1)} %get-tuple-element.165), channel_id=1, source_target_pairs={{0,4},{2,6},{4,0},{6,2},{1,5},{3,7},{5,1},{7,3},{8,12},{10,14},{12... | collective-permute-start | bytes 614408 | tf_op jit(solution)/shard_map/ppermute | solution.py:553
  6.3 1.6 %collective-permute-start = (f32[200,256]{1,0:T(8,128)S(1)}, f32[200,256]{1,0:T(8,128)S(1)}, u32[]{:S(2)}, u32[]{:S(2)}) collective-permute-start(f32[200,256]{1,0:T(8,128)S(1)} %get-tuple-element.166), channel_id=1, source_target_pairs={{0,2},{2,0},{4,6},{6,4},{1,3},{3,1},{5,7},{7,5},{8,10},{10,8},{12,... | collective-permute-start | bytes 614408 | tf_op jit(solution)/shard_map/ppermute | solution.py:553
  15.0 1.7 %prepare.1 = (bf16[1920,200]{1,0:T(8,128)(2,1)S(1)}, bf16[10,272,64]{2,1,0:T(8,128)(2,1)S(1)}, bf16[10,64,272]{2,1,0:T(8,128)(2,1)S(1)}, bf16[200,640]{1,0:T(8,1...) custom-call(s32[9]{0:T(128)S(1)} %stack.35.place.refs_0_.numbers, ...), custom_call_target="tpu_custom_call" | custom-call | flops 4000000000 | bytes 1024 | tf_op jit(solution)/shard_map/prepare/pallas_call | solution.py:79
  16.7 2.5 %keys.2 = (f32[10,272,128]{2,1,0:T(8,128)S(1)}, f32[4,200,256]{2,1,0:T(8,128)S(1)}, bf16[4,1920,256]{2,1,0:T(8,128)(2,1)S(1)}) custom-call(s32[9]{0:T(128)S(1)} %stack.35.place.refs_0_.numbers, f32[200,256]{1,0:T(8,128)S(1)} %get-tuple-element.164.refs_1_, f32[200,8]{1,0:T(8,128)S(1)} %get-tuple-element.89.refs_2_.refs_4_.refs_7_.refs_14_.refs_11_, ...), custom_call_target="tpu_custom_call" | custom-call | flops 3000000000 | bytes 1024 | tf_op jit(solution)/shard_map/keys/pallas_call | solution.py:79
  19.4 2.0 %collective-permute-done.2.refs_3_ = f32[200,256]{1,0:T(8,128)S(1)} collective-permute-done((f32[200,256]{1,0:T(8,128)S(1)}, f32[200,256]{1,0:T(8,128)S(1)}, u32[]{:S(2)}, u32[]{:S(2)}) %collective-permute-start.2) | collective-permute-done | bytes 204832 | tf_op jit(solution)/shard_map/ppermute | solution.py:553
  21.4 3.9 %collective-permute-start.3 = (f32[200,256]{1,0:T(8,128)S(1)}, f32[200,256]{1,0:T(8,128)S(1)}, u32[]{:S(2)}, u32[]{:S(2)}) collective-permute-start(f32[200,256]{1,0:T(8,128)S(1)} %get-tuple-element.96), channel_id=1, source_target_pairs={{0,2},{2,0},{4,6},{6,4},{1,3},{3,1},{5,7},{7,5},{8,10},{10,8},{12,... | collective-permute-start | bytes 614408 | tf_op jit(solution)/shard_map/ppermute | solution.py:553
  25.3 6.3 %keys.3 = (f32[10,272,128]{2,1,0:T(8,128)S(1)}, f32[4,200,256]{2,1,0:T(8,128)S(1)}, bf16[4,1920,256]{2,1,0:T(8,128)(2,1)S(1)}) custom-call(s32[9]{0:T(128)S(1)} %stack.35.place.refs_0_.numbers, f32[200,256]{1,0:T(8,128)S(1)} %collective-permute-done.refs_1_, ...), custom_call_target="tpu_custom_call", output_to_operand_aliasing={{1}: (8, {}), {2}: (9, {})} | custom-call | flops 8999999488 | bytes 1024 | tf_op jit(solution)/shard_map/keys/pallas_call | solution.py:79
  31.6 2.5 %collective-permute-start.5 = (f32[200,256]{1,0:T(8,128)S(1)}, f32[200,256]{1,0:T(8,128)S(1)}, u32[]{:S(2)}, u32[]{:S(2)}) collective-permute-start(f32[200,256]{1,0:T(8,128)S(1)} %get-tuple-element.119), channel_id=1, source_target_pairs={{0,4},{2,6},{4,0},{6,2},{1,5},{3,7},{5,1},{7,3},{8,12},{10,14},{12... | collective-permute-start | bytes 614408 | tf_op jit(solution)/shard_map/ppermute | solution.py:553
  35.2 14.3 %middle.2 = (f32[2,200,256]{2,1,0:T(8,128)S(1)}, f32[2,200,256]{2,1,0:T(8,128)S(1)}, f32[2,200,256]{2,1,0:T(8,128)S(1)}, bf16[10,272,240]{2,1,0:T(8,128)(2,1)S(1...) custom-call(s32[9]{0:T(128)S(1)} %stack.35.place.refs_0_.numbers, ...), custom_call_target="tpu_custom_call" | custom-call | flops 14000000000 | bytes 1024 | tf_op jit(solution)/shard_map/middle/pallas_call | solution.py:79
  49.5 13.7 %middle.3 = (f32[2,200,256]{2,1,0:T(8,128)S(1)}, f32[2,200,256]{2,1,0:T(8,128)S(1)}, f32[2,200,256]{2,1,0:T(8,128)S(1)}, f32[10,272,128]{2,1,0:T(8,128)S(1)}, f3...) custom-call(s32[9]{0:T(128)S(1)} %stack.35.place.refs_0_.numbers, bf16[10,272,240]{2,1,0:T(8,128)(2,1)S(1)} %get-tuple-element.110.refs_1_, ...), custom_call_target="tpu_custom_call" | custom-call | flops 14000000000 | bytes 1024 | tf_op jit(solution)/shard_map/middle/pallas_call | solution.py:79
  63.8 6.2 %collective-permute-start.7 = (f32[2,200,256]{2,1,0:T(8,128)S(1)}, f32[2,200,256]{2,1,0:T(8,128)S(1)}, u32[]{:S(2)}, u32[]{:S(2)}) collective-permute-start(f32[2,200,256]{2,1,0:T(8,128)S(1)} %get-tuple-element.121), channel_id=1, source_target_pairs={{0,4},{2,6},{4,0},{6,2},{1,5},{3,7},{5,1},{7,3},{8,12},{10,14},{12... | collective-permute-start | bytes 1228808 | tf_op jit(solution)/shard_map/ppermute | solution.py:808
  70.6 1.6 %collective-permute-start.14 = (f32[576,128]{1,0:T(8,128)S(1)}, f32[576,128]{1,0:T(8,128)S(1)}, u32[]{:S(2)}, u32[]{:S(2)}) collective-permute-start(f32[576,128]{1,0:T(8,128)S(1)} %get-tuple-element.136), channel_id=1, source_target_pairs={{0,8},{8,0},{16,24},{24,16},{1,9},{9,1},{17,25},{25,17},{2,10},{10... | collective-permute-start | bytes 884744 | tf_op jit(solution)/shard_map/ppermute | solution.py:553
  72.2 1.5 collective-permute-start.15
  74.2 13.6 %last.1 = (f32[200,256]{1,0:T(8,128)S(1)}, f32[200,256]{1,0:T(8,128)S(1)}, f32[200,256]{1,0:T(8,128)S(1)}, f32[200,256]{1,0:T(8,128)S(1)}, f32[1152,128]{1,0:T(8,128)S(1)}, /*index=5*/f32[1152,128]{1,0:T(8,128)S(1)}) custom-call(s32[9]{0:T(128)S(1)} %stack.35.place.refs_0_.numbers, f32[10,272,128]{2,1,0:T(8,128)S(1)} %get-tuple-element.122.refs_1_, ...), custom_call_target="tpu_custom_call" | custom-call | flops 15000000512 | bytes 1024 | tf_op jit(solution)/shard_map/last/pallas_call | solution.py:79
  88.5 1.9 %collective-permute-start.9 = (f32[2,200,256]{2,1,0:T(8,128)S(1)}, f32[2,200,256]{2,1,0:T(8,128)S(1)}, u32[]{:S(2)}, u32[]{:S(2)}) collective-permute-start(f32[2,200,256]{2,1,0:T(8,128)S(1)} %forward_pair.1), channel_id=1, source_target_pairs={{0,2},{2,0},{4,6},{6,4},{1,3},{3,1},{5,7},{7,5},{8,10},{10,8},{12,... | collective-permute-start | bytes 1228808 | tf_op jit(solution)/shard_map/ppermute | solution.py:812
  91.1 1.6 %collective-permute-start.18 = (f32[288,128]{1,0:T(8,128)S(1)}, f32[288,128]{1,0:T(8,128)S(1)}, u32[]{:S(2)}, u32[]{:S(2)}) collective-permute-start(f32[288,128]{1,0:T(8,128)S(1)} %get-tuple-element.142), channel_id=1, source_target_pairs={{0,8},{8,0},{16,24},{24,16},{1,9},{9,1},{17,25},{25,17},{2,10},{10... | collective-permute-start | bytes 442376 | tf_op jit(solution)/shard_map/ppermute | solution.py:553
  92.7 1.5 collective-permute-start.19
  94.7 3.1 %collective-permute-done.18.refs_5_ = f32[288,128]{1,0:T(8,128)S(1)} collective-permute-done((f32[288,128]{1,0:T(8,128)S(1)}, f32[288,128]{1,0:T(8,128)S(1)}, u32[]{:S(2)}, u32[]{:S(2)}) %collective-permute-start.18) | collective-permute-done | bytes 147488 | tf_op jit(solution)/shard_map/ppermute | solution.py:553
  97.8 3.7 %collective-permute-done.19.refs_6_ = f32[288,128]{1,0:T(8,128)S(1)} collective-permute-done((f32[288,128]{1,0:T(8,128)S(1)}, f32[288,128]{1,0:T(8,128)S(1)}, u32[]{:S(2)}, u32[]{:S(2)}) %collective-permute-start.19) | collective-permute-done | bytes 147488 | tf_op jit(solution)/shard_map/ppermute | solution.py:553
  102.1 1.9 %collective-permute-start.21 = (f32[216,128]{1,0:T(8,128)S(1)}, f32[216,128]{1,0:T(8,128)S(1)}, u32[]{:S(2)}, u32[]{:S(2)}) collective-permute-start(f32[216,128]{1,0:T(8,128)S(1)} %get-tuple-element.147), channel_id=1, source_target_pairs={{0,2},{2,0},{4,6},{6,4},{1,3},{3,1},{5,7},{7,5},{8,10},{10,8},{12,... | collective-permute-start | bytes 331784 | tf_op jit(solution)/shard_map/ppermute | solution.py:553
  104.0 2.1 %collective-permute-start.22 = (f32[216,128]{1,0:T(8,128)S(1)}, f32[216,128]{1,0:T(8,128)S(1)}, u32[]{:S(2)}, u32[]{:S(2)}) collective-permute-start(f32[216,128]{1,0:T(8,128)S(1)} %get-tuple-element.148), channel_id=1, source_target_pairs={{0,4},{2,6},{4,0},{6,2},{1,5},{3,7},{5,1},{7,3},{8,12},{10,14},{12... | collective-permute-start | bytes 331784 | tf_op jit(solution)/shard_map/ppermute | solution.py:553
  108.9 6.6 %collective-permute-done.22.refs_2_ = f32[216,128]{1,0:T(8,128)S(1)} collective-permute-done((f32[216,128]{1,0:T(8,128)S(1)}, f32[216,128]{1,0:T(8,128)S(1)}, u32[]{:S(2)}, u32[]{:S(2)}) %collective-permute-start.22) | collective-permute-done | bytes 110624 | tf_op jit(solution)/shard_map/ppermute | solution.py:553
  116.0 2.4 %collective-permute-start.26 = (f32[216,128]{1,0:T(8,128)S(1)}, f32[216,128]{1,0:T(8,128)S(1)}, u32[]{:S(2)}, u32[]{:S(2)}) collective-permute-start(f32[216,128]{1,0:T(8,128)S(1)} %add_split.5.refs_0_), channel_id=1, source_target_pairs={{0,6},{2,4},{4,2},{6,0},{1,7},{3,5},{5,3},{7,1},{8,14},{10,12},{12... | collective-permute-start | bytes 331784 | tf_op jit(solution)/shard_map/ppermute | solution.py:553
  120.5 3.4 %collective-permute-done.26.refs_3_ = f32[216,128]{1,0:T(8,128)S(1)} collective-permute-done((f32[216,128]{1,0:T(8,128)S(1)}, f32[216,128]{1,0:T(8,128)S(1)}, u32[]{:S(2)}, u32[]{:S(2)}) %collective-permute-start.26) | collective-permute-done | bytes 110624 | tf_op jit(solution)/shard_map/ppermute | solution.py:553
  123.9 3.3 %collective-permute-done.25.refs_2_ = f32[216,128]{1,0:T(8,128)S(1)} collective-permute-done((f32[216,128]{1,0:T(8,128)S(1)}, f32[216,128]{1,0:T(8,128)S(1)}, u32[]{:S(2)}, u32[]{:S(2)}) %collective-permute-start.25) | collective-permute-done | bytes 110624 | tf_op jit(solution)/shard_map/ppermute | solution.py:553
  128.4 1.8 %collective-permute-start.28 = (f32[864,128]{1,0:T(8,128)S(1)}, f32[864,128]{1,0:T(8,128)S(1)}, u32[]{:S(2)}, u32[]{:S(2)}) collective-permute-start(f32[864,128]{1,0:T(8,128)S(1)} %stack.36.refs_0_), channel_id=1, source_target_pairs={{0,16},{8,24},{16,0},{24,8},{1,17},{9,25},{17,1},{25,9},{2,18},{10... | collective-permute-start | bytes 1327112 | tf_op jit(solution)/shard_map/ppermute | solution.py:553
  131.4 3.2 %collective-permute-start.10 = (f32[200,256]{1,0:T(8,128)S(1)}, f32[200,256]{1,0:T(8,128)S(1)}, u32[]{:S(2)}, u32[]{:S(2)}) collective-permute-start(f32[200,256]{1,0:T(8,128)S(1)} %get-tuple-element.130), channel_id=1, source_target_pairs={{0,2},{2,0},{4,6},{6,4},{1,3},{3,1},{5,7},{7,5},{8,10},{10,8},{12,... | collective-permute-start | bytes 614408 | tf_op jit(solution)/shard_map/ppermute | solution.py:553
  134.6 5.8 %collective-permute-done.11.refs_2_ = f32[200,256]{1,0:T(8,128)S(1)} collective-permute-done((f32[200,256]{1,0:T(8,128)S(1)}, f32[200,256]{1,0:T(8,128)S(1)}, u32[]{:S(2)}, u32[]{:S(2)}) %collective-permute-start.11) | collective-permute-done | bytes 204832 | tf_op jit(solution)/shard_map/ppermute | solution.py:553
  140.4 3.0 %collective-permute-start.12 = (f32[200,256]{1,0:T(8,128)S(1)}, f32[200,256]{1,0:T(8,128)S(1)}, u32[]{:S(2)}, u32[]{:S(2)}) collective-permute-start(f32[200,256]{1,0:T(8,128)S(1)} %get-tuple-element.132), channel_id=1, source_target_pairs={{0,6},{2,4},{4,2},{6,0},{1,7},{3,5},{5,3},{7,1},{8,14},{10,12},{12... | collective-permute-start | bytes 614408 | tf_op jit(solution)/shard_map/ppermute | solution.py:553
  143.3 3.2 %collective-permute-done.28.refs_2_ = f32[864,128]{1,0:T(8,128)S(1)} collective-permute-done((f32[864,128]{1,0:T(8,128)S(1)}, f32[864,128]{1,0:T(8,128)S(1)}, u32[]{:S(2)}, u32[]{:S(2)}) %collective-permute-start.28) | collective-permute-done | bytes 442400 | tf_op jit(solution)/shard_map/ppermute | solution.py:553
  149.5 2.2 %collective-permute-done.30.other = f32[3456,128]{1,0:T(8,128)S(1)} collective-permute-done((f32[3456,128]{1,0:T(8,128)S(1)}, f32[3456,128]{1,0:T(8,128)S(1)}, u32[]{:S(2)}, u32[]{:S(2)}) %collective-permute-start.30) | collective-permute-done | bytes 1769504 | tf_op jit(solution)/shard_map/ppermute | solution.py:770
  151.7 2.6 %finish.1 = (f32[200,1920]{1,0:T(8,128)}, f32[200,640]{1,0:T(8,128)}, f32[200,800]{1,0:T(8,128)}, f32[200,800]{1,0:T(8,128)}, f32[1,200]{1,0:T(1,128)}, /*index=...) custom-call(s32[9]{0:T(128)S(1)} %stack.35.place.refs_0_.numbers, ...), custom_call_target="tpu_custom_call" | custom-call | flops 1000000000 | bytes 1024 | tf_op jit(solution)/shard_map/finish/pallas_call | solution.py:79
  (85 shorter events, 25.3 us)
Async XLA Ops:
  0.7 9.7 %copy-start.11 = (f32[200]{0:T(256)S(1)}, f32[200]{0:T(256)}, u32[]{:S(2)}) copy-start(f32[200]{0:T(256)} %param.32) | copy-start | bytes 2404
  2.2 17.2 %collective-permute-start.1 = (f32[200,256]{1,0:T(8,128)S(1)}, f32[200,256]{1,0:T(8,128)S(1)}, u32[]{:S(2)}, u32[]{:S(2)}) collective-permute-start(f32[200,256]{1,0:T(8,128)S(1)} %get-tuple-element.165), channel_id=1, source_target_pairs={{0,4},{2,6},{4,0},{6,2},{1,5},{3,7},{5,1},{7,3},{8,12},{10,14},{12... | collective-permute-start | bytes 614408 | tf_op jit(solution)/shard_map/ppermute | solution.py:553
  6.3 13.1 %collective-permute-start = (f32[200,256]{1,0:T(8,128)S(1)}, f32[200,256]{1,0:T(8,128)S(1)}, u32[]{:S(2)}, u32[]{:S(2)}) collective-permute-start(f32[200,256]{1,0:T(8,128)S(1)} %get-tuple-element.166), channel_id=1, source_target_pairs={{0,2},{2,0},{4,6},{6,4},{1,3},{3,1},{5,7},{7,5},{8,10},{10,8},{12,... | collective-permute-start | bytes 614408 | tf_op jit(solution)/shard_map/ppermute | solution.py:553
  7.9 13.5 %collective-permute-start.2 = (f32[200,256]{1,0:T(8,128)S(1)}, f32[200,256]{1,0:T(8,128)S(1)}, u32[]{:S(2)}, u32[]{:S(2)}) collective-permute-start(f32[200,256]{1,0:T(8,128)S(1)} %get-tuple-element.167), channel_id=1, source_target_pairs={{0,6},{2,4},{4,2},{6,0},{1,7},{3,5},{5,3},{7,1},{8,14},{10,12},{12... | collective-permute-start | bytes 614408 | tf_op jit(solution)/shard_map/ppermute | solution.py:553
  21.4 10.2 %collective-permute-start.3 = (f32[200,256]{1,0:T(8,128)S(1)}, f32[200,256]{1,0:T(8,128)S(1)}, u32[]{:S(2)}, u32[]{:S(2)}) collective-permute-start(f32[200,256]{1,0:T(8,128)S(1)} %get-tuple-element.96), channel_id=1, source_target_pairs={{0,2},{2,0},{4,6},{6,4},{1,3},{3,1},{5,7},{7,5},{8,10},{10,8},{12,... | collective-permute-start | bytes 614408 | tf_op jit(solution)/shard_map/ppermute | solution.py:553
  31.6 3.6 %collective-permute-start.4 = (f32[10,272,128]{2,1,0:T(8,128)S(1)}, f32[10,272,128]{2,1,0:T(8,128)S(1)}, u32[]{:S(2)}, u32[]{:S(2)}) collective-permute-start(f32[10,272,128]{2,1,0:T(8,128)S(1)} %get-tuple-element.97.refs_1_.refs_3_), channel_id=1, source_target_pairs={{0,1},{1,0},{2,3},{3,2},{4,5},{5,4},{6,7},{7,6},{8,9},{9,8},{10,11... | collective-permute-start | bytes 4177928 | tf_op jit(solution)/shard_map/ppermute | solution.py:770
  31.6 17.8 %collective-permute-start.5 = (f32[200,256]{1,0:T(8,128)S(1)}, f32[200,256]{1,0:T(8,128)S(1)}, u32[]{:S(2)}, u32[]{:S(2)}) collective-permute-start(f32[200,256]{1,0:T(8,128)S(1)} %get-tuple-element.119), channel_id=1, source_target_pairs={{0,4},{2,6},{4,0},{6,2},{1,5},{3,7},{5,1},{7,3},{8,12},{10,14},{12... | collective-permute-start | bytes 614408 | tf_op jit(solution)/shard_map/ppermute | solution.py:553
  34.2 15.3 %collective-permute-start.6 = (f32[200,256]{1,0:T(8,128)S(1)}, f32[200,256]{1,0:T(8,128)S(1)}, u32[]{:S(2)}, u32[]{:S(2)}) collective-permute-start(f32[200,256]{1,0:T(8,128)S(1)} %get-tuple-element.120), channel_id=1, source_target_pairs={{0,6},{2,4},{4,2},{6,0},{1,7},{3,5},{5,3},{7,1},{8,14},{10,12},{12... | collective-permute-start | bytes 614408 | tf_op jit(solution)/shard_map/ppermute | solution.py:553
  63.2 11.0 %collective-permute-start.8 = (f32[10,272,128]{2,1,0:T(8,128)S(1)}, f32[10,272,128]{2,1,0:T(8,128)S(1)}, u32[]{:S(2)}, u32[]{:S(2)}) collective-permute-start(f32[10,272,128]{2,1,0:T(8,128)S(1)} %get-tuple-element.122.refs_1_), channel_id=1, source_target_pairs={{0,1},{1,0},{2,3},{3,2},{4,5},{5,4},{6,7},{7,6},{8,9},{9,8},{10,11... | collective-permute-start | bytes 4177928 | tf_op jit(solution)/shard_map/ppermute | solution.py:770
  63.3 6.6 %collective-permute-start.13 = (f32[2304,128]{1,0:T(8,128)S(1)}, f32[2304,128]{1,0:T(8,128)S(1)}, u32[]{:S(2)}, u32[]{:S(2)}) collective-permute-start(f32[2304,128]{1,0:T(8,128)S(1)} %get-tuple-element.134), channel_id=1, source_target_pairs={{0,1},{1,0},{2,3},{3,2},{4,5},{5,4},{6,7},{7,6},{8,9},{9,8},{10,11... | collective-permute-start | bytes 3538952 | tf_op jit(solution)/shard_map/ppermute | solution.py:770
  63.8 24.7 %collective-permute-start.7 = (f32[2,200,256]{2,1,0:T(8,128)S(1)}, f32[2,200,256]{2,1,0:T(8,128)S(1)}, u32[]{:S(2)}, u32[]{:S(2)}) collective-permute-start(f32[2,200,256]{2,1,0:T(8,128)S(1)} %get-tuple-element.121), channel_id=1, source_target_pairs={{0,4},{2,6},{4,0},{6,2},{1,5},{3,7},{5,1},{7,3},{8,12},{10,14},{12... | collective-permute-start | bytes 1228808 | tf_op jit(solution)/shard_map/ppermute | solution.py:808
  70.6 17.8 %collective-permute-start.14 = (f32[576,128]{1,0:T(8,128)S(1)}, f32[576,128]{1,0:T(8,128)S(1)}, u32[]{:S(2)}, u32[]{:S(2)}) collective-permute-start(f32[576,128]{1,0:T(8,128)S(1)} %get-tuple-element.136), channel_id=1, source_target_pairs={{0,8},{8,0},{16,24},{24,16},{1,9},{9,1},{17,25},{25,17},{2,10},{10... | collective-permute-start | bytes 884744 | tf_op jit(solution)/shard_map/ppermute | solution.py:553
  72.2 16.3 %collective-permute-start.15 = (f32[576,128]{1,0:T(8,128)S(1)}, f32[576,128]{1,0:T(8,128)S(1)}, u32[]{:S(2)}, u32[]{:S(2)}) collective-permute-start(f32[576,128]{1,0:T(8,128)S(1)} %get-tuple-element.137), channel_id=1, source_target_pairs={{0,16},{8,24},{16,0},{24,8},{1,17},{9,25},{17,1},{25,9},{2,18},{10... | collective-permute-start | bytes 884744 | tf_op jit(solution)/shard_map/ppermute | solution.py:553
  73.7 14.7 %collective-permute-start.16 = (f32[576,128]{1,0:T(8,128)S(1)}, f32[576,128]{1,0:T(8,128)S(1)}, u32[]{:S(2)}, u32[]{:S(2)}) collective-permute-start(f32[576,128]{1,0:T(8,128)S(1)} %get-tuple-element.138), channel_id=1, source_target_pairs={{0,24},{8,16},{16,8},{24,0},{1,25},{9,17},{17,9},{25,1},{2,26},{10... | collective-permute-start | bytes 884744 | tf_op jit(solution)/shard_map/ppermute | solution.py:553
  88.4 2.1 %collective-permute-start.17 = (f32[1152,128]{1,0:T(8,128)S(1)}, f32[1152,128]{1,0:T(8,128)S(1)}, u32[]{:S(2)}, u32[]{:S(2)}) collective-permute-start(f32[1152,128]{1,0:T(8,128)S(1)} %get-tuple-element.140), channel_id=1, source_target_pairs={{0,1},{1,0},{2,3},{3,2},{4,5},{5,4},{6,7},{7,6},{8,9},{9,8},{10,11... | collective-permute-start | bytes 1769480 | tf_op jit(solution)/shard_map/ppermute | solution.py:770
  88.5 18.8 %collective-permute-start.9 = (f32[2,200,256]{2,1,0:T(8,128)S(1)}, f32[2,200,256]{2,1,0:T(8,128)S(1)}, u32[]{:S(2)}, u32[]{:S(2)}) collective-permute-start(f32[2,200,256]{2,1,0:T(8,128)S(1)} %forward_pair.1), channel_id=1, source_target_pairs={{0,2},{2,0},{4,6},{6,4},{1,3},{3,1},{5,7},{7,5},{8,10},{10,8},{12,... | collective-permute-start | bytes 1228808 | tf_op jit(solution)/shard_map/ppermute | solution.py:812
  91.1 6.7 %collective-permute-start.18 = (f32[288,128]{1,0:T(8,128)S(1)}, f32[288,128]{1,0:T(8,128)S(1)}, u32[]{:S(2)}, u32[]{:S(2)}) collective-permute-start(f32[288,128]{1,0:T(8,128)S(1)} %get-tuple-element.142), channel_id=1, source_target_pairs={{0,8},{8,0},{16,24},{24,16},{1,9},{9,1},{17,25},{25,17},{2,10},{10... | collective-permute-start | bytes 442376 | tf_op jit(solution)/shard_map/ppermute | solution.py:553
  92.7 8.8 %collective-permute-start.19 = (f32[288,128]{1,0:T(8,128)S(1)}, f32[288,128]{1,0:T(8,128)S(1)}, u32[]{:S(2)}, u32[]{:S(2)}) collective-permute-start(f32[288,128]{1,0:T(8,128)S(1)} %get-tuple-element.143), channel_id=1, source_target_pairs={{0,16},{8,24},{16,0},{24,8},{1,17},{9,25},{17,1},{25,9},{2,18},{10... | collective-permute-start | bytes 442376 | tf_op jit(solution)/shard_map/ppermute | solution.py:553
  94.2 7.2 %collective-permute-start.20 = (f32[288,128]{1,0:T(8,128)S(1)}, f32[288,128]{1,0:T(8,128)S(1)}, u32[]{:S(2)}, u32[]{:S(2)}) collective-permute-start(f32[288,128]{1,0:T(8,128)S(1)} %get-tuple-element.144), channel_id=1, source_target_pairs={{0,24},{8,16},{16,8},{24,0},{1,25},{9,17},{17,9},{25,1},{2,26},{10... | collective-permute-start | bytes 442376 | tf_op jit(solution)/shard_map/ppermute | solution.py:553
  102.1 6.7 %collective-permute-start.21 = (f32[216,128]{1,0:T(8,128)S(1)}, f32[216,128]{1,0:T(8,128)S(1)}, u32[]{:S(2)}, u32[]{:S(2)}) collective-permute-start(f32[216,128]{1,0:T(8,128)S(1)} %get-tuple-element.147), channel_id=1, source_target_pairs={{0,2},{2,0},{4,6},{6,4},{1,3},{3,1},{5,7},{7,5},{8,10},{10,8},{12,... | collective-permute-start | bytes 331784 | tf_op jit(solution)/shard_map/ppermute | solution.py:553
  104.0 11.4 %collective-permute-start.22 = (f32[216,128]{1,0:T(8,128)S(1)}, f32[216,128]{1,0:T(8,128)S(1)}, u32[]{:S(2)}, u32[]{:S(2)}) collective-permute-start(f32[216,128]{1,0:T(8,128)S(1)} %get-tuple-element.148), channel_id=1, source_target_pairs={{0,4},{2,6},{4,0},{6,2},{1,5},{3,7},{5,1},{7,3},{8,12},{10,14},{12... | collective-permute-start | bytes 331784 | tf_op jit(solution)/shard_map/ppermute | solution.py:553
  106.1 9.3 %collective-permute-start.23 = (f32[216,128]{1,0:T(8,128)S(1)}, f32[216,128]{1,0:T(8,128)S(1)}, u32[]{:S(2)}, u32[]{:S(2)}) collective-permute-start(f32[216,128]{1,0:T(8,128)S(1)} %get-tuple-element.149), channel_id=1, source_target_pairs={{0,6},{2,4},{4,2},{6,0},{1,7},{3,5},{5,3},{7,1},{8,14},{10,12},{12... | collective-permute-start | bytes 331784 | tf_op jit(solution)/shard_map/ppermute | solution.py:553
  116.0 7.8 %collective-permute-start.26 = (f32[216,128]{1,0:T(8,128)S(1)}, f32[216,128]{1,0:T(8,128)S(1)}, u32[]{:S(2)}, u32[]{:S(2)}) collective-permute-start(f32[216,128]{1,0:T(8,128)S(1)} %add_split.5.refs_0_), channel_id=1, source_target_pairs={{0,6},{2,4},{4,2},{6,0},{1,7},{3,5},{5,3},{7,1},{8,14},{10,12},{12... | collective-permute-start | bytes 331784 | tf_op jit(solution)/shard_map/ppermute | solution.py:553
  118.4 8.7 %collective-permute-start.25 = (f32[216,128]{1,0:T(8,128)S(1)}, f32[216,128]{1,0:T(8,128)S(1)}, u32[]{:S(2)}, u32[]{:S(2)}) collective-permute-start(f32[216,128]{1,0:T(8,128)S(1)} %add_split.5.refs_0_), channel_id=1, source_target_pairs={{0,4},{2,6},{4,0},{6,2},{1,5},{3,7},{5,1},{7,3},{8,12},{10,14},{12... | collective-permute-start | bytes 331784 | tf_op jit(solution)/shard_map/ppermute | solution.py:553
  119.3 7.9 %collective-permute-start.24 = (f32[216,128]{1,0:T(8,128)S(1)}, f32[216,128]{1,0:T(8,128)S(1)}, u32[]{:S(2)}, u32[]{:S(2)}) collective-permute-start(f32[216,128]{1,0:T(8,128)S(1)} %add_split.5.refs_0_), channel_id=1, source_target_pairs={{0,2},{2,0},{4,6},{6,4},{1,3},{3,1},{5,7},{7,5},{8,10},{10,8},{12,... | collective-permute-start | bytes 331784 | tf_op jit(solution)/shard_map/ppermute | solution.py:553
  127.2 16.1 %collective-permute-start.29 = (f32[864,128]{1,0:T(8,128)S(1)}, f32[864,128]{1,0:T(8,128)S(1)}, u32[]{:S(2)}, u32[]{:S(2)}) collective-permute-start(f32[864,128]{1,0:T(8,128)S(1)} %stack.36.refs_0_), channel_id=1, source_target_pairs={{0,24},{8,16},{16,8},{24,0},{1,25},{9,17},{17,9},{25,1},{2,26},{10... | collective-permute-start | bytes 1327112 | tf_op jit(solution)/shard_map/ppermute | solution.py:553
  128.4 18.1 %collective-permute-start.28 = (f32[864,128]{1,0:T(8,128)S(1)}, f32[864,128]{1,0:T(8,128)S(1)}, u32[]{:S(2)}, u32[]{:S(2)}) collective-permute-start(f32[864,128]{1,0:T(8,128)S(1)} %stack.36.refs_0_), channel_id=1, source_target_pairs={{0,16},{8,24},{16,0},{24,8},{1,17},{9,25},{17,1},{25,9},{2,18},{10... | collective-permute-start | bytes 1327112 | tf_op jit(solution)/shard_map/ppermute | solution.py:553
  130.2 16.4 %collective-permute-start.27 = (f32[864,128]{1,0:T(8,128)S(1)}, f32[864,128]{1,0:T(8,128)S(1)}, u32[]{:S(2)}, u32[]{:S(2)}) collective-permute-start(f32[864,128]{1,0:T(8,128)S(1)} %stack.36.refs_0_), channel_id=1, source_target_pairs={{0,8},{8,0},{16,24},{24,16},{1,9},{9,1},{17,25},{25,17},{2,10},{10... | collective-permute-start | bytes 1327112 | tf_op jit(solution)/shard_map/ppermute | solution.py:553
  130.8 9.6 %collective-permute-start.11 = (f32[200,256]{1,0:T(8,128)S(1)}, f32[200,256]{1,0:T(8,128)S(1)}, u32[]{:S(2)}, u32[]{:S(2)}) collective-permute-start(f32[200,256]{1,0:T(8,128)S(1)} %get-tuple-element.131), channel_id=1, source_target_pairs={{0,4},{2,6},{4,0},{6,2},{1,5},{3,7},{5,1},{7,3},{8,12},{10,14},{12... | collective-permute-start | bytes 614408 | tf_op jit(solution)/shard_map/ppermute | solution.py:553
  131.4 15.3 %collective-permute-start.10 = (f32[200,256]{1,0:T(8,128)S(1)}, f32[200,256]{1,0:T(8,128)S(1)}, u32[]{:S(2)}, u32[]{:S(2)}) collective-permute-start(f32[200,256]{1,0:T(8,128)S(1)} %get-tuple-element.130), channel_id=1, source_target_pairs={{0,2},{2,0},{4,6},{6,4},{1,3},{3,1},{5,7},{7,5},{8,10},{10,8},{12,... | collective-permute-start | bytes 614408 | tf_op jit(solution)/shard_map/ppermute | solution.py:553
  140.4 7.7 %collective-permute-start.12 = (f32[200,256]{1,0:T(8,128)S(1)}, f32[200,256]{1,0:T(8,128)S(1)}, u32[]{:S(2)}, u32[]{:S(2)}) collective-permute-start(f32[200,256]{1,0:T(8,128)S(1)} %get-tuple-element.132), channel_id=1, source_target_pairs={{0,6},{2,4},{4,2},{6,0},{1,7},{3,5},{5,3},{7,1},{8,14},{10,12},{12... | collective-permute-start | bytes 614408 | tf_op jit(solution)/shard_map/ppermute | solution.py:553
  148.0 3.7 %collective-permute-start.30 = (f32[3456,128]{1,0:T(8,128)S(1)}, f32[3456,128]{1,0:T(8,128)S(1)}, u32[]{:S(2)}, u32[]{:S(2)}) collective-permute-start(f32[3456,128]{1,0:T(8,128)S(1)} %stack.37.own), channel_id=1, source_target_pairs={{0,1},{1,0},{2,3},{3,2},{4,5},{5,4},{6,7},{7,6},{8,9},{9,8},{10,11... | collective-permute-start | bytes 5308424 | tf_op jit(solution)/shard_map/ppermute | solution.py:770
  (15 other events, 98.6 us)

commit v2 on v1

--- a/solution.py
+++ b/solution.py
@@ -325,8 +325,7 @@
             high, low = split_low(jnp.concatenate([numer, tail], 0))
             value = feats[h]
             gap = jnp.zeros((LANES - ext, s.genes), bf16)
-            sums = dot_lanes(value.astype(bf16), jnp.concatenate([high, gap, low, gap], 0))
-            values_grad[h] += sums[:, :LANES] + sums[:, LANES:]
+            values_grad[h] += dot_lanes(value.astype(bf16), jnp.concatenate([high, gap], 0))
             back_feats = dot(kv3[h], jnp.concatenate([high, high, low], 0)) * value
             query = qkv[base + j, rows, :].astype(f32)
             total = jnp.sum(back_feats, 0, keepdims=True)
@@ -542,7 +541,7 @@
         pltpu.VMEM((3, s.width, LANES), f32),
     ]
     args = [place, vg_own, vg_other, kv_own, kv_other, shifted, qkv, *middle_grad, *query_part, *weights]
-    return call("last", functools.partial(last_body, s, groups), args, out, scratch, LAST_MB, 1, flops=15e9)
+    return call("last", functools.partial(last_body, s, groups), args, out, scratch, LAST_MB, 1, flops=1e9)
 
 
 def partners(size, step):
@@ -666,7 +665,7 @@
     for ref in (ob, sg, sb, rb):
         ref[...] = columns[at : at + 1, :]
         at += 1
-    hb[...] = columns[at : at + s.hidden // w, :]
+    hb[...] = jnp.concatenate([columns[at + n, :] for n in range(s.hidden // w)], 0)
     columns = tile(late, 2 * ni).T
     fg[...] = columns[0:1, :]
     fb[...] = columns[1:2, :]
@@ -677,7 +676,7 @@
     w = s.width
     row = array(1, w)
     out = [array(w, 3 * s.inner), array(w, s.inner), array(w, s.hidden), array(w, s.hidden)]
-    out += [row, row, row, row, array(s.hidden // w, w), array(tissues, w), row, row]
+    out += [row, row, row, row, array(s.hidden), array(tissues, w), row, row]
     scratch = [pltpu.VMEM((32 * n if split else ref.shape[0], LANES), f32) for n, ref in zip(rows, (own, other))]
     body = functools.partial(finish_body, s, split, tissues, rows)
     return call("finish", body, [place, own, other], out, scratch, 8, 1, flops=1e9)
@@ -858,7 +857,7 @@
         sg[0],
         sb[0],
         hid,
-        hb.reshape(-1),
+        hb,
         ret_t.T,
         rb[0],
     )

time: 155 us -> 151 us (0.974)
  starting transfers between devices: 49 us -> 46.4 us
  Pallas kernels: 60.5 us -> 58.1 us
    pallas_call x16, Pallas kernels: 60.5 us -> 58.1 us  [call(): pl.pallas_call(body, out_shape=out, in_specs=[SMEM] * smem + [VMEM] * (le...]
    ppermute x1, starting transfers between devices: 1.86 us -> 0.07 us  [finish_outputs(): lax.ppermute(forward_pair(out_blocks[0], far), 'home', partners(homes, 1))]
    ppermute x5, waiting for transfers between devices: 2.3 us -> 4.08 us  [other(): return lax.ppermute(value, 'rest', partners(2, 1))]
  transfers between devices with their start and end apart: 31 -> 31, of which waited for: 12 -> 13; matrix products, arithmetic and copies ran while one was open for 2% -> 2% of each run, Pallas kernels for 28% -> 28%
where the time goes in v2:
time: 151 us
  Pallas kernels  58.1 us (38%)
  starting transfers between devices  46.4 us (31%)
  waiting for transfers between devices  36.7 us (24%)
  local copies, waits for them, and re-layouts  8.45 us (6%)
    pallas_call x16, Pallas kernels, call(): pl.pallas_call(body, out_shape=out, in_specs=[SMEM] * smem + [VMEM] * (le...  58.1 us
    ppermute x24, starting transfers between devices, send(): lax.ppermute(values[k], axis, partners(size, k))  39.2 us
    ppermute x24, waiting for transfers between devices, send(): lax.ppermute(values[k], axis, partners(size, k))  31.9 us
    ppermute x1, starting transfers between devices, local(): out_far = lax.ppermute(out_blocks[1], 'home', partners(homes, 2))  6.41 us
    unnamed x32, local copies, waits for them, and re-layouts  4.5 us
    ppermute x5, waiting for transfers between devices, other(): return lax.ppermute(value, 'rest', partners(2, 1))  4.08 us
  transfers between devices with their start and end apart: 31, of which 13 were waited for; matrix products, arithmetic and copies ran while one was open for 2% of the time, Pallas kernels for 28%

profile of v2, /device:TPU:0, one launch (start us, length us, event | category | flops | bytes accessed | tf_op | source)
XLA Modules:
  0.0 150.8 jit_solution(9717910285968643419)
XLA Ops:
  2.2 4.1 %collective-permute-start.1 = (f32[200,256]{1,0:T(8,128)S(1)}, f32[200,256]{1,0:T(8,128)S(1)}, u32[]{:S(2)}, u32[]{:S(2)}) collective-permute-start(f32[200,256]{1,0:T(8,128)S(1)} %get-tuple-element.165), channel_id=1, source_target_pairs={{0,4},{2,6},{4,0},{6,2},{1,5},{3,7},{5,1},{7,3},{8,12},{10,14},{12... | collective-permute-start | bytes 614408 | tf_op jit(solution)/shard_map/ppermute | solution.py:552
  6.3 1.6 %collective-permute-start = (f32[200,256]{1,0:T(8,128)S(1)}, f32[200,256]{1,0:T(8,128)S(1)}, u32[]{:S(2)}, u32[]{:S(2)}) collective-permute-start(f32[200,256]{1,0:T(8,128)S(1)} %get-tuple-element.166), channel_id=1, source_target_pairs={{0,2},{2,0},{4,6},{6,4},{1,3},{3,1},{5,7},{7,5},{8,10},{10,8},{12,... | collective-permute-start | bytes 614408 | tf_op jit(solution)/shard_map/ppermute | solution.py:552
  15.0 1.7 %prepare.1 = (bf16[1920,200]{1,0:T(8,128)(2,1)S(1)}, bf16[10,272,64]{2,1,0:T(8,128)(2,1)S(1)}, bf16[10,64,272]{2,1,0:T(8,128)(2,1)S(1)}, bf16[200,640]{1,0:T(8,1...) custom-call(s32[9]{0:T(128)S(1)} %stack.35.place.refs_0_.numbers, ...), custom_call_target="tpu_custom_call" | custom-call | flops 4000000000 | bytes 1024 | tf_op jit(solution)/shard_map/prepare/pallas_call | solution.py:79
  16.7 2.6 %keys.2 = (f32[10,272,128]{2,1,0:T(8,128)S(1)}, f32[4,200,256]{2,1,0:T(8,128)S(1)}, bf16[4,1920,256]{2,1,0:T(8,128)(2,1)S(1)}) custom-call(s32[9]{0:T(128)S(1)} %stack.35.place.refs_0_.numbers, f32[200,256]{1,0:T(8,128)S(1)} %get-tuple-element.164.refs_1_, f32[200,8]{1,0:T(8,128)S(1)} %get-tuple-element.89.refs_2_.refs_4_.refs_7_.refs_14_.refs_11_, ...), custom_call_target="tpu_custom_call" | custom-call | flops 3000000000 | bytes 1024 | tf_op jit(solution)/shard_map/keys/pallas_call | solution.py:79
  19.4 2.0 %collective-permute-done.2.refs_3_ = f32[200,256]{1,0:T(8,128)S(1)} collective-permute-done((f32[200,256]{1,0:T(8,128)S(1)}, f32[200,256]{1,0:T(8,128)S(1)}, u32[]{:S(2)}, u32[]{:S(2)}) %collective-permute-start.2) | collective-permute-done | bytes 204832 | tf_op jit(solution)/shard_map/ppermute | solution.py:552
  21.4 3.9 %collective-permute-start.3 = (f32[200,256]{1,0:T(8,128)S(1)}, f32[200,256]{1,0:T(8,128)S(1)}, u32[]{:S(2)}, u32[]{:S(2)}) collective-permute-start(f32[200,256]{1,0:T(8,128)S(1)} %get-tuple-element.96), channel_id=1, source_target_pairs={{0,2},{2,0},{4,6},{6,4},{1,3},{3,1},{5,7},{7,5},{8,10},{10,8},{12,... | collective-permute-start | bytes 614408 | tf_op jit(solution)/shard_map/ppermute | solution.py:552
  25.3 6.3 %keys.3 = (f32[10,272,128]{2,1,0:T(8,128)S(1)}, f32[4,200,256]{2,1,0:T(8,128)S(1)}, bf16[4,1920,256]{2,1,0:T(8,128)(2,1)S(1)}) custom-call(s32[9]{0:T(128)S(1)} %stack.35.place.refs_0_.numbers, f32[200,256]{1,0:T(8,128)S(1)} %collective-permute-done.refs_1_, ...), custom_call_target="tpu_custom_call", output_to_operand_aliasing={{1}: (8, {}), {2}: (9, {})} | custom-call | flops 8999999488 | bytes 1024 | tf_op jit(solution)/shard_map/keys/pallas_call | solution.py:79
  31.7 2.5 %collective-permute-start.5 = (f32[200,256]{1,0:T(8,128)S(1)}, f32[200,256]{1,0:T(8,128)S(1)}, u32[]{:S(2)}, u32[]{:S(2)}) collective-permute-start(f32[200,256]{1,0:T(8,128)S(1)} %get-tuple-element.119), channel_id=1, source_target_pairs={{0,4},{2,6},{4,0},{6,2},{1,5},{3,7},{5,1},{7,3},{8,12},{10,14},{12... | collective-permute-start | bytes 614408 | tf_op jit(solution)/shard_map/ppermute | solution.py:552
  35.2 13.1 %middle.2 = (f32[2,200,256]{2,1,0:T(8,128)S(1)}, f32[2,200,256]{2,1,0:T(8,128)S(1)}, f32[2,200,256]{2,1,0:T(8,128)S(1)}, bf16[10,272,240]{2,1,0:T(8,128)(2,1)S(1...) custom-call(s32[9]{0:T(128)S(1)} %stack.35.place.refs_0_.numbers, ...), custom_call_target="tpu_custom_call" | custom-call | flops 14000000000 | bytes 1024 | tf_op jit(solution)/shard_map/middle/pallas_call | solution.py:79
  49.3 12.5 %middle.3 = (f32[2,200,256]{2,1,0:T(8,128)S(1)}, f32[2,200,256]{2,1,0:T(8,128)S(1)}, f32[2,200,256]{2,1,0:T(8,128)S(1)}, f32[10,272,128]{2,1,0:T(8,128)S(1)}, f3...) custom-call(s32[9]{0:T(128)S(1)} %stack.35.place.refs_0_.numbers, bf16[10,272,240]{2,1,0:T(8,128)(2,1)S(1)} %get-tuple-element.110.refs_1_, ...), custom_call_target="tpu_custom_call" | custom-call | flops 14000000000 | bytes 1024 | tf_op jit(solution)/shard_map/middle/pallas_call | solution.py:79
  62.3 6.4 %collective-permute-start.7 = (f32[2,200,256]{2,1,0:T(8,128)S(1)}, f32[2,200,256]{2,1,0:T(8,128)S(1)}, u32[]{:S(2)}, u32[]{:S(2)}) collective-permute-start(f32[2,200,256]{2,1,0:T(8,128)S(1)} %get-tuple-element.121), channel_id=1, source_target_pairs={{0,4},{2,6},{4,0},{6,2},{1,5},{3,7},{5,1},{7,3},{8,12},{10,14},{12... | collective-permute-start | bytes 1228808 | tf_op jit(solution)/shard_map/ppermute | solution.py:807
  69.4 1.6 %collective-permute-start.14 = (f32[576,128]{1,0:T(8,128)S(1)}, f32[576,128]{1,0:T(8,128)S(1)}, u32[]{:S(2)}, u32[]{:S(2)}) collective-permute-start(f32[576,128]{1,0:T(8,128)S(1)} %get-tuple-element.136), channel_id=1, source_target_pairs={{0,8},{8,0},{16,24},{24,16},{1,9},{9,1},{17,25},{25,17},{2,10},{10... | collective-permute-start | bytes 884744 | tf_op jit(solution)/shard_map/ppermute | solution.py:552
  71.0 1.5 %collective-permute-start.15 = (f32[576,128]{1,0:T(8,128)S(1)}, f32[576,128]{1,0:T(8,128)S(1)}, u32[]{:S(2)}, u32[]{:S(2)}) collective-permute-start(f32[576,128]{1,0:T(8,128)S(1)} %get-tuple-element.137), channel_id=1, source_target_pairs={{0,16},{8,24},{16,0},{24,8},{1,17},{9,25},{17,1},{25,9},{2,18},{10... | collective-permute-start | bytes 884744 | tf_op jit(solution)/shard_map/ppermute | solution.py:552
  73.0 13.6 %last.1 = (f32[200,256]{1,0:T(8,128)S(1)}, f32[200,256]{1,0:T(8,128)S(1)}, f32[200,256]{1,0:T(8,128)S(1)}, f32[200,256]{1,0:T(8,128)S(1)}, f32[1152,128]{1,0:T(8,128)S(1)}, /*index=5*/f32[1152,128]{1,0:T(8,128)S(1)}) custom-call(s32[9]{0:T(128)S(1)} %stack.35.place.refs_0_.numbers, f32[10,272,128]{2,1,0:T(8,128)S(1)} %get-tuple-element.122.refs_1_, ...), custom_call_target="tpu_custom_call" | custom-call | flops 1000000000 | bytes 1024 | tf_op jit(solution)/shard_map/last/pallas_call | solution.py:79
  87.4 1.9 %collective-permute-done.17.refs_1_ = f32[1152,128]{1,0:T(8,128)S(1)} collective-permute-done((f32[1152,128]{1,0:T(8,128)S(1)}, f32[1152,128]{1,0:T(8,128)S(1)}, u32[]{:S(2)}, u32[]{:S(2)}) %collective-permute-start.17) | collective-permute-done | bytes 589856 | tf_op jit(solution)/shard_map/ppermute | solution.py:769
  89.9 1.6 %collective-permute-start.18 = (f32[288,128]{1,0:T(8,128)S(1)}, f32[288,128]{1,0:T(8,128)S(1)}, u32[]{:S(2)}, u32[]{:S(2)}) collective-permute-start(f32[288,128]{1,0:T(8,128)S(1)} %get-tuple-element.142), channel_id=1, source_target_pairs={{0,8},{8,0},{16,24},{24,16},{1,9},{9,1},{17,25},{25,17},{2,10},{10... | collective-permute-start | bytes 442376 | tf_op jit(solution)/shard_map/ppermute | solution.py:552
  91.5 1.5 %collective-permute-start.19 = (f32[288,128]{1,0:T(8,128)S(1)}, f32[288,128]{1,0:T(8,128)S(1)}, u32[]{:S(2)}, u32[]{:S(2)}) collective-permute-start(f32[288,128]{1,0:T(8,128)S(1)} %get-tuple-element.143), channel_id=1, source_target_pairs={{0,16},{8,24},{16,0},{24,8},{1,17},{9,25},{17,1},{25,9},{2,18},{10... | collective-permute-start | bytes 442376 | tf_op jit(solution)/shard_map/ppermute | solution.py:552
  93.5 3.1 %collective-permute-done.18.refs_5_ = f32[288,128]{1,0:T(8,128)S(1)} collective-permute-done((f32[288,128]{1,0:T(8,128)S(1)}, f32[288,128]{1,0:T(8,128)S(1)}, u32[]{:S(2)}, u32[]{:S(2)}) %collective-permute-start.18) | collective-permute-done | bytes 147488 | tf_op jit(solution)/shard_map/ppermute | solution.py:552
  96.6 3.7 %collective-permute-done.19.refs_6_ = f32[288,128]{1,0:T(8,128)S(1)} collective-permute-done((f32[288,128]{1,0:T(8,128)S(1)}, f32[288,128]{1,0:T(8,128)S(1)}, u32[]{:S(2)}, u32[]{:S(2)}) %collective-permute-start.19) | collective-permute-done | bytes 147488 | tf_op jit(solution)/shard_map/ppermute | solution.py:552
  101.2 1.7 %collective-permute-start.22 = (f32[216,128]{1,0:T(8,128)S(1)}, f32[216,128]{1,0:T(8,128)S(1)}, u32[]{:S(2)}, u32[]{:S(2)}) collective-permute-start(f32[216,128]{1,0:T(8,128)S(1)} %get-tuple-element.148), channel_id=1, source_target_pairs={{0,4},{2,6},{4,0},{6,2},{1,5},{3,7},{5,1},{7,3},{8,12},{10,14},{12... | collective-permute-start | bytes 331784 | tf_op jit(solution)/shard_map/ppermute | solution.py:552
  102.9 2.5 %collective-permute-start.23 = (f32[216,128]{1,0:T(8,128)S(1)}, f32[216,128]{1,0:T(8,128)S(1)}, u32[]{:S(2)}, u32[]{:S(2)}) collective-permute-start(f32[216,128]{1,0:T(8,128)S(1)} %get-tuple-element.149), channel_id=1, source_target_pairs={{0,6},{2,4},{4,2},{6,0},{1,7},{3,5},{5,3},{7,1},{8,14},{10,12},{12... | collective-permute-start | bytes 331784 | tf_op jit(solution)/shard_map/ppermute | solution.py:552
  106.9 5.3 %collective-permute-done.22.refs_2_ = f32[216,128]{1,0:T(8,128)S(1)} collective-permute-done((f32[216,128]{1,0:T(8,128)S(1)}, f32[216,128]{1,0:T(8,128)S(1)}, u32[]{:S(2)}, u32[]{:S(2)}) %collective-permute-start.22) | collective-permute-done | bytes 110624 | tf_op jit(solution)/shard_map/ppermute | solution.py:552
  112.8 2.4 %collective-permute-start.26 = (f32[216,128]{1,0:T(8,128)S(1)}, f32[216,128]{1,0:T(8,128)S(1)}, u32[]{:S(2)}, u32[]{:S(2)}) collective-permute-start(f32[216,128]{1,0:T(8,128)S(1)} %add_split.5.refs_0_), channel_id=1, source_target_pairs={{0,6},{2,4},{4,2},{6,0},{1,7},{3,5},{5,3},{7,1},{8,14},{10,12},{12... | collective-permute-start | bytes 331784 | tf_op jit(solution)/shard_map/ppermute | solution.py:552
  117.2 3.3 %collective-permute-done.26.refs_3_ = f32[216,128]{1,0:T(8,128)S(1)} collective-permute-done((f32[216,128]{1,0:T(8,128)S(1)}, f32[216,128]{1,0:T(8,128)S(1)}, u32[]{:S(2)}, u32[]{:S(2)}) %collective-permute-start.26) | collective-permute-done | bytes 110624 | tf_op jit(solution)/shard_map/ppermute | solution.py:552
  120.5 3.2 %collective-permute-done.25.refs_2_ = f32[216,128]{1,0:T(8,128)S(1)} collective-permute-done((f32[216,128]{1,0:T(8,128)S(1)}, f32[216,128]{1,0:T(8,128)S(1)}, u32[]{:S(2)}, u32[]{:S(2)}) %collective-permute-start.25) | collective-permute-done | bytes 110624 | tf_op jit(solution)/shard_map/ppermute | solution.py:552
  125.1 1.6 %collective-permute-start.28 = (f32[864,128]{1,0:T(8,128)S(1)}, f32[864,128]{1,0:T(8,128)S(1)}, u32[]{:S(2)}, u32[]{:S(2)}) collective-permute-start(f32[864,128]{1,0:T(8,128)S(1)} %stack.36.refs_0_), channel_id=1, source_target_pairs={{0,16},{8,24},{16,0},{24,8},{1,17},{9,25},{17,1},{25,9},{2,18},{10... | collective-permute-start | bytes 1327112 | tf_op jit(solution)/shard_map/ppermute | solution.py:552
  127.9 2.6 %collective-permute-start.10 = (f32[200,256]{1,0:T(8,128)S(1)}, f32[200,256]{1,0:T(8,128)S(1)}, u32[]{:S(2)}, u32[]{:S(2)}) collective-permute-start(f32[200,256]{1,0:T(8,128)S(1)} %get-tuple-element.130), channel_id=1, source_target_pairs={{0,2},{2,0},{4,6},{6,4},{1,3},{3,1},{5,7},{7,5},{8,10},{10,8},{12,... | collective-permute-start | bytes 614408 | tf_op jit(solution)/shard_map/ppermute | solution.py:552
  130.6 6.1 %collective-permute-done.11.refs_2_ = f32[200,256]{1,0:T(8,128)S(1)} collective-permute-done((f32[200,256]{1,0:T(8,128)S(1)}, f32[200,256]{1,0:T(8,128)S(1)}, u32[]{:S(2)}, u32[]{:S(2)}) %collective-permute-start.11) | collective-permute-done | bytes 204832 | tf_op jit(solution)/shard_map/ppermute | solution.py:552
  136.6 3.3 %collective-permute-start.12 = (f32[200,256]{1,0:T(8,128)S(1)}, f32[200,256]{1,0:T(8,128)S(1)}, u32[]{:S(2)}, u32[]{:S(2)}) collective-permute-start(f32[200,256]{1,0:T(8,128)S(1)} %get-tuple-element.132), channel_id=1, source_target_pairs={{0,6},{2,4},{4,2},{6,0},{1,7},{3,5},{5,3},{7,1},{8,14},{10,12},{12... | collective-permute-start | bytes 614408 | tf_op jit(solution)/shard_map/ppermute | solution.py:552
  139.9 2.9 %collective-permute-done.28.refs_2_ = f32[864,128]{1,0:T(8,128)S(1)} collective-permute-done((f32[864,128]{1,0:T(8,128)S(1)}, f32[864,128]{1,0:T(8,128)S(1)}, u32[]{:S(2)}, u32[]{:S(2)}) %collective-permute-start.28) | collective-permute-done | bytes 442400 | tf_op jit(solution)/shard_map/ppermute | solution.py:552
  145.8 2.2 %collective-permute-done.30.other = f32[3456,128]{1,0:T(8,128)S(1)} collective-permute-done((f32[3456,128]{1,0:T(8,128)S(1)}, f32[3456,128]{1,0:T(8,128)S(1)}, u32[]{:S(2)}, u32[]{:S(2)}) %collective-permute-start.30) | collective-permute-done | bytes 1769504 | tf_op jit(solution)/shard_map/ppermute | solution.py:769
  148.0 2.7 %finish.1 = (f32[200,1920]{1,0:T(8,128)}, f32[200,640]{1,0:T(8,128)}, f32[200,800]{1,0:T(8,128)}, f32[200,800]{1,0:T(8,128)}, f32[1,200]{1,0:T(1,128)}, /*index=...) custom-call(s32[9]{0:T(128)S(1)} %stack.35.place.refs_0_.numbers, ...), custom_call_target="tpu_custom_call" | custom-call | flops 1000000000 | bytes 1024 | tf_op jit(solution)/shard_map/finish/pallas_call | solution.py:79
  (84 shorter events, 24.8 us)
Async XLA Ops:
  0.7 9.7 %copy-start.11 = (f32[200]{0:T(256)S(1)}, f32[200]{0:T(256)}, u32[]{:S(2)}) copy-start(f32[200]{0:T(256)} %param.32) | copy-start | bytes 2404
  2.2 17.2 %collective-permute-start.1 = (f32[200,256]{1,0:T(8,128)S(1)}, f32[200,256]{1,0:T(8,128)S(1)}, u32[]{:S(2)}, u32[]{:S(2)}) collective-permute-start(f32[200,256]{1,0:T(8,128)S(1)} %get-tuple-element.165), channel_id=1, source_target_pairs={{0,4},{2,6},{4,0},{6,2},{1,5},{3,7},{5,1},{7,3},{8,12},{10,14},{12... | collective-permute-start | bytes 614408 | tf_op jit(solution)/shard_map/ppermute | solution.py:552
  6.3 13.1 %collective-permute-start = (f32[200,256]{1,0:T(8,128)S(1)}, f32[200,256]{1,0:T(8,128)S(1)}, u32[]{:S(2)}, u32[]{:S(2)}) collective-permute-start(f32[200,256]{1,0:T(8,128)S(1)} %get-tuple-element.166), channel_id=1, source_target_pairs={{0,2},{2,0},{4,6},{6,4},{1,3},{3,1},{5,7},{7,5},{8,10},{10,8},{12,... | collective-permute-start | bytes 614408 | tf_op jit(solution)/shard_map/ppermute | solution.py:552
  7.9 13.5 %collective-permute-start.2 = (f32[200,256]{1,0:T(8,128)S(1)}, f32[200,256]{1,0:T(8,128)S(1)}, u32[]{:S(2)}, u32[]{:S(2)}) collective-permute-start(f32[200,256]{1,0:T(8,128)S(1)} %get-tuple-element.167), channel_id=1, source_target_pairs={{0,6},{2,4},{4,2},{6,0},{1,7},{3,5},{5,3},{7,1},{8,14},{10,12},{12... | collective-permute-start | bytes 614408 | tf_op jit(solution)/shard_map/ppermute | solution.py:552
  21.4 10.2 %collective-permute-start.3 = (f32[200,256]{1,0:T(8,128)S(1)}, f32[200,256]{1,0:T(8,128)S(1)}, u32[]{:S(2)}, u32[]{:S(2)}) collective-permute-start(f32[200,256]{1,0:T(8,128)S(1)} %get-tuple-element.96), channel_id=1, source_target_pairs={{0,2},{2,0},{4,6},{6,4},{1,3},{3,1},{5,7},{7,5},{8,10},{10,8},{12,... | collective-permute-start | bytes 614408 | tf_op jit(solution)/shard_map/ppermute | solution.py:552
  31.6 3.6 %collective-permute-start.4 = (f32[10,272,128]{2,1,0:T(8,128)S(1)}, f32[10,272,128]{2,1,0:T(8,128)S(1)}, u32[]{:S(2)}, u32[]{:S(2)}) collective-permute-start(f32[10,272,128]{2,1,0:T(8,128)S(1)} %get-tuple-element.97.refs_1_.refs_3_), channel_id=1, source_target_pairs={{0,1},{1,0},{2,3},{3,2},{4,5},{5,4},{6,7},{7,6},{8,9},{9,8},{10,11... | collective-permute-start | bytes 4177928 | tf_op jit(solution)/shard_map/ppermute | solution.py:769
  31.7 17.6 %collective-permute-start.5 = (f32[200,256]{1,0:T(8,128)S(1)}, f32[200,256]{1,0:T(8,128)S(1)}, u32[]{:S(2)}, u32[]{:S(2)}) collective-permute-start(f32[200,256]{1,0:T(8,128)S(1)} %get-tuple-element.119), channel_id=1, source_target_pairs={{0,4},{2,6},{4,0},{6,2},{1,5},{3,7},{5,1},{7,3},{8,12},{10,14},{12... | collective-permute-start | bytes 614408 | tf_op jit(solution)/shard_map/ppermute | solution.py:552
  34.2 15.1 %collective-permute-start.6 = (f32[200,256]{1,0:T(8,128)S(1)}, f32[200,256]{1,0:T(8,128)S(1)}, u32[]{:S(2)}, u32[]{:S(2)}) collective-permute-start(f32[200,256]{1,0:T(8,128)S(1)} %get-tuple-element.120), channel_id=1, source_target_pairs={{0,6},{2,4},{4,2},{6,0},{1,7},{3,5},{5,3},{7,1},{8,14},{10,12},{12... | collective-permute-start | bytes 614408 | tf_op jit(solution)/shard_map/ppermute | solution.py:552
  61.8 7.0 %collective-permute-start.13 = (f32[2304,128]{1,0:T(8,128)S(1)}, f32[2304,128]{1,0:T(8,128)S(1)}, u32[]{:S(2)}, u32[]{:S(2)}) collective-permute-start(f32[2304,128]{1,0:T(8,128)S(1)} %get-tuple-element.134), channel_id=1, source_target_pairs={{0,1},{1,0},{2,3},{3,2},{4,5},{5,4},{6,7},{7,6},{8,9},{9,8},{10,11... | collective-permute-start | bytes 3538952 | tf_op jit(solution)/shard_map/ppermute | solution.py:769
  61.8 11.1 %collective-permute-start.8 = (f32[10,272,128]{2,1,0:T(8,128)S(1)}, f32[10,272,128]{2,1,0:T(8,128)S(1)}, u32[]{:S(2)}, u32[]{:S(2)}) collective-permute-start(f32[10,272,128]{2,1,0:T(8,128)S(1)} %get-tuple-element.122.refs_1_), channel_id=1, source_target_pairs={{0,1},{1,0},{2,3},{3,2},{4,5},{5,4},{6,7},{7,6},{8,9},{9,8},{10,11... | collective-permute-start | bytes 4177928 | tf_op jit(solution)/shard_map/ppermute | solution.py:769
  62.3 24.9 %collective-permute-start.7 = (f32[2,200,256]{2,1,0:T(8,128)S(1)}, f32[2,200,256]{2,1,0:T(8,128)S(1)}, u32[]{:S(2)}, u32[]{:S(2)}) collective-permute-start(f32[2,200,256]{2,1,0:T(8,128)S(1)} %get-tuple-element.121), channel_id=1, source_target_pairs={{0,4},{2,6},{4,0},{6,2},{1,5},{3,7},{5,1},{7,3},{8,12},{10,14},{12... | collective-permute-start | bytes 1228808 | tf_op jit(solution)/shard_map/ppermute | solution.py:807
  69.4 17.8 %collective-permute-start.14 = (f32[576,128]{1,0:T(8,128)S(1)}, f32[576,128]{1,0:T(8,128)S(1)}, u32[]{:S(2)}, u32[]{:S(2)}) collective-permute-start(f32[576,128]{1,0:T(8,128)S(1)} %get-tuple-element.136), channel_id=1, source_target_pairs={{0,8},{8,0},{16,24},{24,16},{1,9},{9,1},{17,25},{25,17},{2,10},{10... | collective-permute-start | bytes 884744 | tf_op jit(solution)/shard_map/ppermute | solution.py:552
  71.0 16.3 %collective-permute-start.15 = (f32[576,128]{1,0:T(8,128)S(1)}, f32[576,128]{1,0:T(8,128)S(1)}, u32[]{:S(2)}, u32[]{:S(2)}) collective-permute-start(f32[576,128]{1,0:T(8,128)S(1)} %get-tuple-element.137), channel_id=1, source_target_pairs={{0,16},{8,24},{16,0},{24,8},{1,17},{9,25},{17,1},{25,9},{2,18},{10... | collective-permute-start | bytes 884744 | tf_op jit(solution)/shard_map/ppermute | solution.py:552
  72.5 14.7 %collective-permute-start.16 = (f32[576,128]{1,0:T(8,128)S(1)}, f32[576,128]{1,0:T(8,128)S(1)}, u32[]{:S(2)}, u32[]{:S(2)}) collective-permute-start(f32[576,128]{1,0:T(8,128)S(1)} %get-tuple-element.138), channel_id=1, source_target_pairs={{0,24},{8,16},{16,8},{24,0},{1,25},{9,17},{17,9},{25,1},{2,26},{10... | collective-permute-start | bytes 884744 | tf_op jit(solution)/shard_map/ppermute | solution.py:552
  87.2 2.1 %collective-permute-start.17 = (f32[1152,128]{1,0:T(8,128)S(1)}, f32[1152,128]{1,0:T(8,128)S(1)}, u32[]{:S(2)}, u32[]{:S(2)}) collective-permute-start(f32[1152,128]{1,0:T(8,128)S(1)} %get-tuple-element.140), channel_id=1, source_target_pairs={{0,1},{1,0},{2,3},{3,2},{4,5},{5,4},{6,7},{7,6},{8,9},{9,8},{10,11... | collective-permute-start | bytes 1769480 | tf_op jit(solution)/shard_map/ppermute | solution.py:769
  87.4 18.0 %collective-permute-start.9 = (f32[2,200,256]{2,1,0:T(8,128)S(1)}, f32[2,200,256]{2,1,0:T(8,128)S(1)}, u32[]{:S(2)}, u32[]{:S(2)}) collective-permute-start(f32[2,200,256]{2,1,0:T(8,128)S(1)} %forward_pair.1), channel_id=1, source_target_pairs={{0,2},{2,0},{4,6},{6,4},{1,3},{3,1},{5,7},{7,5},{8,10},{10,8},{12,... | collective-permute-start | bytes 1228808 | tf_op jit(solution)/shard_map/ppermute | solution.py:811
  89.9 6.6 %collective-permute-start.18 = (f32[288,128]{1,0:T(8,128)S(1)}, f32[288,128]{1,0:T(8,128)S(1)}, u32[]{:S(2)}, u32[]{:S(2)}) collective-permute-start(f32[288,128]{1,0:T(8,128)S(1)} %get-tuple-element.142), channel_id=1, source_target_pairs={{0,8},{8,0},{16,24},{24,16},{1,9},{9,1},{17,25},{25,17},{2,10},{10... | collective-permute-start | bytes 442376 | tf_op jit(solution)/shard_map/ppermute | solution.py:552
  91.5 8.8 %collective-permute-start.19 = (f32[288,128]{1,0:T(8,128)S(1)}, f32[288,128]{1,0:T(8,128)S(1)}, u32[]{:S(2)}, u32[]{:S(2)}) collective-permute-start(f32[288,128]{1,0:T(8,128)S(1)} %get-tuple-element.143), channel_id=1, source_target_pairs={{0,16},{8,24},{16,0},{24,8},{1,17},{9,25},{17,1},{25,9},{2,18},{10... | collective-permute-start | bytes 442376 | tf_op jit(solution)/shard_map/ppermute | solution.py:552
  93.0 7.3 %collective-permute-start.20 = (f32[288,128]{1,0:T(8,128)S(1)}, f32[288,128]{1,0:T(8,128)S(1)}, u32[]{:S(2)}, u32[]{:S(2)}) collective-permute-start(f32[288,128]{1,0:T(8,128)S(1)} %get-tuple-element.144), channel_id=1, source_target_pairs={{0,24},{8,16},{16,8},{24,0},{1,25},{9,17},{17,9},{25,1},{2,26},{10... | collective-permute-start | bytes 442376 | tf_op jit(solution)/shard_map/ppermute | solution.py:552
  100.9 5.9 %collective-permute-start.21 = (f32[216,128]{1,0:T(8,128)S(1)}, f32[216,128]{1,0:T(8,128)S(1)}, u32[]{:S(2)}, u32[]{:S(2)}) collective-permute-start(f32[216,128]{1,0:T(8,128)S(1)} %get-tuple-element.147), channel_id=1, source_target_pairs={{0,2},{2,0},{4,6},{6,4},{1,3},{3,1},{5,7},{7,5},{8,10},{10,8},{12,... | collective-permute-start | bytes 331784 | tf_op jit(solution)/shard_map/ppermute | solution.py:552
  101.2 11.0 %collective-permute-start.22 = (f32[216,128]{1,0:T(8,128)S(1)}, f32[216,128]{1,0:T(8,128)S(1)}, u32[]{:S(2)}, u32[]{:S(2)}) collective-permute-start(f32[216,128]{1,0:T(8,128)S(1)} %get-tuple-element.148), channel_id=1, source_target_pairs={{0,4},{2,6},{4,0},{6,2},{1,5},{3,7},{5,1},{7,3},{8,12},{10,14},{12... | collective-permute-start | bytes 331784 | tf_op jit(solution)/shard_map/ppermute | solution.py:552
  102.9 9.3 %collective-permute-start.23 = (f32[216,128]{1,0:T(8,128)S(1)}, f32[216,128]{1,0:T(8,128)S(1)}, u32[]{:S(2)}, u32[]{:S(2)}) collective-permute-start(f32[216,128]{1,0:T(8,128)S(1)} %get-tuple-element.149), channel_id=1, source_target_pairs={{0,6},{2,4},{4,2},{6,0},{1,7},{3,5},{5,3},{7,1},{8,14},{10,12},{12... | collective-permute-start | bytes 331784 | tf_op jit(solution)/shard_map/ppermute | solution.py:552
  112.8 7.8 %collective-permute-start.26 = (f32[216,128]{1,0:T(8,128)S(1)}, f32[216,128]{1,0:T(8,128)S(1)}, u32[]{:S(2)}, u32[]{:S(2)}) collective-permute-start(f32[216,128]{1,0:T(8,128)S(1)} %add_split.5.refs_0_), channel_id=1, source_target_pairs={{0,6},{2,4},{4,2},{6,0},{1,7},{3,5},{5,3},{7,1},{8,14},{10,12},{12... | collective-permute-start | bytes 331784 | tf_op jit(solution)/shard_map/ppermute | solution.py:552
  115.2 8.6 %collective-permute-start.25 = (f32[216,128]{1,0:T(8,128)S(1)}, f32[216,128]{1,0:T(8,128)S(1)}, u32[]{:S(2)}, u32[]{:S(2)}) collective-permute-start(f32[216,128]{1,0:T(8,128)S(1)} %add_split.5.refs_0_), channel_id=1, source_target_pairs={{0,4},{2,6},{4,0},{6,2},{1,5},{3,7},{5,1},{7,3},{8,12},{10,14},{12... | collective-permute-start | bytes 331784 | tf_op jit(solution)/shard_map/ppermute | solution.py:552
  116.1 7.7 %collective-permute-start.24 = (f32[216,128]{1,0:T(8,128)S(1)}, f32[216,128]{1,0:T(8,128)S(1)}, u32[]{:S(2)}, u32[]{:S(2)}) collective-permute-start(f32[216,128]{1,0:T(8,128)S(1)} %add_split.5.refs_0_), channel_id=1, source_target_pairs={{0,2},{2,0},{4,6},{6,4},{1,3},{3,1},{5,7},{7,5},{8,10},{10,8},{12,... | collective-permute-start | bytes 331784 | tf_op jit(solution)/shard_map/ppermute | solution.py:552
  123.8 16.1 %collective-permute-start.29 = (f32[864,128]{1,0:T(8,128)S(1)}, f32[864,128]{1,0:T(8,128)S(1)}, u32[]{:S(2)}, u32[]{:S(2)}) collective-permute-start(f32[864,128]{1,0:T(8,128)S(1)} %stack.36.refs_0_), channel_id=1, source_target_pairs={{0,24},{8,16},{16,8},{24,0},{1,25},{9,17},{17,9},{25,1},{2,26},{10... | collective-permute-start | bytes 1327112 | tf_op jit(solution)/shard_map/ppermute | solution.py:552
  125.1 17.7 %collective-permute-start.28 = (f32[864,128]{1,0:T(8,128)S(1)}, f32[864,128]{1,0:T(8,128)S(1)}, u32[]{:S(2)}, u32[]{:S(2)}) collective-permute-start(f32[864,128]{1,0:T(8,128)S(1)} %stack.36.refs_0_), channel_id=1, source_target_pairs={{0,16},{8,24},{16,0},{24,8},{1,17},{9,25},{17,1},{25,9},{2,18},{10... | collective-permute-start | bytes 1327112 | tf_op jit(solution)/shard_map/ppermute | solution.py:552
  126.8 16.1 %collective-permute-start.27 = (f32[864,128]{1,0:T(8,128)S(1)}, f32[864,128]{1,0:T(8,128)S(1)}, u32[]{:S(2)}, u32[]{:S(2)}) collective-permute-start(f32[864,128]{1,0:T(8,128)S(1)} %stack.36.refs_0_), channel_id=1, source_target_pairs={{0,8},{8,0},{16,24},{24,16},{1,9},{9,1},{17,25},{25,17},{2,10},{10... | collective-permute-start | bytes 1327112 | tf_op jit(solution)/shard_map/ppermute | solution.py:552
  127.3 9.3 %collective-permute-start.11 = (f32[200,256]{1,0:T(8,128)S(1)}, f32[200,256]{1,0:T(8,128)S(1)}, u32[]{:S(2)}, u32[]{:S(2)}) collective-permute-start(f32[200,256]{1,0:T(8,128)S(1)} %get-tuple-element.131), channel_id=1, source_target_pairs={{0,4},{2,6},{4,0},{6,2},{1,5},{3,7},{5,1},{7,3},{8,12},{10,14},{12... | collective-permute-start | bytes 614408 | tf_op jit(solution)/shard_map/ppermute | solution.py:552
  127.9 15.0 %collective-permute-start.10 = (f32[200,256]{1,0:T(8,128)S(1)}, f32[200,256]{1,0:T(8,128)S(1)}, u32[]{:S(2)}, u32[]{:S(2)}) collective-permute-start(f32[200,256]{1,0:T(8,128)S(1)} %get-tuple-element.130), channel_id=1, source_target_pairs={{0,2},{2,0},{4,6},{6,4},{1,3},{3,1},{5,7},{7,5},{8,10},{10,8},{12,... | collective-permute-start | bytes 614408 | tf_op jit(solution)/shard_map/ppermute | solution.py:552
  136.6 7.7 %collective-permute-start.12 = (f32[200,256]{1,0:T(8,128)S(1)}, f32[200,256]{1,0:T(8,128)S(1)}, u32[]{:S(2)}, u32[]{:S(2)}) collective-permute-start(f32[200,256]{1,0:T(8,128)S(1)} %get-tuple-element.132), channel_id=1, source_target_pairs={{0,6},{2,4},{4,2},{6,0},{1,7},{3,5},{5,3},{7,1},{8,14},{10,12},{12... | collective-permute-start | bytes 614408 | tf_op jit(solution)/shard_map/ppermute | solution.py:552
  144.3 3.7 %collective-permute-start.30 = (f32[3456,128]{1,0:T(8,128)S(1)}, f32[3456,128]{1,0:T(8,128)S(1)}, u32[]{:S(2)}, u32[]{:S(2)}) collective-permute-start(f32[3456,128]{1,0:T(8,128)S(1)} %stack.37.own), channel_id=1, source_target_pairs={{0,1},{1,0},{2,3},{3,2},{4,5},{5,4},{6,7},{7,6},{8,9},{9,8},{10,11... | collective-permute-start | bytes 5308424 | tf_op jit(solution)/shard_map/ppermute | solution.py:769
  (15 other events, 98.6 us)

commit v3 on v2

--- a/solution.py
+++ b/solution.py
@@ -221,7 +221,7 @@
     return (row_index((size, size)) == lane_index((size, size))).astype(f32).astype(bf16)
 
 
-def middle_body(s, base, count, first, final, *refs):
+def middle_body(s, base, count, later, first, final, *refs):
     refs = list(refs)
 
     def take(n):
@@ -230,20 +230,22 @@
         return taken
 
     (place,) = take(1)
-    before = take(2) if first else take(9)
+    before = take(2) if first else take(13)
     shifted, qkv = take(2)
     cots = take(count)
     cols, hidden_bias, draws, draws_t, out_w, out_wt = take(6)
     hid_w, hid_wt, ret_w, ret_wt, joint = take(5)
     outputs, middle_grad, query_part = take(3)
-    results = take(3) if final else take(9)
+    results = take(3) if final else take(13)
     if first:
         kv3, kv_t = take(2) if final else results[:2]
     else:
         kv3, kv_t = before[:2]
-    feats, att, att_low, over, att_grad, query_grad = take(6)
+    mine = take(4) if first else None
+    ahead = before[9:] if not first else results[9:]
+    att_grad, query_grad = take(2)
     cot_all, acts, pre_grads = take(3)
-    sums = refs if final else results[2:]
+    sums = refs if final else results[2:9]
     acc_q, acc_o, acc_r, acc_h, acc_cols, acc_hb, values_grad = sums
     scale = s.scale
     ext = s.ext
@@ -263,10 +265,10 @@
     for n in range(count):
         cot_all[n] = cots[n][...]
 
-    def block(j, carry):
-        def attend(h):
+    def attend(index, feats, att, att_low, over):
+        for h in range(s.heads):
             rows = slice(h * s.head, (h + 1) * s.head)
-            query = qkv[base + j, rows, :]
+            query = qkv[index, rows, :]
             query_f = query.astype(f32)
             cut = jnp.sum(query_f * query_f, 0, keepdims=True) * (scale * scale * 0.5)
             value = jnp.exp(scale * dot(draws[h], query) - cut)
@@ -279,9 +281,10 @@
             att[rows, :] = result
             att_low[rows, :] = result.astype(bf16)
 
-        for h in range(s.heads):
-            attend(h)
-
+    def block(j, carry):
+        feats, att, att_low, over = mine if first else [ref.at[j] for ref in ahead]
+        if first:
+            attend(base + j, feats, att, att_low, over)
         x = shifted[base + j]
         middle = x + dot(out_wt[...], att_low[...]) + cols[:, 2:3]
         normed, inverse = norm_rows(middle)
@@ -341,6 +344,12 @@
 
     lax.fori_loop(0, count, block, 0)
     if not final:
+
+        def attend_ahead(n, carry):
+            attend(base + count + n, *[ref.at[n] for ref in ahead])
+            return carry
+
+        lax.fori_loop(0, later, attend_ahead, 0)
         if not first:
             results[0][...], results[1][...] = kv3[...], kv_t[...]
         return
@@ -421,6 +430,12 @@
         array(s.heads, s.rows, 3 * s.ext, dtype=bf16),
         array(s.heads, 2 * s.ext, s.rows, dtype=bf16),
     ]
+    attention = [
+        array(s.heads, s.rows, s.genes),
+        array(s.inner, s.genes),
+        array(s.inner, s.genes, dtype=bf16),
+        array(16, s.genes),
+    ]
     ends = [array(s.heads, s.rows, LANES)]
     ends += halves(s, 2 * (s.inner // LANES) + 2 * (s.hidden // LANES) + 1, parts)
     before, base = [kv_own, kv_other], 0
@@ -429,13 +444,12 @@
         first, final = index == 0, index == len(groups) - 1
         tokens = array(count, s.width, s.genes)
         out = [tokens, tokens, tokens]
-        out += ends if final else forms + sums
+        later = sum(groups[index + 1 :])
+        ahead = [array(later, *a.shape, dtype=a.dtype) for a in attention]
+        out += ends if final else forms + sums + ahead
         scratch = list(forms) if first and final else []
+        scratch += attention if first else []
         scratch += [
-            array(s.heads, s.rows, s.genes),
-            array(s.inner, s.genes),
-            array(s.inner, s.genes, dtype=bf16),
-            array(16, s.genes),
             array(s.inner, s.genes),
             array(s.inner, s.genes, dtype=bf16),
             tokens,
@@ -445,7 +459,7 @@
         scratch += sums if final else []
         scratch = [pltpu.VMEM(a.shape, a.dtype) for a in scratch]
         args = [place, *before, shifted, qkv, *cots[base : base + count], *weights]
-        body = functools.partial(middle_body, s, base, count, first, final)
+        body = functools.partial(middle_body, s, base, count, later, first, final)
         made = call("middle", body, args, out, scratch, FINAL_MB if final else FIRST_MB, 1, flops=7e9 * count)
         outputs.append(made[0])
         middle_grad.append(made[1])

time: 151 us -> 149 us (0.987)
  starting transfers between devices: 46.4 us -> 43.9 us
    ppermute x1, starting transfers between devices: 6.41 us -> 3.93 us  [local(): out_far = lax.ppermute(out_blocks[1], 'home', partners(homes, 2))]
    pallas_call x16, Pallas kernels: 58.1 us -> 59.6 us  [call(): pl.pallas_call(body, out_shape=out, in_specs=[SMEM] * smem + [VMEM] * (le...]
  transfers between devices with their start and end apart: 31 -> 31, of which waited for: 13 -> 12; matrix products, arithmetic and copies ran while one was open for 2% -> 2% of each run, Pallas kernels for 28% -> 31%
where the time goes in v3:
time: 149 us
  Pallas kernels  59.6 us (40%)
  starting transfers between devices  43.9 us (29%)
  waiting for transfers between devices  35.8 us (24%)
  local copies, waits for them, and re-layouts  8.45 us (6%)
    pallas_call x16, Pallas kernels, call(): pl.pallas_call(body, out_shape=out, in_specs=[SMEM] * smem + [VMEM] * (le...  59.6 us
    ppermute x24, starting transfers between devices, send(): lax.ppermute(values[k], axis, partners(size, k))  39.2 us
    ppermute x24, waiting for transfers between devices, send(): lax.ppermute(values[k], axis, partners(size, k))  31.1 us
    unnamed x32, local copies, waits for them, and re-layouts  4.5 us
    ppermute x5, waiting for transfers between devices, other(): return lax.ppermute(value, 'rest', partners(2, 1))  4.08 us
    ppermute x1, starting transfers between devices, local(): out_far = lax.ppermute(out_blocks[1], 'home', partners(homes, 2))  3.93 us
  transfers between devices with their start and end apart: 31, of which 12 were waited for; matrix products, arithmetic and copies ran while one was open for 2% of the time, Pallas kernels for 31%

profile of v3, /device:TPU:0, one launch (start us, length us, event | category | flops | bytes accessed | tf_op | source)
XLA Modules:
  0.0 149.0 jit_solution(7798057096495574078)
XLA Ops:
  2.2 4.1 %collective-permute-start.1 = (f32[200,256]{1,0:T(8,128)S(1)}, f32[200,256]{1,0:T(8,128)S(1)}, u32[]{:S(2)}, u32[]{:S(2)}) collective-permute-start(f32[200,256]{1,0:T(8,128)S(1)} %get-tuple-element.173), channel_id=1, source_target_pairs={{0,4},{2,6},{4,0},{6,2},{1,5},{3,7},{5,1},{7,3},{8,12},{10,14},{12... | collective-permute-start | bytes 614408 | tf_op jit(solution)/shard_map/ppermute | solution.py:566
  6.3 1.6 %collective-permute-start = (f32[200,256]{1,0:T(8,128)S(1)}, f32[200,256]{1,0:T(8,128)S(1)}, u32[]{:S(2)}, u32[]{:S(2)}) collective-permute-start(f32[200,256]{1,0:T(8,128)S(1)} %get-tuple-element.174), channel_id=1, source_target_pairs={{0,2},{2,0},{4,6},{6,4},{1,3},{3,1},{5,7},{7,5},{8,10},{10,8},{12,... | collective-permute-start | bytes 614408 | tf_op jit(solution)/shard_map/ppermute | solution.py:566
  15.0 1.7 %prepare.1 = (bf16[1920,200]{1,0:T(8,128)(2,1)S(1)}, bf16[10,272,64]{2,1,0:T(8,128)(2,1)S(1)}, bf16[10,64,272]{2,1,0:T(8,128)(2,1)S(1)}, bf16[200,640]{1,0:T(8,1...) custom-call(s32[9]{0:T(128)S(1)} %stack.35.place.refs_0_.numbers, ...), custom_call_target="tpu_custom_call" | custom-call | flops 4000000000 | bytes 1024 | tf_op jit(solution)/shard_map/prepare/pallas_call | solution.py:79
  16.7 2.6 %keys.2 = (f32[10,272,128]{2,1,0:T(8,128)S(1)}, f32[4,200,256]{2,1,0:T(8,128)S(1)}, bf16[4,1920,256]{2,1,0:T(8,128)(2,1)S(1)}) custom-call(s32[9]{0:T(128)S(1)} %stack.35.place.refs_0_.numbers, f32[200,256]{1,0:T(8,128)S(1)} %get-tuple-element.172.refs_1_, f32[200,8]{1,0:T(8,128)S(1)} %get-tuple-element.93.refs_2_.refs_4_.refs_7_.refs_18_.refs_11_, ...), custom_call_target="tpu_custom_call" | custom-call | flops 3000000000 | bytes 1024 | tf_op jit(solution)/shard_map/keys/pallas_call | solution.py:79
  19.4 2.0 %collective-permute-done.2.refs_3_ = f32[200,256]{1,0:T(8,128)S(1)} collective-permute-done((f32[200,256]{1,0:T(8,128)S(1)}, f32[200,256]{1,0:T(8,128)S(1)}, u32[]{:S(2)}, u32[]{:S(2)}) %collective-permute-start.2) | collective-permute-done | bytes 204832 | tf_op jit(solution)/shard_map/ppermute | solution.py:566
  21.4 3.9 %collective-permute-start.3 = (f32[200,256]{1,0:T(8,128)S(1)}, f32[200,256]{1,0:T(8,128)S(1)}, u32[]{:S(2)}, u32[]{:S(2)}) collective-permute-start(f32[200,256]{1,0:T(8,128)S(1)} %get-tuple-element.100), channel_id=1, source_target_pairs={{0,2},{2,0},{4,6},{6,4},{1,3},{3,1},{5,7},{7,5},{8,10},{10,8},{12,... | collective-permute-start | bytes 614408 | tf_op jit(solution)/shard_map/ppermute | solution.py:566
  25.3 6.3 %keys.3 = (f32[10,272,128]{2,1,0:T(8,128)S(1)}, f32[4,200,256]{2,1,0:T(8,128)S(1)}, bf16[4,1920,256]{2,1,0:T(8,128)(2,1)S(1)}) custom-call(s32[9]{0:T(128)S(1)} %stack.35.place.refs_0_.numbers, f32[200,256]{1,0:T(8,128)S(1)} %collective-permute-done.refs_1_, ...), custom_call_target="tpu_custom_call", output_to_operand_aliasing={{1}: (8, {}), {2}: (9, {})} | custom-call | flops 8999999488 | bytes 1024 | tf_op jit(solution)/shard_map/keys/pallas_call | solution.py:79
  31.7 2.5 %collective-permute-start.5 = (f32[200,256]{1,0:T(8,128)S(1)}, f32[200,256]{1,0:T(8,128)S(1)}, u32[]{:S(2)}, u32[]{:S(2)}) collective-permute-start(f32[200,256]{1,0:T(8,128)S(1)} %get-tuple-element.127), channel_id=1, source_target_pairs={{0,4},{2,6},{4,0},{6,2},{1,5},{3,7},{5,1},{7,3},{8,12},{10,14},{12... | collective-permute-start | bytes 614408 | tf_op jit(solution)/shard_map/ppermute | solution.py:566
  35.2 16.5 %middle.2 = (f32[2,200,256]{2,1,0:T(8,128)S(1)}, f32[2,200,256]{2,1,0:T(8,128)S(1)}, f32[2,200,256]{2,1,0:T(8,128)S(1)}, bf16[10,272,240]{2,1,0:T(8,128)(2,1)S(1...) custom-call(s32[9]{0:T(128)S(1)} %stack.35.place.refs_0_.numbers, ...), custom_call_target="tpu_custom_call" | custom-call | flops 14000000000 | bytes 1024 | tf_op jit(solution)/shard_map/middle/pallas_call | solution.py:79
  51.7 10.6 %middle.3 = (f32[2,200,256]{2,1,0:T(8,128)S(1)}, f32[2,200,256]{2,1,0:T(8,128)S(1)}, f32[2,200,256]{2,1,0:T(8,128)S(1)}, f32[10,272,128]{2,1,0:T(8,128)S(1)}, f3...) custom-call(s32[9]{0:T(128)S(1)} %stack.35.place.refs_0_.numbers, bf16[10,272,240]{2,1,0:T(8,128)(2,1)S(1)} %get-tuple-element.114.refs_1_, ...), custom_call_target="tpu_custom_call" | custom-call | flops 14000000000 | bytes 1024 | tf_op jit(solution)/shard_map/middle/pallas_call | solution.py:79
  62.9 3.9 %collective-permute-start.7 = (f32[2,200,256]{2,1,0:T(8,128)S(1)}, f32[2,200,256]{2,1,0:T(8,128)S(1)}, u32[]{:S(2)}, u32[]{:S(2)}) collective-permute-start(f32[2,200,256]{2,1,0:T(8,128)S(1)} %get-tuple-element.129), channel_id=1, source_target_pairs={{0,4},{2,6},{4,0},{6,2},{1,5},{3,7},{5,1},{7,3},{8,12},{10,14},{12... | collective-permute-start | bytes 1228808 | tf_op jit(solution)/shard_map/ppermute | solution.py:821
  67.5 1.6 %collective-permute-start.14 = (f32[576,128]{1,0:T(8,128)S(1)}, f32[576,128]{1,0:T(8,128)S(1)}, u32[]{:S(2)}, u32[]{:S(2)}) collective-permute-start(f32[576,128]{1,0:T(8,128)S(1)} %get-tuple-element.144), channel_id=1, source_target_pairs={{0,8},{8,0},{16,24},{24,16},{1,9},{9,1},{17,25},{25,17},{2,10},{10... | collective-permute-start | bytes 884744 | tf_op jit(solution)/shard_map/ppermute | solution.py:566
  69.1 1.5 %collective-permute-start.15 = (f32[576,128]{1,0:T(8,128)S(1)}, f32[576,128]{1,0:T(8,128)S(1)}, u32[]{:S(2)}, u32[]{:S(2)}) collective-permute-start(f32[576,128]{1,0:T(8,128)S(1)} %get-tuple-element.145), channel_id=1, source_target_pairs={{0,16},{8,24},{16,0},{24,8},{1,17},{9,25},{17,1},{25,9},{2,18},{10... | collective-permute-start | bytes 884744 | tf_op jit(solution)/shard_map/ppermute | solution.py:566
  71.0 13.6 %last.1 = (f32[200,256]{1,0:T(8,128)S(1)}, f32[200,256]{1,0:T(8,128)S(1)}, f32[200,256]{1,0:T(8,128)S(1)}, f32[200,256]{1,0:T(8,128)S(1)}, f32[1152,128]{1,0:T(8,128)S(1)}, /*index=5*/f32[1152,128]{1,0:T(8,128)S(1)}) custom-call(s32[9]{0:T(128)S(1)} %stack.35.place.refs_0_.numbers, f32[10,272,128]{2,1,0:T(8,128)S(1)} %get-tuple-element.130.refs_1_, ...), custom_call_target="tpu_custom_call" | custom-call | flops 1000000000 | bytes 1024 | tf_op jit(solution)/shard_map/last/pallas_call | solution.py:79
  85.5 1.9 %collective-permute-done.17.refs_1_ = f32[1152,128]{1,0:T(8,128)S(1)} collective-permute-done((f32[1152,128]{1,0:T(8,128)S(1)}, f32[1152,128]{1,0:T(8,128)S(1)}, u32[]{:S(2)}, u32[]{:S(2)}) %collective-permute-start.17) | collective-permute-done | bytes 589856 | tf_op jit(solution)/shard_map/ppermute | solution.py:783
  88.0 1.6 %collective-permute-start.18 = (f32[288,128]{1,0:T(8,128)S(1)}, f32[288,128]{1,0:T(8,128)S(1)}, u32[]{:S(2)}, u32[]{:S(2)}) collective-permute-start(f32[288,128]{1,0:T(8,128)S(1)} %get-tuple-element.150), channel_id=1, source_target_pairs={{0,8},{8,0},{16,24},{24,16},{1,9},{9,1},{17,25},{25,17},{2,10},{10... | collective-permute-start | bytes 442376 | tf_op jit(solution)/shard_map/ppermute | solution.py:566
  89.6 1.5 %collective-permute-start.19 = (f32[288,128]{1,0:T(8,128)S(1)}, f32[288,128]{1,0:T(8,128)S(1)}, u32[]{:S(2)}, u32[]{:S(2)}) collective-permute-start(f32[288,128]{1,0:T(8,128)S(1)} %get-tuple-element.151), channel_id=1, source_target_pairs={{0,16},{8,24},{16,0},{24,8},{1,17},{9,25},{17,1},{25,9},{2,18},{10... | collective-permute-start | bytes 442376 | tf_op jit(solution)/shard_map/ppermute | solution.py:566
  91.5 3.1 %collective-permute-done.18.refs_5_ = f32[288,128]{1,0:T(8,128)S(1)} collective-permute-done((f32[288,128]{1,0:T(8,128)S(1)}, f32[288,128]{1,0:T(8,128)S(1)}, u32[]{:S(2)}, u32[]{:S(2)}) %collective-permute-start.18) | collective-permute-done | bytes 147488 | tf_op jit(solution)/shard_map/ppermute | solution.py:566
  94.6 3.7 %collective-permute-done.19.refs_6_ = f32[288,128]{1,0:T(8,128)S(1)} collective-permute-done((f32[288,128]{1,0:T(8,128)S(1)}, f32[288,128]{1,0:T(8,128)S(1)}, u32[]{:S(2)}, u32[]{:S(2)}) %collective-permute-start.19) | collective-permute-done | bytes 147488 | tf_op jit(solution)/shard_map/ppermute | solution.py:566
  99.3 2.1 %collective-permute-start.22 = (f32[216,128]{1,0:T(8,128)S(1)}, f32[216,128]{1,0:T(8,128)S(1)}, u32[]{:S(2)}, u32[]{:S(2)}) collective-permute-start(f32[216,128]{1,0:T(8,128)S(1)} %get-tuple-element.156), channel_id=1, source_target_pairs={{0,4},{2,6},{4,0},{6,2},{1,5},{3,7},{5,1},{7,3},{8,12},{10,14},{12... | collective-permute-start | bytes 331784 | tf_op jit(solution)/shard_map/ppermute | solution.py:566
  101.4 2.1 %collective-permute-start.23 = (f32[216,128]{1,0:T(8,128)S(1)}, f32[216,128]{1,0:T(8,128)S(1)}, u32[]{:S(2)}, u32[]{:S(2)}) collective-permute-start(f32[216,128]{1,0:T(8,128)S(1)} %get-tuple-element.157), channel_id=1, source_target_pairs={{0,6},{2,4},{4,2},{6,0},{1,7},{3,5},{5,3},{7,1},{8,14},{10,12},{12... | collective-permute-start | bytes 331784 | tf_op jit(solution)/shard_map/ppermute | solution.py:566
  104.9 5.3 %collective-permute-done.22.refs_2_ = f32[216,128]{1,0:T(8,128)S(1)} collective-permute-done((f32[216,128]{1,0:T(8,128)S(1)}, f32[216,128]{1,0:T(8,128)S(1)}, u32[]{:S(2)}, u32[]{:S(2)}) %collective-permute-start.22) | collective-permute-done | bytes 110624 | tf_op jit(solution)/shard_map/ppermute | solution.py:566
  110.9 2.6 %collective-permute-start.26 = (f32[216,128]{1,0:T(8,128)S(1)}, f32[216,128]{1,0:T(8,128)S(1)}, u32[]{:S(2)}, u32[]{:S(2)}) collective-permute-start(f32[216,128]{1,0:T(8,128)S(1)} %add_split.5.refs_0_), channel_id=1, source_target_pairs={{0,6},{2,4},{4,2},{6,0},{1,7},{3,5},{5,3},{7,1},{8,14},{10,12},{12... | collective-permute-start | bytes 331784 | tf_op jit(solution)/shard_map/ppermute | solution.py:566
  115.3 3.4 %collective-permute-done.26.refs_3_ = f32[216,128]{1,0:T(8,128)S(1)} collective-permute-done((f32[216,128]{1,0:T(8,128)S(1)}, f32[216,128]{1,0:T(8,128)S(1)}, u32[]{:S(2)}, u32[]{:S(2)}) %collective-permute-start.26) | collective-permute-done | bytes 110624 | tf_op jit(solution)/shard_map/ppermute | solution.py:566
  118.7 3.3 %collective-permute-done.25.refs_2_ = f32[216,128]{1,0:T(8,128)S(1)} collective-permute-done((f32[216,128]{1,0:T(8,128)S(1)}, f32[216,128]{1,0:T(8,128)S(1)}, u32[]{:S(2)}, u32[]{:S(2)}) %collective-permute-start.25) | collective-permute-done | bytes 110624 | tf_op jit(solution)/shard_map/ppermute | solution.py:566
  123.4 1.6 %collective-permute-start.28 = (f32[864,128]{1,0:T(8,128)S(1)}, f32[864,128]{1,0:T(8,128)S(1)}, u32[]{:S(2)}, u32[]{:S(2)}) collective-permute-start(f32[864,128]{1,0:T(8,128)S(1)} %stack.36.refs_0_), channel_id=1, source_target_pairs={{0,16},{8,24},{16,0},{24,8},{1,17},{9,25},{17,1},{25,9},{2,18},{10... | collective-permute-start | bytes 1327112 | tf_op jit(solution)/shard_map/ppermute | solution.py:566
  126.2 2.6 %collective-permute-start.10 = (f32[200,256]{1,0:T(8,128)S(1)}, f32[200,256]{1,0:T(8,128)S(1)}, u32[]{:S(2)}, u32[]{:S(2)}) collective-permute-start(f32[200,256]{1,0:T(8,128)S(1)} %get-tuple-element.138), channel_id=1, source_target_pairs={{0,2},{2,0},{4,6},{6,4},{1,3},{3,1},{5,7},{7,5},{8,10},{10,8},{12,... | collective-permute-start | bytes 614408 | tf_op jit(solution)/shard_map/ppermute | solution.py:566
  128.8 6.0 %collective-permute-done.11.refs_2_ = f32[200,256]{1,0:T(8,128)S(1)} collective-permute-done((f32[200,256]{1,0:T(8,128)S(1)}, f32[200,256]{1,0:T(8,128)S(1)}, u32[]{:S(2)}, u32[]{:S(2)}) %collective-permute-start.11) | collective-permute-done | bytes 204832 | tf_op jit(solution)/shard_map/ppermute | solution.py:566
  134.8 3.3 %collective-permute-start.12 = (f32[200,256]{1,0:T(8,128)S(1)}, f32[200,256]{1,0:T(8,128)S(1)}, u32[]{:S(2)}, u32[]{:S(2)}) collective-permute-start(f32[200,256]{1,0:T(8,128)S(1)} %get-tuple-element.140), channel_id=1, source_target_pairs={{0,6},{2,4},{4,2},{6,0},{1,7},{3,5},{5,3},{7,1},{8,14},{10,12},{12... | collective-permute-start | bytes 614408 | tf_op jit(solution)/shard_map/ppermute | solution.py:566
  138.2 3.2 %collective-permute-done.28.refs_2_ = f32[864,128]{1,0:T(8,128)S(1)} collective-permute-done((f32[864,128]{1,0:T(8,128)S(1)}, f32[864,128]{1,0:T(8,128)S(1)}, u32[]{:S(2)}, u32[]{:S(2)}) %collective-permute-start.28) | collective-permute-done | bytes 442400 | tf_op jit(solution)/shard_map/ppermute | solution.py:566
  144.0 2.2 %collective-permute-done.30.other = f32[3456,128]{1,0:T(8,128)S(1)} collective-permute-done((f32[3456,128]{1,0:T(8,128)S(1)}, f32[3456,128]{1,0:T(8,128)S(1)}, u32[]{:S(2)}, u32[]{:S(2)}) %collective-permute-start.30) | collective-permute-done | bytes 1769504 | tf_op jit(solution)/shard_map/ppermute | solution.py:783
  146.2 2.7 %finish.1 = (f32[200,1920]{1,0:T(8,128)}, f32[200,640]{1,0:T(8,128)}, f32[200,800]{1,0:T(8,128)}, f32[200,800]{1,0:T(8,128)}, f32[1,200]{1,0:T(1,128)}, /*index=...) custom-call(s32[9]{0:T(128)S(1)} %stack.35.place.refs_0_.numbers, ...), custom_call_target="tpu_custom_call" | custom-call | flops 1000000000 | bytes 1024 | tf_op jit(solution)/shard_map/finish/pallas_call | solution.py:79
  (84 shorter events, 23.3 us)
Async XLA Ops:
  0.7 9.7 %copy-start.11 = (f32[200]{0:T(256)S(1)}, f32[200]{0:T(256)}, u32[]{:S(2)}) copy-start(f32[200]{0:T(256)} %param.32) | copy-start | bytes 2404
  2.2 17.2 %collective-permute-start.1 = (f32[200,256]{1,0:T(8,128)S(1)}, f32[200,256]{1,0:T(8,128)S(1)}, u32[]{:S(2)}, u32[]{:S(2)}) collective-permute-start(f32[200,256]{1,0:T(8,128)S(1)} %get-tuple-element.173), channel_id=1, source_target_pairs={{0,4},{2,6},{4,0},{6,2},{1,5},{3,7},{5,1},{7,3},{8,12},{10,14},{12... | collective-permute-start | bytes 614408 | tf_op jit(solution)/shard_map/ppermute | solution.py:566
  6.3 13.1 %collective-permute-start = (f32[200,256]{1,0:T(8,128)S(1)}, f32[200,256]{1,0:T(8,128)S(1)}, u32[]{:S(2)}, u32[]{:S(2)}) collective-permute-start(f32[200,256]{1,0:T(8,128)S(1)} %get-tuple-element.174), channel_id=1, source_target_pairs={{0,2},{2,0},{4,6},{6,4},{1,3},{3,1},{5,7},{7,5},{8,10},{10,8},{12,... | collective-permute-start | bytes 614408 | tf_op jit(solution)/shard_map/ppermute | solution.py:566
  7.9 13.5 %collective-permute-start.2 = (f32[200,256]{1,0:T(8,128)S(1)}, f32[200,256]{1,0:T(8,128)S(1)}, u32[]{:S(2)}, u32[]{:S(2)}) collective-permute-start(f32[200,256]{1,0:T(8,128)S(1)} %get-tuple-element.175), channel_id=1, source_target_pairs={{0,6},{2,4},{4,2},{6,0},{1,7},{3,5},{5,3},{7,1},{8,14},{10,12},{12... | collective-permute-start | bytes 614408 | tf_op jit(solution)/shard_map/ppermute | solution.py:566
  21.4 10.2 %collective-permute-start.3 = (f32[200,256]{1,0:T(8,128)S(1)}, f32[200,256]{1,0:T(8,128)S(1)}, u32[]{:S(2)}, u32[]{:S(2)}) collective-permute-start(f32[200,256]{1,0:T(8,128)S(1)} %get-tuple-element.100), channel_id=1, source_target_pairs={{0,2},{2,0},{4,6},{6,4},{1,3},{3,1},{5,7},{7,5},{8,10},{10,8},{12,... | collective-permute-start | bytes 614408 | tf_op jit(solution)/shard_map/ppermute | solution.py:566
  31.6 3.6 %collective-permute-start.4 = (f32[10,272,128]{2,1,0:T(8,128)S(1)}, f32[10,272,128]{2,1,0:T(8,128)S(1)}, u32[]{:S(2)}, u32[]{:S(2)}) collective-permute-start(f32[10,272,128]{2,1,0:T(8,128)S(1)} %get-tuple-element.101.refs_1_.refs_3_), channel_id=1, source_target_pairs={{0,1},{1,0},{2,3},{3,2},{4,5},{5,4},{6,7},{7,6},{8,9},{9,8},{10,11... | collective-permute-start | bytes 4177928 | tf_op jit(solution)/shard_map/ppermute | solution.py:783
  31.7 20.0 %collective-permute-start.5 = (f32[200,256]{1,0:T(8,128)S(1)}, f32[200,256]{1,0:T(8,128)S(1)}, u32[]{:S(2)}, u32[]{:S(2)}) collective-permute-start(f32[200,256]{1,0:T(8,128)S(1)} %get-tuple-element.127), channel_id=1, source_target_pairs={{0,4},{2,6},{4,0},{6,2},{1,5},{3,7},{5,1},{7,3},{8,12},{10,14},{12... | collective-permute-start | bytes 614408 | tf_op jit(solution)/shard_map/ppermute | solution.py:566
  34.2 17.5 %collective-permute-start.6 = (f32[200,256]{1,0:T(8,128)S(1)}, f32[200,256]{1,0:T(8,128)S(1)}, u32[]{:S(2)}, u32[]{:S(2)}) collective-permute-start(f32[200,256]{1,0:T(8,128)S(1)} %get-tuple-element.128), channel_id=1, source_target_pairs={{0,6},{2,4},{4,2},{6,0},{1,7},{3,5},{5,3},{7,1},{8,14},{10,12},{12... | collective-permute-start | bytes 614408 | tf_op jit(solution)/shard_map/ppermute | solution.py:566
  62.3 4.5 %collective-permute-start.13 = (f32[2304,128]{1,0:T(8,128)S(1)}, f32[2304,128]{1,0:T(8,128)S(1)}, u32[]{:S(2)}, u32[]{:S(2)}) collective-permute-start(f32[2304,128]{1,0:T(8,128)S(1)} %get-tuple-element.142), channel_id=1, source_target_pairs={{0,1},{1,0},{2,3},{3,2},{4,5},{5,4},{6,7},{7,6},{8,9},{9,8},{10,11... | collective-permute-start | bytes 3538952 | tf_op jit(solution)/shard_map/ppermute | solution.py:783
  62.5 8.6 %collective-permute-start.8 = (f32[10,272,128]{2,1,0:T(8,128)S(1)}, f32[10,272,128]{2,1,0:T(8,128)S(1)}, u32[]{:S(2)}, u32[]{:S(2)}) collective-permute-start(f32[10,272,128]{2,1,0:T(8,128)S(1)} %get-tuple-element.130.refs_1_), channel_id=1, source_target_pairs={{0,1},{1,0},{2,3},{3,2},{4,5},{5,4},{6,7},{7,6},{8,9},{9,8},{10,11... | collective-permute-start | bytes 4177928 | tf_op jit(solution)/shard_map/ppermute | solution.py:783
  62.9 22.4 %collective-permute-start.7 = (f32[2,200,256]{2,1,0:T(8,128)S(1)}, f32[2,200,256]{2,1,0:T(8,128)S(1)}, u32[]{:S(2)}, u32[]{:S(2)}) collective-permute-start(f32[2,200,256]{2,1,0:T(8,128)S(1)} %get-tuple-element.129), channel_id=1, source_target_pairs={{0,4},{2,6},{4,0},{6,2},{1,5},{3,7},{5,1},{7,3},{8,12},{10,14},{12... | collective-permute-start | bytes 1228808 | tf_op jit(solution)/shard_map/ppermute | solution.py:821
  67.5 17.8 %collective-permute-start.14 = (f32[576,128]{1,0:T(8,128)S(1)}, f32[576,128]{1,0:T(8,128)S(1)}, u32[]{:S(2)}, u32[]{:S(2)}) collective-permute-start(f32[576,128]{1,0:T(8,128)S(1)} %get-tuple-element.144), channel_id=1, source_target_pairs={{0,8},{8,0},{16,24},{24,16},{1,9},{9,1},{17,25},{25,17},{2,10},{10... | collective-permute-start | bytes 884744 | tf_op jit(solution)/shard_map/ppermute | solution.py:566
  69.1 16.3 %collective-permute-start.15 = (f32[576,128]{1,0:T(8,128)S(1)}, f32[576,128]{1,0:T(8,128)S(1)}, u32[]{:S(2)}, u32[]{:S(2)}) collective-permute-start(f32[576,128]{1,0:T(8,128)S(1)} %get-tuple-element.145), channel_id=1, source_target_pairs={{0,16},{8,24},{16,0},{24,8},{1,17},{9,25},{17,1},{25,9},{2,18},{10... | collective-permute-start | bytes 884744 | tf_op jit(solution)/shard_map/ppermute | solution.py:566
  70.6 14.7 %collective-permute-start.16 = (f32[576,128]{1,0:T(8,128)S(1)}, f32[576,128]{1,0:T(8,128)S(1)}, u32[]{:S(2)}, u32[]{:S(2)}) collective-permute-start(f32[576,128]{1,0:T(8,128)S(1)} %get-tuple-element.146), channel_id=1, source_target_pairs={{0,24},{8,16},{16,8},{24,0},{1,25},{9,17},{17,9},{25,1},{2,26},{10... | collective-permute-start | bytes 884744 | tf_op jit(solution)/shard_map/ppermute | solution.py:566
  85.3 2.1 %collective-permute-start.17 = (f32[1152,128]{1,0:T(8,128)S(1)}, f32[1152,128]{1,0:T(8,128)S(1)}, u32[]{:S(2)}, u32[]{:S(2)}) collective-permute-start(f32[1152,128]{1,0:T(8,128)S(1)} %get-tuple-element.148), channel_id=1, source_target_pairs={{0,1},{1,0},{2,3},{3,2},{4,5},{5,4},{6,7},{7,6},{8,9},{9,8},{10,11... | collective-permute-start | bytes 1769480 | tf_op jit(solution)/shard_map/ppermute | solution.py:783
  85.4 18.0 %collective-permute-start.9 = (f32[2,200,256]{2,1,0:T(8,128)S(1)}, f32[2,200,256]{2,1,0:T(8,128)S(1)}, u32[]{:S(2)}, u32[]{:S(2)}) collective-permute-start(f32[2,200,256]{2,1,0:T(8,128)S(1)} %forward_pair.1), channel_id=1, source_target_pairs={{0,2},{2,0},{4,6},{6,4},{1,3},{3,1},{5,7},{7,5},{8,10},{10,8},{12,... | collective-permute-start | bytes 1228808 | tf_op jit(solution)/shard_map/ppermute | solution.py:825
  88.0 6.6 %collective-permute-start.18 = (f32[288,128]{1,0:T(8,128)S(1)}, f32[288,128]{1,0:T(8,128)S(1)}, u32[]{:S(2)}, u32[]{:S(2)}) collective-permute-start(f32[288,128]{1,0:T(8,128)S(1)} %get-tuple-element.150), channel_id=1, source_target_pairs={{0,8},{8,0},{16,24},{24,16},{1,9},{9,1},{17,25},{25,17},{2,10},{10... | collective-permute-start | bytes 442376 | tf_op jit(solution)/shard_map/ppermute | solution.py:566
  89.6 8.8 %collective-permute-start.19 = (f32[288,128]{1,0:T(8,128)S(1)}, f32[288,128]{1,0:T(8,128)S(1)}, u32[]{:S(2)}, u32[]{:S(2)}) collective-permute-start(f32[288,128]{1,0:T(8,128)S(1)} %get-tuple-element.151), channel_id=1, source_target_pairs={{0,16},{8,24},{16,0},{24,8},{1,17},{9,25},{17,1},{25,9},{2,18},{10... | collective-permute-start | bytes 442376 | tf_op jit(solution)/shard_map/ppermute | solution.py:566
  91.1 7.2 %collective-permute-start.20 = (f32[288,128]{1,0:T(8,128)S(1)}, f32[288,128]{1,0:T(8,128)S(1)}, u32[]{:S(2)}, u32[]{:S(2)}) collective-permute-start(f32[288,128]{1,0:T(8,128)S(1)} %get-tuple-element.152), channel_id=1, source_target_pairs={{0,24},{8,16},{16,8},{24,0},{1,25},{9,17},{17,9},{25,1},{2,26},{10... | collective-permute-start | bytes 442376 | tf_op jit(solution)/shard_map/ppermute | solution.py:566
  99.0 5.9 %collective-permute-start.21 = (f32[216,128]{1,0:T(8,128)S(1)}, f32[216,128]{1,0:T(8,128)S(1)}, u32[]{:S(2)}, u32[]{:S(2)}) collective-permute-start(f32[216,128]{1,0:T(8,128)S(1)} %get-tuple-element.155), channel_id=1, source_target_pairs={{0,2},{2,0},{4,6},{6,4},{1,3},{3,1},{5,7},{7,5},{8,10},{10,8},{12,... | collective-permute-start | bytes 331784 | tf_op jit(solution)/shard_map/ppermute | solution.py:566
  99.3 11.0 %collective-permute-start.22 = (f32[216,128]{1,0:T(8,128)S(1)}, f32[216,128]{1,0:T(8,128)S(1)}, u32[]{:S(2)}, u32[]{:S(2)}) collective-permute-start(f32[216,128]{1,0:T(8,128)S(1)} %get-tuple-element.156), channel_id=1, source_target_pairs={{0,4},{2,6},{4,0},{6,2},{1,5},{3,7},{5,1},{7,3},{8,12},{10,14},{12... | collective-permute-start | bytes 331784 | tf_op jit(solution)/shard_map/ppermute | solution.py:566
  101.4 8.9 %collective-permute-start.23 = (f32[216,128]{1,0:T(8,128)S(1)}, f32[216,128]{1,0:T(8,128)S(1)}, u32[]{:S(2)}, u32[]{:S(2)}) collective-permute-start(f32[216,128]{1,0:T(8,128)S(1)} %get-tuple-element.157), channel_id=1, source_target_pairs={{0,6},{2,4},{4,2},{6,0},{1,7},{3,5},{5,3},{7,1},{8,14},{10,12},{12... | collective-permute-start | bytes 331784 | tf_op jit(solution)/shard_map/ppermute | solution.py:566
  110.9 7.8 %collective-permute-start.26 = (f32[216,128]{1,0:T(8,128)S(1)}, f32[216,128]{1,0:T(8,128)S(1)}, u32[]{:S(2)}, u32[]{:S(2)}) collective-permute-start(f32[216,128]{1,0:T(8,128)S(1)} %add_split.5.refs_0_), channel_id=1, source_target_pairs={{0,6},{2,4},{4,2},{6,0},{1,7},{3,5},{5,3},{7,1},{8,14},{10,12},{12... | collective-permute-start | bytes 331784 | tf_op jit(solution)/shard_map/ppermute | solution.py:566
  113.5 8.5 %collective-permute-start.25 = (f32[216,128]{1,0:T(8,128)S(1)}, f32[216,128]{1,0:T(8,128)S(1)}, u32[]{:S(2)}, u32[]{:S(2)}) collective-permute-start(f32[216,128]{1,0:T(8,128)S(1)} %add_split.5.refs_0_), channel_id=1, source_target_pairs={{0,4},{2,6},{4,0},{6,2},{1,5},{3,7},{5,1},{7,3},{8,12},{10,14},{12... | collective-permute-start | bytes 331784 | tf_op jit(solution)/shard_map/ppermute | solution.py:566
  114.1 7.9 %collective-permute-start.24 = (f32[216,128]{1,0:T(8,128)S(1)}, f32[216,128]{1,0:T(8,128)S(1)}, u32[]{:S(2)}, u32[]{:S(2)}) collective-permute-start(f32[216,128]{1,0:T(8,128)S(1)} %add_split.5.refs_0_), channel_id=1, source_target_pairs={{0,2},{2,0},{4,6},{6,4},{1,3},{3,1},{5,7},{7,5},{8,10},{10,8},{12,... | collective-permute-start | bytes 331784 | tf_op jit(solution)/shard_map/ppermute | solution.py:566
  122.0 16.1 %collective-permute-start.29 = (f32[864,128]{1,0:T(8,128)S(1)}, f32[864,128]{1,0:T(8,128)S(1)}, u32[]{:S(2)}, u32[]{:S(2)}) collective-permute-start(f32[864,128]{1,0:T(8,128)S(1)} %stack.36.refs_0_), channel_id=1, source_target_pairs={{0,24},{8,16},{16,8},{24,0},{1,25},{9,17},{17,9},{25,1},{2,26},{10... | collective-permute-start | bytes 1327112 | tf_op jit(solution)/shard_map/ppermute | solution.py:566
  123.4 18.0 %collective-permute-start.28 = (f32[864,128]{1,0:T(8,128)S(1)}, f32[864,128]{1,0:T(8,128)S(1)}, u32[]{:S(2)}, u32[]{:S(2)}) collective-permute-start(f32[864,128]{1,0:T(8,128)S(1)} %stack.36.refs_0_), channel_id=1, source_target_pairs={{0,16},{8,24},{16,0},{24,8},{1,17},{9,25},{17,1},{25,9},{2,18},{10... | collective-permute-start | bytes 1327112 | tf_op jit(solution)/shard_map/ppermute | solution.py:566
  125.0 16.4 %collective-permute-start.27 = (f32[864,128]{1,0:T(8,128)S(1)}, f32[864,128]{1,0:T(8,128)S(1)}, u32[]{:S(2)}, u32[]{:S(2)}) collective-permute-start(f32[864,128]{1,0:T(8,128)S(1)} %stack.36.refs_0_), channel_id=1, source_target_pairs={{0,8},{8,0},{16,24},{24,16},{1,9},{9,1},{17,25},{25,17},{2,10},{10... | collective-permute-start | bytes 1327112 | tf_op jit(solution)/shard_map/ppermute | solution.py:566
  125.6 9.2 %collective-permute-start.11 = (f32[200,256]{1,0:T(8,128)S(1)}, f32[200,256]{1,0:T(8,128)S(1)}, u32[]{:S(2)}, u32[]{:S(2)}) collective-permute-start(f32[200,256]{1,0:T(8,128)S(1)} %get-tuple-element.139), channel_id=1, source_target_pairs={{0,4},{2,6},{4,0},{6,2},{1,5},{3,7},{5,1},{7,3},{8,12},{10,14},{12... | collective-permute-start | bytes 614408 | tf_op jit(solution)/shard_map/ppermute | solution.py:566
  126.2 15.3 %collective-permute-start.10 = (f32[200,256]{1,0:T(8,128)S(1)}, f32[200,256]{1,0:T(8,128)S(1)}, u32[]{:S(2)}, u32[]{:S(2)}) collective-permute-start(f32[200,256]{1,0:T(8,128)S(1)} %get-tuple-element.138), channel_id=1, source_target_pairs={{0,2},{2,0},{4,6},{6,4},{1,3},{3,1},{5,7},{7,5},{8,10},{10,8},{12,... | collective-permute-start | bytes 614408 | tf_op jit(solution)/shard_map/ppermute | solution.py:566
  134.8 7.7 %collective-permute-start.12 = (f32[200,256]{1,0:T(8,128)S(1)}, f32[200,256]{1,0:T(8,128)S(1)}, u32[]{:S(2)}, u32[]{:S(2)}) collective-permute-start(f32[200,256]{1,0:T(8,128)S(1)} %get-tuple-element.140), channel_id=1, source_target_pairs={{0,6},{2,4},{4,2},{6,0},{1,7},{3,5},{5,3},{7,1},{8,14},{10,12},{12... | collective-permute-start | bytes 614408 | tf_op jit(solution)/shard_map/ppermute | solution.py:566
  142.5 3.7 %collective-permute-start.30 = (f32[3456,128]{1,0:T(8,128)S(1)}, f32[3456,128]{1,0:T(8,128)S(1)}, u32[]{:S(2)}, u32[]{:S(2)}) collective-permute-start(f32[3456,128]{1,0:T(8,128)S(1)} %stack.37.own), channel_id=1, source_target_pairs={{0,1},{1,0},{2,3},{3,2},{4,5},{5,4},{6,7},{7,6},{8,9},{9,8},{10,11... | collective-permute-start | bytes 5308424 | tf_op jit(solution)/shard_map/ppermute | solution.py:783
  (15 other events, 98.6 us)

commit v4 on v3

--- a/solution.py
+++ b/solution.py
@@ -70,7 +70,7 @@
         self.scale = self.head ** (-0.25)
 
 
-FIRST_MB, FINAL_MB, LAST_MB = 13, 15, 12
+FIRST_MB, FINAL_MB, LAST_MB = 15, 14, 12
 VMEM = pl.BlockSpec(memory_space=pltpu.VMEM)
 SMEM = pl.BlockSpec(memory_space=pltpu.SMEM)
 
@@ -230,21 +230,22 @@
         return taken
 
     (place,) = take(1)
-    before = take(2) if first else take(13)
+    before = take(2) if first else take(17)
     shifted, qkv = take(2)
     cots = take(count)
     cols, hidden_bias, draws, draws_t, out_w, out_wt = take(6)
     hid_w, hid_wt, ret_w, ret_wt, joint = take(5)
-    outputs, middle_grad, query_part = take(3)
-    results = take(3) if final else take(13)
+    outputs = take(1 if final else 2) if first else None
+    middle_grad, query_part = take(2)
+    results = take(3) if final else take(17)
     if first:
         kv3, kv_t = take(2) if final else results[:2]
     else:
         kv3, kv_t = before[:2]
-    mine = take(4) if first else None
+    mine = take(8) if first else None
     ahead = before[9:] if not first else results[9:]
     att_grad, query_grad = take(2)
-    cot_all, acts, pre_grads = take(3)
+    cot_all, pre_grads = take(2)
     sums = refs if final else results[2:9]
     acc_q, acc_o, acc_r, acc_h, acc_cols, acc_hb, values_grad = sums
     scale = s.scale
@@ -281,29 +282,39 @@
             att[rows, :] = result
             att_low[rows, :] = result.astype(bf16)
 
-    def block(j, carry):
-        feats, att, att_low, over = mine if first else [ref.at[j] for ref in ahead]
-        if first:
-            attend(base + j, feats, att, att_low, over)
-        x = shifted[base + j]
-        middle = x + dot(out_wt[...], att_low[...]) + cols[:, 2:3]
+    gain = cols[:, 3:4]
+
+    def forward(index, result, att_low, acts, slopes, normal, inverses):
+        middle = shifted[index] + dot(out_wt[...], att_low[...]) + cols[:, 2:3]
         normed, inverse = norm_rows(middle)
-        gain = cols[:, 3:4]
+        normal[...] = normed
+        inverses[0:1, :] = inverse
         second = (normed * gain + cols[:, 4:5]).astype(bf16)
-        cot = cot_all[j]
-        cot_low = cot.astype(bf16)
-        result = middle + cols[:, 5:6]
         step = s.hidden // 2
         for at in range(0, s.hidden, step):
             part = slice(at, at + step)
             pre = dot(hid_wt[part, :], second) + hidden_bias[part, 0:1]
             cumulative = 0.5 * (1.0 + lax.erf(pre * 0.7071067811865476))
             acts[part, :] = (pre * cumulative).astype(bf16)
-            slope = cumulative + pre * (jnp.exp(-0.5 * pre * pre) * 0.3989422804014327)
-            pre_low = (dot(ret_w[part, :], cot_low) * slope).astype(bf16)
+            slopes[part, :] = cumulative + pre * (jnp.exp(-0.5 * pre * pre) * 0.3989422804014327)
+        result[...] = middle + cols[:, 5:6] + dot(ret_wt[...], acts[...])
+
+    def block(j, carry):
+        feats, att, att_low, over, acts, slopes, normal, inverses = mine if first else [ref.at[j] for ref in ahead]
+        if first:
+            attend(base + j, feats, att, att_low, over)
+            forward(base + j, outputs[0].at[j], att_low, acts, slopes, normal, inverses)
+        x = shifted[base + j]
+        normed, inverse = normal[...], inverses[0:1, :]
+        second = (normed * gain + cols[:, 4:5]).astype(bf16)
+        cot = cot_all[j]
+        cot_low = cot.astype(bf16)
+        step = s.hidden // 2
+        for at in range(0, s.hidden, step):
+            part = slice(at, at + step)
+            pre_low = (dot(ret_w[part, :], cot_low) * slopes[part, :]).astype(bf16)
             pre_grads[part, :] = pre_low
             acc_hb[part, :] += fold(pre_low.astype(f32))
-        outputs[j] = result + dot(ret_wt[...], acts[...])
         acc_r[...] += dot_lanes(cot_low, acts[...])
         acc_h[...] += dot_lanes(second, pre_grads[...])
         second_grad = dot(hid_w[...], pre_grads[...])
@@ -337,8 +348,8 @@
 
         for h in range(s.heads):
             back(h)
-        normal = (norm_rows(x)[0] * cols[:, 0:1] + cols[:, 1:2]).astype(bf16)
-        acc_q[...] += dot_lanes(normal, query_grad[...])
+        first_low = (norm_rows(x)[0] * cols[:, 0:1] + cols[:, 1:2]).astype(bf16)
+        acc_q[...] += dot_lanes(first_low, query_grad[...])
         query_part[j] = dot(joint[:, : s.inner], query_grad[...])
         return carry
 
@@ -346,7 +357,9 @@
     if not final:
 
         def attend_ahead(n, carry):
-            attend(base + count + n, *[ref.at[n] for ref in ahead])
+            views = [ref.at[n] for ref in ahead]
+            attend(base + count + n, *views[:4])
+            forward(base + count + n, outputs[1].at[n], views[2], *views[4:])
             return carry
 
         lax.fori_loop(0, later, attend_ahead, 0)
@@ -435,6 +448,10 @@
         array(s.inner, s.genes),
         array(s.inner, s.genes, dtype=bf16),
         array(16, s.genes),
+        array(s.hidden, s.genes, dtype=bf16),
+        array(s.hidden, s.genes),
+        array(s.width, s.genes),
+        array(8, s.genes),
     ]
     ends = [array(s.heads, s.rows, LANES)]
     ends += halves(s, 2 * (s.inner // LANES) + 2 * (s.hidden // LANES) + 1, parts)
@@ -443,8 +460,10 @@
     for index, count in enumerate(groups):
         first, final = index == 0, index == len(groups) - 1
         tokens = array(count, s.width, s.genes)
-        out = [tokens, tokens, tokens]
         later = sum(groups[index + 1 :])
+        out = [tokens, tokens]
+        if first:
+            out = [array(n, s.width, s.genes) for n in groups] + out
         ahead = [array(later, *a.shape, dtype=a.dtype) for a in attention]
         out += ends if final else forms + sums + ahead
         scratch = list(forms) if first and final else []
@@ -454,17 +473,17 @@
             array(s.inner, s.genes, dtype=bf16),
             tokens,
             array(s.hidden, s.genes, dtype=bf16),
-            array(s.hidden, s.genes, dtype=bf16),
         ]
         scratch += sums if final else []
         scratch = [pltpu.VMEM(a.shape, a.dtype) for a in scratch]
         args = [place, *before, shifted, qkv, *cots[base : base + count], *weights]
         body = functools.partial(middle_body, s, base, count, later, first, final)
         made = call("middle", body, args, out, scratch, FINAL_MB if final else FIRST_MB, 1, flops=7e9 * count)
-        outputs.append(made[0])
-        middle_grad.append(made[1])
-        query_part.append(made[2])
-        before, base = made[3:], base + count
+        if first:
+            outputs, made = made[: len(groups)], made[len(groups) :]
+        middle_grad.append(made[0])
+        query_part.append(made[1])
+        before, base = made[2:], base + count
     return outputs, middle_grad, query_part, before
 
 
@@ -843,9 +862,9 @@
         both[0] = after(both[0], outputs)
         both = repeated(add_split(place, homes + 4, both, 1)[0], "home", homes)
         both = repeated(stack_rows(both), "cells", cells)
-        both[0] = after(both[0], grad_received[1])
+        both[0] = after(both[0], grad_received[2])
         both = stack_rows(both)
-        sums = (both, other(after(both, grad_received[0], grad_received[2])))
+        sums = (both, other(after(both, grad_received[0], grad_received[1])))
     else:
         axes = ("rest", "cells", "home")
 

time: 149 us -> 151 us (1.013)
  waiting for transfers between devices: 35.8 us -> 41.3 us
  starting transfers between devices: 43.9 us -> 38.9 us
    ppermute x24, waiting for transfers between devices: 31.1 us -> 36.4 us  [send(): lax.ppermute(values[k], axis, partners(size, k))]
    ppermute x24, starting transfers between devices: 39.2 us -> 35.7 us  [send(): lax.ppermute(values[k], axis, partners(size, k))]
    ppermute x1, starting transfers between devices: 3.93 us -> 2.16 us  [local(): out_far = lax.ppermute(out_blocks[1], 'home', partners(homes, 2))]
  transfers between devices with their start and end apart: 31 -> 31, of which waited for: 12 -> 15; matrix products, arithmetic and copies ran while one was open for 2% -> 2% of each run, Pallas kernels for 31% -> 33%
where the time goes in v4:
time: 151 us
  Pallas kernels  60.6 us (40%)
  waiting for transfers between devices  41.3 us (27%)
  starting transfers between devices  38.9 us (26%)
  local copies, waits for them, and re-layouts  8.45 us (6%)
    pallas_call x16, Pallas kernels, call(): pl.pallas_call(body, out_shape=out, in_specs=[SMEM] * smem + [VMEM] * (le...  60.6 us
    ppermute x24, waiting for transfers between devices, send(): lax.ppermute(values[k], axis, partners(size, k))  36.4 us
    ppermute x24, starting transfers between devices, send(): lax.ppermute(values[k], axis, partners(size, k))  35.7 us
    unnamed x32, local copies, waits for them, and re-layouts  4.5 us
    ppermute x5, waiting for transfers between devices, other(): return lax.ppermute(value, 'rest', partners(2, 1))  3.97 us
  transfers between devices with their start and end apart: 31, of which 15 were waited for; matrix products, arithmetic and copies ran while one was open for 2% of the time, Pallas kernels for 33%

profile of v4, /device:TPU:0, one launch (start us, length us, event | category | flops | bytes accessed | tf_op | source)
XLA Modules:
  0.0 150.5 jit_solution(2653309472626319472)
XLA Ops:
  2.2 4.1 %collective-permute-start.1 = (f32[200,256]{1,0:T(8,128)S(1)}, f32[200,256]{1,0:T(8,128)S(1)}, u32[]{:S(2)}, u32[]{:S(2)}) collective-permute-start(f32[200,256]{1,0:T(8,128)S(1)} %get-tuple-element.181), channel_id=1, source_target_pairs={{0,4},{2,6},{4,0},{6,2},{1,5},{3,7},{5,1},{7,3},{8,12},{10,14},{12... | collective-permute-start | bytes 614408 | tf_op jit(solution)/shard_map/ppermute | solution.py:585
  6.3 1.6 %collective-permute-start = (f32[200,256]{1,0:T(8,128)S(1)}, f32[200,256]{1,0:T(8,128)S(1)}, u32[]{:S(2)}, u32[]{:S(2)}) collective-permute-start(f32[200,256]{1,0:T(8,128)S(1)} %get-tuple-element.182), channel_id=1, source_target_pairs={{0,2},{2,0},{4,6},{6,4},{1,3},{3,1},{5,7},{7,5},{8,10},{10,8},{12,... | collective-permute-start | bytes 614408 | tf_op jit(solution)/shard_map/ppermute | solution.py:585
  15.0 1.7 %prepare.1 = (bf16[1920,200]{1,0:T(8,128)(2,1)S(1)}, bf16[10,272,64]{2,1,0:T(8,128)(2,1)S(1)}, bf16[10,64,272]{2,1,0:T(8,128)(2,1)S(1)}, bf16[200,640]{1,0:T(8,1...) custom-call(s32[9]{0:T(128)S(1)} %stack.35.place.refs_0_.numbers, ...), custom_call_target="tpu_custom_call" | custom-call | flops 4000000000 | bytes 1024 | tf_op jit(solution)/shard_map/prepare/pallas_call | solution.py:79
  16.7 2.5 %keys.2 = (f32[10,272,128]{2,1,0:T(8,128)S(1)}, f32[4,200,256]{2,1,0:T(8,128)S(1)}, bf16[4,1920,256]{2,1,0:T(8,128)(2,1)S(1)}) custom-call(s32[9]{0:T(128)S(1)} %stack.35.place.refs_0_.numbers, f32[200,256]{1,0:T(8,128)S(1)} %get-tuple-element.180.refs_1_, f32[200,8]{1,0:T(8,128)S(1)} %get-tuple-element.97.refs_2_.refs_4_.refs_7_.refs_22_.refs_11_, ...), custom_call_target="tpu_custom_call" | custom-call | flops 3000000000 | bytes 1024 | tf_op jit(solution)/shard_map/keys/pallas_call | solution.py:79
  19.4 2.0 %collective-permute-done.2.refs_3_ = f32[200,256]{1,0:T(8,128)S(1)} collective-permute-done((f32[200,256]{1,0:T(8,128)S(1)}, f32[200,256]{1,0:T(8,128)S(1)}, u32[]{:S(2)}, u32[]{:S(2)}) %collective-permute-start.2) | collective-permute-done | bytes 204832 | tf_op jit(solution)/shard_map/ppermute | solution.py:585
  21.4 3.9 %collective-permute-start.3 = (f32[200,256]{1,0:T(8,128)S(1)}, f32[200,256]{1,0:T(8,128)S(1)}, u32[]{:S(2)}, u32[]{:S(2)}) collective-permute-start(f32[200,256]{1,0:T(8,128)S(1)} %get-tuple-element.104), channel_id=1, source_target_pairs={{0,2},{2,0},{4,6},{6,4},{1,3},{3,1},{5,7},{7,5},{8,10},{10,8},{12,... | collective-permute-start | bytes 614408 | tf_op jit(solution)/shard_map/ppermute | solution.py:585
  25.3 6.3 %keys.3 = (f32[10,272,128]{2,1,0:T(8,128)S(1)}, f32[4,200,256]{2,1,0:T(8,128)S(1)}, bf16[4,1920,256]{2,1,0:T(8,128)(2,1)S(1)}) custom-call(s32[9]{0:T(128)S(1)} %stack.35.place.refs_0_.numbers, f32[200,256]{1,0:T(8,128)S(1)} %collective-permute-done.refs_1_, ...), custom_call_target="tpu_custom_call", output_to_operand_aliasing={{1}: (8, {}), {2}: (9, {})} | custom-call | flops 8999999488 | bytes 1024 | tf_op jit(solution)/shard_map/keys/pallas_call | solution.py:79
  31.6 2.5 %collective-permute-start.6 = (f32[200,256]{1,0:T(8,128)S(1)}, f32[200,256]{1,0:T(8,128)S(1)}, u32[]{:S(2)}, u32[]{:S(2)}) collective-permute-start(f32[200,256]{1,0:T(8,128)S(1)} %get-tuple-element.136), channel_id=1, source_target_pairs={{0,4},{2,6},{4,0},{6,2},{1,5},{3,7},{5,1},{7,3},{8,12},{10,14},{12... | collective-permute-start | bytes 614408 | tf_op jit(solution)/shard_map/ppermute | solution.py:585
  35.2 19.7 %middle.2 = (f32[2,200,256]{2,1,0:T(8,128)S(1)}, f32[2,200,256]{2,1,0:T(8,128)S(1)}, f32[2,200,256]{2,1,0:T(8,128)S(1)}, f32[2,200,256]{2,1,0:T(8,128)S(1)}, bf1...) custom-call(s32[9]{0:T(128)S(1)} %stack.35.place.refs_0_.numbers, ...), custom_call_target="tpu_custom_call" | custom-call | flops 14000000000 | bytes 1024 | tf_op jit(solution)/shard_map/middle/pallas_call | solution.py:79
  54.9 8.4 %middle.3 = (f32[2,200,256]{2,1,0:T(8,128)S(1)}, f32[2,200,256]{2,1,0:T(8,128)S(1)}, f32[10,272,128]{2,1,0:T(8,128)S(1)}, f32[2304,128]{1,0:T(8,128)S(1)}, f32[2304,128]{1,0:T(8,128)S(1)}) custom-call(s32[9]{0:T(128)S(1)} %stack.35.place.refs_0_.numbers, bf16[10,272,240]{2,1,0:T(8,128)(2,1)S(1)} %get-tuple-element.119.refs_1_, ...), custom_call_target="tpu_custom_call" | custom-call | flops 14000000000 | bytes 1024 | tf_op jit(solution)/shard_map/middle/pallas_call | solution.py:79
  63.9 2.2 %collective-permute-start.5 = (f32[2,200,256]{2,1,0:T(8,128)S(1)}, f32[2,200,256]{2,1,0:T(8,128)S(1)}, u32[]{:S(2)}, u32[]{:S(2)}) collective-permute-start(f32[2,200,256]{2,1,0:T(8,128)S(1)} %get-tuple-element.118), channel_id=1, source_target_pairs={{0,4},{2,6},{4,0},{6,2},{1,5},{3,7},{5,1},{7,3},{8,12},{10,14},{12... | collective-permute-start | bytes 1228808 | tf_op jit(solution)/shard_map/ppermute | solution.py:840
  66.9 1.6 %collective-permute-start.14 = (f32[576,128]{1,0:T(8,128)S(1)}, f32[576,128]{1,0:T(8,128)S(1)}, u32[]{:S(2)}, u32[]{:S(2)}) collective-permute-start(f32[576,128]{1,0:T(8,128)S(1)} %get-tuple-element.152), channel_id=1, source_target_pairs={{0,8},{8,0},{16,24},{24,16},{1,9},{9,1},{17,25},{25,17},{2,10},{10... | collective-permute-start | bytes 884744 | tf_op jit(solution)/shard_map/ppermute | solution.py:585
  68.4 1.5 %collective-permute-start.15 = (f32[576,128]{1,0:T(8,128)S(1)}, f32[576,128]{1,0:T(8,128)S(1)}, u32[]{:S(2)}, u32[]{:S(2)}) collective-permute-start(f32[576,128]{1,0:T(8,128)S(1)} %get-tuple-element.153), channel_id=1, source_target_pairs={{0,16},{8,24},{16,0},{24,8},{1,17},{9,25},{17,1},{25,9},{2,18},{10... | collective-permute-start | bytes 884744 | tf_op jit(solution)/shard_map/ppermute | solution.py:585
  70.4 13.6 %last.1 = (f32[200,256]{1,0:T(8,128)S(1)}, f32[200,256]{1,0:T(8,128)S(1)}, f32[200,256]{1,0:T(8,128)S(1)}, f32[200,256]{1,0:T(8,128)S(1)}, f32[1152,128]{1,0:T(8,128)S(1)}, /*index=5*/f32[1152,128]{1,0:T(8,128)S(1)}) custom-call(s32[9]{0:T(128)S(1)} %stack.35.place.refs_0_.numbers, f32[10,272,128]{2,1,0:T(8,128)S(1)} %get-tuple-element.138.refs_1_, ...), custom_call_target="tpu_custom_call" | custom-call | flops 1000000000 | bytes 1024 | tf_op jit(solution)/shard_map/last/pallas_call | solution.py:79
  85.5 1.6 %collective-permute-done.17.refs_1_ = f32[1152,128]{1,0:T(8,128)S(1)} collective-permute-done((f32[1152,128]{1,0:T(8,128)S(1)}, f32[1152,128]{1,0:T(8,128)S(1)}, u32[]{:S(2)}, u32[]{:S(2)}) %collective-permute-start.17) | collective-permute-done | bytes 589856 | tf_op jit(solution)/shard_map/ppermute | solution.py:802
  87.7 1.6 %collective-permute-start.18 = (f32[288,128]{1,0:T(8,128)S(1)}, f32[288,128]{1,0:T(8,128)S(1)}, u32[]{:S(2)}, u32[]{:S(2)}) collective-permute-start(f32[288,128]{1,0:T(8,128)S(1)} %get-tuple-element.158), channel_id=1, source_target_pairs={{0,8},{8,0},{16,24},{24,16},{1,9},{9,1},{17,25},{25,17},{2,10},{10... | collective-permute-start | bytes 442376 | tf_op jit(solution)/shard_map/ppermute | solution.py:585
  89.2 1.5 %collective-permute-start.19 = (f32[288,128]{1,0:T(8,128)S(1)}, f32[288,128]{1,0:T(8,128)S(1)}, u32[]{:S(2)}, u32[]{:S(2)}) collective-permute-start(f32[288,128]{1,0:T(8,128)S(1)} %get-tuple-element.159), channel_id=1, source_target_pairs={{0,16},{8,24},{16,0},{24,8},{1,17},{9,25},{17,1},{25,9},{2,18},{10... | collective-permute-start | bytes 442376 | tf_op jit(solution)/shard_map/ppermute | solution.py:585
  91.2 3.1 %collective-permute-done.18.refs_5_ = f32[288,128]{1,0:T(8,128)S(1)} collective-permute-done((f32[288,128]{1,0:T(8,128)S(1)}, f32[288,128]{1,0:T(8,128)S(1)}, u32[]{:S(2)}, u32[]{:S(2)}) %collective-permute-start.18) | collective-permute-done | bytes 147488 | tf_op jit(solution)/shard_map/ppermute | solution.py:585
  94.3 3.7 %collective-permute-done.19.refs_6_ = f32[288,128]{1,0:T(8,128)S(1)} collective-permute-done((f32[288,128]{1,0:T(8,128)S(1)}, f32[288,128]{1,0:T(8,128)S(1)}, u32[]{:S(2)}, u32[]{:S(2)}) %collective-permute-start.19) | collective-permute-done | bytes 147488 | tf_op jit(solution)/shard_map/ppermute | solution.py:585
  99.0 3.3 %collective-permute-start.22 = (f32[216,128]{1,0:T(8,128)S(1)}, f32[216,128]{1,0:T(8,128)S(1)}, u32[]{:S(2)}, u32[]{:S(2)}) collective-permute-start(f32[216,128]{1,0:T(8,128)S(1)} %get-tuple-element.164), channel_id=1, source_target_pairs={{0,4},{2,6},{4,0},{6,2},{1,5},{3,7},{5,1},{7,3},{8,12},{10,14},{12... | collective-permute-start | bytes 331784 | tf_op jit(solution)/shard_map/ppermute | solution.py:585
  103.1 1.5 place_blocks.1
  104.7 5.7 %collective-permute-done.22.refs_2_ = f32[216,128]{1,0:T(8,128)S(1)} collective-permute-done((f32[216,128]{1,0:T(8,128)S(1)}, f32[216,128]{1,0:T(8,128)S(1)}, u32[]{:S(2)}, u32[]{:S(2)}) %collective-permute-start.22) | collective-permute-done | bytes 110624 | tf_op jit(solution)/shard_map/ppermute | solution.py:585
  110.9 2.6 %collective-permute-start.26 = (f32[216,128]{1,0:T(8,128)S(1)}, f32[216,128]{1,0:T(8,128)S(1)}, u32[]{:S(2)}, u32[]{:S(2)}) collective-permute-start(f32[216,128]{1,0:T(8,128)S(1)} %add_split.5.refs_0_), channel_id=1, source_target_pairs={{0,6},{2,4},{4,2},{6,0},{1,7},{3,5},{5,3},{7,1},{8,14},{10,12},{12... | collective-permute-start | bytes 331784 | tf_op jit(solution)/shard_map/ppermute | solution.py:585
  115.4 3.3 %collective-permute-done.26.refs_3_ = f32[216,128]{1,0:T(8,128)S(1)} collective-permute-done((f32[216,128]{1,0:T(8,128)S(1)}, f32[216,128]{1,0:T(8,128)S(1)}, u32[]{:S(2)}, u32[]{:S(2)}) %collective-permute-start.26) | collective-permute-done | bytes 110624 | tf_op jit(solution)/shard_map/ppermute | solution.py:585
  118.7 3.8 %collective-permute-done.25.refs_2_ = f32[216,128]{1,0:T(8,128)S(1)} collective-permute-done((f32[216,128]{1,0:T(8,128)S(1)}, f32[216,128]{1,0:T(8,128)S(1)}, u32[]{:S(2)}, u32[]{:S(2)}) %collective-permute-start.25) | collective-permute-done | bytes 110624 | tf_op jit(solution)/shard_map/ppermute | solution.py:585
  123.6 1.8 %collective-permute-start.28 = (f32[864,128]{1,0:T(8,128)S(1)}, f32[864,128]{1,0:T(8,128)S(1)}, u32[]{:S(2)}, u32[]{:S(2)}) collective-permute-start(f32[864,128]{1,0:T(8,128)S(1)} %stack.36.refs_0_), channel_id=1, source_target_pairs={{0,16},{8,24},{16,0},{24,8},{1,17},{9,25},{17,1},{25,9},{2,18},{10... | collective-permute-start | bytes 1327112 | tf_op jit(solution)/shard_map/ppermute | solution.py:585
  126.1 2.6 %collective-permute-start.12 = (f32[200,256]{1,0:T(8,128)S(1)}, f32[200,256]{1,0:T(8,128)S(1)}, u32[]{:S(2)}, u32[]{:S(2)}) collective-permute-start(f32[200,256]{1,0:T(8,128)S(1)} %get-tuple-element.148), channel_id=1, source_target_pairs={{0,6},{2,4},{4,2},{6,0},{1,7},{3,5},{5,3},{7,1},{8,14},{10,12},{12... | collective-permute-start | bytes 614408 | tf_op jit(solution)/shard_map/ppermute | solution.py:585
  128.7 6.1 %collective-permute-done.12.refs_3_ = f32[200,256]{1,0:T(8,128)S(1)} collective-permute-done((f32[200,256]{1,0:T(8,128)S(1)}, f32[200,256]{1,0:T(8,128)S(1)}, u32[]{:S(2)}, u32[]{:S(2)}) %collective-permute-start.12) | collective-permute-done | bytes 204832 | tf_op jit(solution)/shard_map/ppermute | solution.py:585
  136.6 6.5 %collective-permute-done.28.refs_2_ = f32[864,128]{1,0:T(8,128)S(1)} collective-permute-done((f32[864,128]{1,0:T(8,128)S(1)}, f32[864,128]{1,0:T(8,128)S(1)}, u32[]{:S(2)}, u32[]{:S(2)}) %collective-permute-start.28) | collective-permute-done | bytes 442400 | tf_op jit(solution)/shard_map/ppermute | solution.py:585
  144.0 1.5 place_apart.1
  145.5 2.2 %collective-permute-done.30.other = f32[3456,128]{1,0:T(8,128)S(1)} collective-permute-done((f32[3456,128]{1,0:T(8,128)S(1)}, f32[3456,128]{1,0:T(8,128)S(1)}, u32[]{:S(2)}, u32[]{:S(2)}) %collective-permute-start.30) | collective-permute-done | bytes 1769504 | tf_op jit(solution)/shard_map/ppermute | solution.py:802
  147.7 2.7 %finish.1 = (f32[200,1920]{1,0:T(8,128)}, f32[200,640]{1,0:T(8,128)}, f32[200,800]{1,0:T(8,128)}, f32[200,800]{1,0:T(8,128)}, f32[1,200]{1,0:T(1,128)}, /*index=...) custom-call(s32[9]{0:T(128)S(1)} %stack.35.place.refs_0_.numbers, ...), custom_call_target="tpu_custom_call" | custom-call | flops 1000000000 | bytes 1024 | tf_op jit(solution)/shard_map/finish/pallas_call | solution.py:79
  (84 shorter events, 22.6 us)
Async XLA Ops:
  0.7 9.7 %copy-start.11 = (f32[200]{0:T(256)S(1)}, f32[200]{0:T(256)}, u32[]{:S(2)}) copy-start(f32[200]{0:T(256)} %param.32) | copy-start | bytes 2404
  2.2 17.2 %collective-permute-start.1 = (f32[200,256]{1,0:T(8,128)S(1)}, f32[200,256]{1,0:T(8,128)S(1)}, u32[]{:S(2)}, u32[]{:S(2)}) collective-permute-start(f32[200,256]{1,0:T(8,128)S(1)} %get-tuple-element.181), channel_id=1, source_target_pairs={{0,4},{2,6},{4,0},{6,2},{1,5},{3,7},{5,1},{7,3},{8,12},{10,14},{12... | collective-permute-start | bytes 614408 | tf_op jit(solution)/shard_map/ppermute | solution.py:585
  6.3 13.1 %collective-permute-start = (f32[200,256]{1,0:T(8,128)S(1)}, f32[200,256]{1,0:T(8,128)S(1)}, u32[]{:S(2)}, u32[]{:S(2)}) collective-permute-start(f32[200,256]{1,0:T(8,128)S(1)} %get-tuple-element.182), channel_id=1, source_target_pairs={{0,2},{2,0},{4,6},{6,4},{1,3},{3,1},{5,7},{7,5},{8,10},{10,8},{12,... | collective-permute-start | bytes 614408 | tf_op jit(solution)/shard_map/ppermute | solution.py:585
  7.9 13.5 %collective-permute-start.2 = (f32[200,256]{1,0:T(8,128)S(1)}, f32[200,256]{1,0:T(8,128)S(1)}, u32[]{:S(2)}, u32[]{:S(2)}) collective-permute-start(f32[200,256]{1,0:T(8,128)S(1)} %get-tuple-element.183), channel_id=1, source_target_pairs={{0,6},{2,4},{4,2},{6,0},{1,7},{3,5},{5,3},{7,1},{8,14},{10,12},{12... | collective-permute-start | bytes 614408 | tf_op jit(solution)/shard_map/ppermute | solution.py:585
  21.4 10.2 %collective-permute-start.3 = (f32[200,256]{1,0:T(8,128)S(1)}, f32[200,256]{1,0:T(8,128)S(1)}, u32[]{:S(2)}, u32[]{:S(2)}) collective-permute-start(f32[200,256]{1,0:T(8,128)S(1)} %get-tuple-element.104), channel_id=1, source_target_pairs={{0,2},{2,0},{4,6},{6,4},{1,3},{3,1},{5,7},{7,5},{8,10},{10,8},{12,... | collective-permute-start | bytes 614408 | tf_op jit(solution)/shard_map/ppermute | solution.py:585
  31.6 3.6 %collective-permute-start.4 = (f32[10,272,128]{2,1,0:T(8,128)S(1)}, f32[10,272,128]{2,1,0:T(8,128)S(1)}, u32[]{:S(2)}, u32[]{:S(2)}) collective-permute-start(f32[10,272,128]{2,1,0:T(8,128)S(1)} %get-tuple-element.105.refs_1_.refs_3_), channel_id=1, source_target_pairs={{0,1},{1,0},{2,3},{3,2},{4,5},{5,4},{6,7},{7,6},{8,9},{9,8},{10,11... | collective-permute-start | bytes 4177928 | tf_op jit(solution)/shard_map/ppermute | solution.py:802
  31.6 23.2 %collective-permute-start.6 = (f32[200,256]{1,0:T(8,128)S(1)}, f32[200,256]{1,0:T(8,128)S(1)}, u32[]{:S(2)}, u32[]{:S(2)}) collective-permute-start(f32[200,256]{1,0:T(8,128)S(1)} %get-tuple-element.136), channel_id=1, source_target_pairs={{0,4},{2,6},{4,0},{6,2},{1,5},{3,7},{5,1},{7,3},{8,12},{10,14},{12... | collective-permute-start | bytes 614408 | tf_op jit(solution)/shard_map/ppermute | solution.py:585
  34.2 20.7 %collective-permute-start.7 = (f32[200,256]{1,0:T(8,128)S(1)}, f32[200,256]{1,0:T(8,128)S(1)}, u32[]{:S(2)}, u32[]{:S(2)}) collective-permute-start(f32[200,256]{1,0:T(8,128)S(1)} %get-tuple-element.137), channel_id=1, source_target_pairs={{0,6},{2,4},{4,2},{6,0},{1,7},{3,5},{5,3},{7,1},{8,14},{10,12},{12... | collective-permute-start | bytes 614408 | tf_op jit(solution)/shard_map/ppermute | solution.py:585
  63.3 2.9 %collective-permute-start.13 = (f32[2304,128]{1,0:T(8,128)S(1)}, f32[2304,128]{1,0:T(8,128)S(1)}, u32[]{:S(2)}, u32[]{:S(2)}) collective-permute-start(f32[2304,128]{1,0:T(8,128)S(1)} %get-tuple-element.150), channel_id=1, source_target_pairs={{0,1},{1,0},{2,3},{3,2},{4,5},{5,4},{6,7},{7,6},{8,9},{9,8},{10,11... | collective-permute-start | bytes 3538952 | tf_op jit(solution)/shard_map/ppermute | solution.py:802
  63.4 7.0 %collective-permute-start.8 = (f32[10,272,128]{2,1,0:T(8,128)S(1)}, f32[10,272,128]{2,1,0:T(8,128)S(1)}, u32[]{:S(2)}, u32[]{:S(2)}) collective-permute-start(f32[10,272,128]{2,1,0:T(8,128)S(1)} %get-tuple-element.138.refs_1_), channel_id=1, source_target_pairs={{0,1},{1,0},{2,3},{3,2},{4,5},{5,4},{6,7},{7,6},{8,9},{9,8},{10,11... | collective-permute-start | bytes 4177928 | tf_op jit(solution)/shard_map/ppermute | solution.py:802
  63.9 21.1 %collective-permute-start.5 = (f32[2,200,256]{2,1,0:T(8,128)S(1)}, f32[2,200,256]{2,1,0:T(8,128)S(1)}, u32[]{:S(2)}, u32[]{:S(2)}) collective-permute-start(f32[2,200,256]{2,1,0:T(8,128)S(1)} %get-tuple-element.118), channel_id=1, source_target_pairs={{0,4},{2,6},{4,0},{6,2},{1,5},{3,7},{5,1},{7,3},{8,12},{10,14},{12... | collective-permute-start | bytes 1228808 | tf_op jit(solution)/shard_map/ppermute | solution.py:840
  66.9 18.1 %collective-permute-start.14 = (f32[576,128]{1,0:T(8,128)S(1)}, f32[576,128]{1,0:T(8,128)S(1)}, u32[]{:S(2)}, u32[]{:S(2)}) collective-permute-start(f32[576,128]{1,0:T(8,128)S(1)} %get-tuple-element.152), channel_id=1, source_target_pairs={{0,8},{8,0},{16,24},{24,16},{1,9},{9,1},{17,25},{25,17},{2,10},{10... | collective-permute-start | bytes 884744 | tf_op jit(solution)/shard_map/ppermute | solution.py:585
  68.4 16.6 %collective-permute-start.15 = (f32[576,128]{1,0:T(8,128)S(1)}, f32[576,128]{1,0:T(8,128)S(1)}, u32[]{:S(2)}, u32[]{:S(2)}) collective-permute-start(f32[576,128]{1,0:T(8,128)S(1)} %get-tuple-element.153), channel_id=1, source_target_pairs={{0,16},{8,24},{16,0},{24,8},{1,17},{9,25},{17,1},{25,9},{2,18},{10... | collective-permute-start | bytes 884744 | tf_op jit(solution)/shard_map/ppermute | solution.py:585
  70.0 15.0 %collective-permute-start.16 = (f32[576,128]{1,0:T(8,128)S(1)}, f32[576,128]{1,0:T(8,128)S(1)}, u32[]{:S(2)}, u32[]{:S(2)}) collective-permute-start(f32[576,128]{1,0:T(8,128)S(1)} %get-tuple-element.154), channel_id=1, source_target_pairs={{0,24},{8,16},{16,8},{24,0},{1,25},{9,17},{17,9},{25,1},{2,26},{10... | collective-permute-start | bytes 884744 | tf_op jit(solution)/shard_map/ppermute | solution.py:585
  85.0 2.1 %collective-permute-start.17 = (f32[1152,128]{1,0:T(8,128)S(1)}, f32[1152,128]{1,0:T(8,128)S(1)}, u32[]{:S(2)}, u32[]{:S(2)}) collective-permute-start(f32[1152,128]{1,0:T(8,128)S(1)} %get-tuple-element.156), channel_id=1, source_target_pairs={{0,1},{1,0},{2,3},{3,2},{4,5},{5,4},{6,7},{7,6},{8,9},{9,8},{10,11... | collective-permute-start | bytes 1769480 | tf_op jit(solution)/shard_map/ppermute | solution.py:802
  85.1 18.0 %collective-permute-start.9 = (f32[2,200,256]{2,1,0:T(8,128)S(1)}, f32[2,200,256]{2,1,0:T(8,128)S(1)}, u32[]{:S(2)}, u32[]{:S(2)}) collective-permute-start(f32[2,200,256]{2,1,0:T(8,128)S(1)} %forward_pair.1), channel_id=1, source_target_pairs={{0,2},{2,0},{4,6},{6,4},{1,3},{3,1},{5,7},{7,5},{8,10},{10,8},{12,... | collective-permute-start | bytes 1228808 | tf_op jit(solution)/shard_map/ppermute | solution.py:844
  87.7 6.6 %collective-permute-start.18 = (f32[288,128]{1,0:T(8,128)S(1)}, f32[288,128]{1,0:T(8,128)S(1)}, u32[]{:S(2)}, u32[]{:S(2)}) collective-permute-start(f32[288,128]{1,0:T(8,128)S(1)} %get-tuple-element.158), channel_id=1, source_target_pairs={{0,8},{8,0},{16,24},{24,16},{1,9},{9,1},{17,25},{25,17},{2,10},{10... | collective-permute-start | bytes 442376 | tf_op jit(solution)/shard_map/ppermute | solution.py:585
  89.2 8.8 %collective-permute-start.19 = (f32[288,128]{1,0:T(8,128)S(1)}, f32[288,128]{1,0:T(8,128)S(1)}, u32[]{:S(2)}, u32[]{:S(2)}) collective-permute-start(f32[288,128]{1,0:T(8,128)S(1)} %get-tuple-element.159), channel_id=1, source_target_pairs={{0,16},{8,24},{16,0},{24,8},{1,17},{9,25},{17,1},{25,9},{2,18},{10... | collective-permute-start | bytes 442376 | tf_op jit(solution)/shard_map/ppermute | solution.py:585
  90.8 7.2 %collective-permute-start.20 = (f32[288,128]{1,0:T(8,128)S(1)}, f32[288,128]{1,0:T(8,128)S(1)}, u32[]{:S(2)}, u32[]{:S(2)}) collective-permute-start(f32[288,128]{1,0:T(8,128)S(1)} %get-tuple-element.160), channel_id=1, source_target_pairs={{0,24},{8,16},{16,8},{24,0},{1,25},{9,17},{17,9},{25,1},{2,26},{10... | collective-permute-start | bytes 442376 | tf_op jit(solution)/shard_map/ppermute | solution.py:585
  98.7 6.0 %collective-permute-start.21 = (f32[216,128]{1,0:T(8,128)S(1)}, f32[216,128]{1,0:T(8,128)S(1)}, u32[]{:S(2)}, u32[]{:S(2)}) collective-permute-start(f32[216,128]{1,0:T(8,128)S(1)} %get-tuple-element.163), channel_id=1, source_target_pairs={{0,2},{2,0},{4,6},{6,4},{1,3},{3,1},{5,7},{7,5},{8,10},{10,8},{12,... | collective-permute-start | bytes 331784 | tf_op jit(solution)/shard_map/ppermute | solution.py:585
  99.0 11.3 %collective-permute-start.22 = (f32[216,128]{1,0:T(8,128)S(1)}, f32[216,128]{1,0:T(8,128)S(1)}, u32[]{:S(2)}, u32[]{:S(2)}) collective-permute-start(f32[216,128]{1,0:T(8,128)S(1)} %get-tuple-element.164), channel_id=1, source_target_pairs={{0,4},{2,6},{4,0},{6,2},{1,5},{3,7},{5,1},{7,3},{8,12},{10,14},{12... | collective-permute-start | bytes 331784 | tf_op jit(solution)/shard_map/ppermute | solution.py:585
  102.4 8.0 %collective-permute-start.23 = (f32[216,128]{1,0:T(8,128)S(1)}, f32[216,128]{1,0:T(8,128)S(1)}, u32[]{:S(2)}, u32[]{:S(2)}) collective-permute-start(f32[216,128]{1,0:T(8,128)S(1)} %get-tuple-element.165), channel_id=1, source_target_pairs={{0,6},{2,4},{4,2},{6,0},{1,7},{3,5},{5,3},{7,1},{8,14},{10,12},{12... | collective-permute-start | bytes 331784 | tf_op jit(solution)/shard_map/ppermute | solution.py:585
  110.9 7.8 %collective-permute-start.26 = (f32[216,128]{1,0:T(8,128)S(1)}, f32[216,128]{1,0:T(8,128)S(1)}, u32[]{:S(2)}, u32[]{:S(2)}) collective-permute-start(f32[216,128]{1,0:T(8,128)S(1)} %add_split.5.refs_0_), channel_id=1, source_target_pairs={{0,6},{2,4},{4,2},{6,0},{1,7},{3,5},{5,3},{7,1},{8,14},{10,12},{12... | collective-permute-start | bytes 331784 | tf_op jit(solution)/shard_map/ppermute | solution.py:585
  113.6 8.9 %collective-permute-start.25 = (f32[216,128]{1,0:T(8,128)S(1)}, f32[216,128]{1,0:T(8,128)S(1)}, u32[]{:S(2)}, u32[]{:S(2)}) collective-permute-start(f32[216,128]{1,0:T(8,128)S(1)} %add_split.5.refs_0_), channel_id=1, source_target_pairs={{0,4},{2,6},{4,0},{6,2},{1,5},{3,7},{5,1},{7,3},{8,12},{10,14},{12... | collective-permute-start | bytes 331784 | tf_op jit(solution)/shard_map/ppermute | solution.py:585
  114.3 8.2 %collective-permute-start.24 = (f32[216,128]{1,0:T(8,128)S(1)}, f32[216,128]{1,0:T(8,128)S(1)}, u32[]{:S(2)}, u32[]{:S(2)}) collective-permute-start(f32[216,128]{1,0:T(8,128)S(1)} %add_split.5.refs_0_), channel_id=1, source_target_pairs={{0,2},{2,0},{4,6},{6,4},{1,3},{3,1},{5,7},{7,5},{8,10},{10,8},{12,... | collective-permute-start | bytes 331784 | tf_op jit(solution)/shard_map/ppermute | solution.py:585
  122.5 14.1 %collective-permute-start.29 = (f32[864,128]{1,0:T(8,128)S(1)}, f32[864,128]{1,0:T(8,128)S(1)}, u32[]{:S(2)}, u32[]{:S(2)}) collective-permute-start(f32[864,128]{1,0:T(8,128)S(1)} %stack.36.refs_0_), channel_id=1, source_target_pairs={{0,24},{8,16},{16,8},{24,0},{1,25},{9,17},{17,9},{25,1},{2,26},{10... | collective-permute-start | bytes 1327112 | tf_op jit(solution)/shard_map/ppermute | solution.py:585
  123.6 19.5 %collective-permute-start.28 = (f32[864,128]{1,0:T(8,128)S(1)}, f32[864,128]{1,0:T(8,128)S(1)}, u32[]{:S(2)}, u32[]{:S(2)}) collective-permute-start(f32[864,128]{1,0:T(8,128)S(1)} %stack.36.refs_0_), channel_id=1, source_target_pairs={{0,16},{8,24},{16,0},{24,8},{1,17},{9,25},{17,1},{25,9},{2,18},{10... | collective-permute-start | bytes 1327112 | tf_op jit(solution)/shard_map/ppermute | solution.py:585
  125.4 17.7 %collective-permute-start.27 = (f32[864,128]{1,0:T(8,128)S(1)}, f32[864,128]{1,0:T(8,128)S(1)}, u32[]{:S(2)}, u32[]{:S(2)}) collective-permute-start(f32[864,128]{1,0:T(8,128)S(1)} %stack.36.refs_0_), channel_id=1, source_target_pairs={{0,8},{8,0},{16,24},{24,16},{1,9},{9,1},{17,25},{25,17},{2,10},{10... | collective-permute-start | bytes 1327112 | tf_op jit(solution)/shard_map/ppermute | solution.py:585
  126.1 8.7 %collective-permute-start.12 = (f32[200,256]{1,0:T(8,128)S(1)}, f32[200,256]{1,0:T(8,128)S(1)}, u32[]{:S(2)}, u32[]{:S(2)}) collective-permute-start(f32[200,256]{1,0:T(8,128)S(1)} %get-tuple-element.148), channel_id=1, source_target_pairs={{0,6},{2,4},{4,2},{6,0},{1,7},{3,5},{5,3},{7,1},{8,14},{10,12},{12... | collective-permute-start | bytes 614408 | tf_op jit(solution)/shard_map/ppermute | solution.py:585
  128.7 14.6 %collective-permute-start.10 = (f32[200,256]{1,0:T(8,128)S(1)}, f32[200,256]{1,0:T(8,128)S(1)}, u32[]{:S(2)}, u32[]{:S(2)}) collective-permute-start(f32[200,256]{1,0:T(8,128)S(1)} %get-tuple-element.146), channel_id=1, source_target_pairs={{0,2},{2,0},{4,6},{6,4},{1,3},{3,1},{5,7},{7,5},{8,10},{10,8},{12,... | collective-permute-start | bytes 614408 | tf_op jit(solution)/shard_map/ppermute | solution.py:585
  134.8 9.1 %collective-permute-start.11 = (f32[200,256]{1,0:T(8,128)S(1)}, f32[200,256]{1,0:T(8,128)S(1)}, u32[]{:S(2)}, u32[]{:S(2)}) collective-permute-start(f32[200,256]{1,0:T(8,128)S(1)} %get-tuple-element.147), channel_id=1, source_target_pairs={{0,4},{2,6},{4,0},{6,2},{1,5},{3,7},{5,1},{7,3},{8,12},{10,14},{12... | collective-permute-start | bytes 614408 | tf_op jit(solution)/shard_map/ppermute | solution.py:585
  144.0 3.7 %collective-permute-start.30 = (f32[3456,128]{1,0:T(8,128)S(1)}, f32[3456,128]{1,0:T(8,128)S(1)}, u32[]{:S(2)}, u32[]{:S(2)}) collective-permute-start(f32[3456,128]{1,0:T(8,128)S(1)} %stack.37.own), channel_id=1, source_target_pairs={{0,1},{1,0},{2,3},{3,2},{4,5},{5,4},{6,7},{7,6},{8,9},{9,8},{10,11... | collective-permute-start | bytes 5308424 | tf_op jit(solution)/shard_map/ppermute | solution.py:802
  (15 other events, 98.6 us)
